TPU v7x, 512 devices: a whole 4x8x8 slice. The times are simulated.
512 devices in a mesh: row: 16 (over y, core), col: 32 (over z, x).
Axes of the slice: x: 4, y: 8, z: 8, core: 2. Of those that a mesh axis runs over, the one named last changes fastest.
Arguments:
- amplitudes: bfloat16 [4096, 8192], P('row', 'col'), may hold values from -6 to 6
- drive: float32 [4096, 8192], P('row', 'col'), may hold values from -6 to 6
- pair_irrep: int32 [8192], replicated, may hold values from 0 to 7, as said below
- occ_irrep: int32 [4096], replicated, may hold values from 0 to 7
- ladder_ints: bfloat16 [8192, 8192], P('row', 'col'), may hold values from -0.1875 to 0.1875
- hole_ints: bfloat16 [4096, 4096], P('row'), may hold values from -0.25 to 0.25, as said below
- occ_energy: float32 [64], replicated, may hold values from -1.5 to -0.5
- pair_energy: float32 [8192], P('col'), may hold values from 1 to 3
Outputs:
- residual: float32 [4096, 8192], P('row', 'col')
- updated: bfloat16 [4096, 8192], P('row', 'col')
Inputs may be any that keep to these rules, and one draw needn't show every extreme that they name: hole_ints is symmetric: hole_ints[ij, kl] == hole_ints[kl, ij]. `pair_irrep`: any irrep may hold any share of the virtual pairs, all of them included.
All inputs are finite; a program needn't handle non-finite values.
Results may differ from a plain program's by a relative error of at most 0.001.
Values may be sent and summed in bfloat16 or wider, within the bound.
No kernel may reach another device: no remote copies, remote signals or barrier semaphores. Data moves between devices by JAX's collectives and lax.ppermute only.
A program may use at most 64 MiB of HBM per device.

v0:
```python
import jax
import jax.numpy as jnp
from jax import lax
from jax.sharding import PartitionSpec as P


def body(amplitudes, drive, pair_irrep, occ_irrep, ladder_ints, hole_ints, occ_energy, pair_energy):
    row_rank = lax.axis_index("row")
    col_rank = lax.axis_index("col")
    occ_rows = amplitudes.shape[0]
    pair_cols = amplitudes.shape[1]
    ladder_rows = ladder_ints.shape[0]
    own_pairs = lax.dynamic_slice_in_dim(pair_irrep, col_rank * pair_cols, pair_cols)
    ladder_labels = lax.dynamic_slice_in_dim(pair_irrep, row_rank * ladder_rows, ladder_rows)
    own_occ = lax.dynamic_slice_in_dim(occ_irrep, row_rank * occ_rows, occ_rows)
    ladder_kept = jnp.where(
        ladder_labels[:, None] == own_pairs[None, :], ladder_ints, jnp.zeros_like(ladder_ints)
    )
    ladder_full = lax.all_gather(ladder_kept, "row", axis=0, tiled=True)
    particle = jnp.dot(
        lax.all_gather(amplitudes, "col", axis=1, tiled=True),
        ladder_full,
        preferred_element_type=jnp.float32,
    )
    hole_kept = jnp.where(
        own_occ[:, None] == occ_irrep[None, :], hole_ints, jnp.zeros_like(hole_ints)
    )
    hole_part = lax.psum_scatter(
        lax.dot_general(
            hole_kept, amplitudes, (((0,), (0,)), ((), ())), preferred_element_type=jnp.float32
        ),
        "row",
        scatter_dimension=0,
        tiled=True,
    )
    residual = drive + particle + hole_part
    pair_occ = (occ_energy[:, None] + occ_energy[None, :]).reshape(-1)
    own_energy = lax.dynamic_slice_in_dim(pair_occ, row_rank * occ_rows, occ_rows)
    denominator = pair_energy[None, :] - own_energy[:, None]
    updated = (amplitudes.astype(jnp.float32) - residual / denominator).astype(jnp.bfloat16)
    return (residual, updated)


def solution(mesh):
    in_specs = (
        P("row", "col"),
        P("row", "col"),
        P(),
        P(),
        P("row", "col"),
        P("row", None),
        P(),
        P("col"),
    )
    out_specs = (P("row", "col"), P("row", "col"))
    return jax.shard_map(body, mesh=mesh, in_specs=in_specs, out_specs=out_specs, check_vma=False)
```

profile of v0, /device:TPU:1, one launch (start us, length us, event | category | flops | bytes accessed | tf_op | source)
XLA Modules:
  0.0 231.4 jit_solution(11000255282303883108)
XLA Ops:
  7.2 0.0 all-gather.3.cloned.1.call-start
  7.2 0.8 dynamic_slice.12
  8.0 0.8 dynamic_slice.13
  8.7 1.8 compare_select_fusion.2
  10.5 0.0 all-gather.3.cloned.1.call-update
  10.6 0.0 all-gather.5.cloned.1.call-start
  10.6 0.7 all-gather.5.cloned.1.call-update
  11.3 0.0 reduce-scatter.2.cloned.1.call-start
  11.4 0.8 dynamic_slice.14
  12.1 4.4 %fusion = f32[4096,256]{0,1:T(8,128)} fusion(bf16[256,256]{1,0:T(8,128)(2,1)} %param.8, bf16[256,4096]{1,0:T(8,128)(2,1)} %param.13, s32[4096]{0:T(1024)} %param.11, s32[256]{0:T(256)S(1)} %dynamic_slice.14), kind=kOutput, calls=%fused_computation.1 | convolution fusion | flops 538968064 | bytes 6439936 | tf_op jit(solution)/shard_map/dot_general | solution.py:29
  16.5 0.0 copy-start
  16.5 0.0 copy-start.2
  16.6 0.0 copy-start.1
  16.6 0.0 copy-start.3
  16.6 0.0 reduce-scatter.2.cloned.1.call-update
  16.6 0.9 copy-done
  17.5 0.1 copy.12
  17.6 0.0 copy-done.2
  17.6 0.1 broadcast_add_fusion
  17.6 0.1 add.43
  17.7 0.1 dynamic_slice.15
  17.8 0.0 copy-done.1
  17.8 0.1 copy.10
  17.9 43.3 %all-gather.3.cloned.1.call-done = bf16[8192,256]{1,0:T(8,128)(2,1)} async-done(((bf16[512,256]{1,0:T(8,128)(2,1)}), bf16[8192,256]{1,0:T(8,128)(2,1)}) %all-gather.3.cloned.1.call-update) | async-done | bytes 4194320 | tf_op jit(solution)/shard_map/all_gather | solution.py:19
  61.2 88.2 %all-gather.5.cloned.1.call-done = bf16[256,8192]{1,0:T(8,128)(2,1)} async-done(((bf16[256,256]{1,0:T(8,128)(2,1)}), bf16[256,8192]{1,0:T(8,128)(2,1)}) %all-gather.5.cloned.1.call-update) | async-done | bytes 4194320 | tf_op jit(solution)/shard_map/all_gather | solution.py:21
  149.4 69.1 %reduce-scatter.2.cloned.1.call-done = f32[256,256]{0,1:T(8,128)} async-done(((f32[4096,256]{0,1:T(8,128)}), f32[256,256]{0,1:T(8,128)}) %reduce-scatter.2.cloned.1.call-update) | async-done | bytes 262160 | tf_op jit(solution)/shard_map/reduce_scatter | solution.py:28
  218.5 0.0 copy-done.3
  218.5 4.8 %subtract_convert_fusion = (bf16[256,256]{0,1:T(8,128)(2,1)S(1)}, f32[256,256]{0,1:T(8,128)S(1)}) fusion(bf16[256,256]{0,1:T(8,128)(2,1)S(1)} %copy.12, f32[256]{0:T(256)S(1)} %dynamic_slice.15, f32[256]{0:T(256)S(1)} %copy-done.3, f32[256,256]{0,1:T(8,128)} %reduce-scatter.2.cloned.1.call-done, f32[256,256]{0,1:T(8,128)S(1)} %copy.10, ...), kind=kOutput, calls=%fused_computation.9 | convolution fusion | flops 1074200576 | bytes 9439232 | tf_op jit(solution)/shard_map/dot_general | solution.py:20
  223.2 0.8 copy.13
  224.1 0.8 copy.14
Async XLA Ops:
  7.2 54.0 %all-gather.3.cloned.1.call-start = ((), (), s32[]{:S(2)}) async-start(), calls=%async_computation.1 | async-start | bytes 4456448 | tf_op jit(solution)/shard_map/all_gather | solution.py:19
  10.6 138.8 %all-gather.5.cloned.1.call-start = ((), (), s32[]{:S(2)}) async-start(), calls=%async_computation.2 | async-start | bytes 4325376 | tf_op jit(solution)/shard_map/all_gather | solution.py:21
  11.3 207.2 %reduce-scatter.2.cloned.1.call-start = ((), (), s32[]{:S(2)}) async-start(), calls=%async_computation.3 | async-start | bytes 4456448 | tf_op jit(solution)/shard_map/reduce_scatter | solution.py:28
  16.5 0.9 copy-start
  16.5 1.0 copy-start.2
  16.6 1.2 copy-start.1
  16.6 201.9 %copy-start.3 = (f32[256]{0:T(256)S(1)}, f32[256]{0:T(256)}, u32[]{:S(2)}) copy-start(f32[256]{0:T(256)} %param.15) | copy-start | bytes 3076
Sparse Core Ops, SparseCore 0:
  10.7 50.4 all-gather.2
  64.2 85.0 all-gather.4
  152.2 66.2 reduce-scatter.1
where the time goes:
time: 233 us; the launch traced here: 231 us
  waiting for transfers between devices  201 us (86%)
  between operations  13.8 us (6%)
  matrix products  9.2 us (4%)
  local copies, waits for them, and re-layouts  5.14 us (2%)
    all_gather x1, waiting for transfers between devices, body(): lax.all_gather(amplitudes, 'col', axis=1, tiled=True)  88.2 us
    reduce_scatter x1, waiting for transfers between devices, body(): lax.psum_scatter(lax.dot_general(hole_kept, amplitudes, (((0,), (0,)), ((...  69.1 us
    all_gather x1, waiting for transfers between devices, body(): ladder_full = lax.all_gather(ladder_kept, 'row', axis=0, tiled=True)  43.3 us
    dot_general x1, matrix products, body(): jnp.dot(lax.all_gather(amplitudes, 'col', axis=1, tiled=True), ladder_ful...  4.77 us
  transfers between devices with their start and end apart: 3, of which 3 were waited for; matrix products, arithmetic and copies ran while one was open for 2% of the time, Pallas kernels for 0%

commit v1 on v0

v1 whole, which is shorter than its diff:
```python
import jax
import jax.numpy as jnp
from jax import lax
from jax.experimental import pallas as pl
from jax.experimental.pallas import tpu as pltpu
from jax.sharding import Mesh, PartitionSpec as P

NY, NCORE, NZ, NX = 8, 2, 8, 4
BF16, F32 = jnp.bfloat16, jnp.float32


def shift(n, by):
    return [(i, (i + by) % n) for i in range(n)]


def place_kernel(where_ref, p0, p1, p2, p3, out_ref, sems):
    copies = []
    for j, piece in enumerate((p0, p1, p2, p3)):
        slot = lax.rem(where_ref[1] + j, NX)
        copies.append(pltpu.make_async_copy(piece, out_ref.at[slot], sems.at[j]))
    for copy in copies:
        copy.start()
    for copy in copies:
        copy.wait()


def place(where, pieces):
    return pl.pallas_call(
        place_kernel,
        out_shape=jax.ShapeDtypeStruct((NX,) + pieces[0].shape, BF16),
        in_specs=[pl.BlockSpec(memory_space=pltpu.SMEM)]
        + [pl.BlockSpec(memory_space=pl.ANY)] * NX,
        out_specs=pl.BlockSpec(memory_space=pl.ANY),
        scratch_shapes=[pltpu.SemaphoreType.DMA((NX,))],
        cost_estimate=pl.CostEstimate(flops=0, bytes_accessed=1 << 20, transcendentals=0),
    )(where, *pieces)


def final_kernel(
    where_ref, gathered, own, f1, f2, f3, f4, b1, b2, b3, b4, hole, amps, drive, own_energy, pair_energy,
    residual_ref, updated_ref, rows_v, amps_v, acc, row_sems, amp_sems,
):
    z = where_ref[0]
    amp_copies = []

    def bring(src, slot, lo, count):
        dst = amps_v.at[slot, pl.ds(lo, count)]
        amp_copies.append(pltpu.make_async_copy(src, dst, amp_sems.at[len(amp_copies)]))
        amp_copies[-1].start()

    row_copies = [
        pltpu.make_async_copy(gathered.at[r], rows_v.at[r], row_sems.at[r])
        for r in range(gathered.shape[0])
    ]
    bring(own, z, 0, NX)
    for back, src in ((1, f1), (2, f2), (3, f3)):
        bring(src, lax.rem(z + NZ - back, NZ), 0, NX)
    for ahead, src in ((1, b1), (2, b2), (3, b3)):
        bring(src, lax.rem(z + ahead, NZ), 0, NX)
    opposite = lax.rem(z + NZ // 2, NZ)
    bring(f4, opposite, 0, NX // 2)
    bring(b4, opposite, NX // 2, NX // 2)
    for copy in row_copies:
        copy.start()
    for copy in amp_copies:
        copy.wait()
    acc[...] = drive[...]
    for r, copy in enumerate(row_copies):
        copy.wait()
        part = jnp.dot(
            amps_v[r // 2, 2 * (r % 2)], rows_v[r, 0:256, :], preferred_element_type=F32
        )
        part += jnp.dot(
            amps_v[r // 2, 2 * (r % 2) + 1], rows_v[r, 256:512, :], preferred_element_type=F32
        )
        part += jnp.dot(
            hole[:, 256 * r : 256 * (r + 1)], rows_v[r, 512:768, :], preferred_element_type=F32
        )
        acc[...] += part
    residual = acc[...]
    residual_ref[...] = residual
    denominator = pair_energy[...] - own_energy[...]
    updated_ref[...] = (amps[...].astype(F32) - residual / denominator).astype(BF16)


def final(where, gathered, ring, hole, amps, drive, own_energy, pair_energy):
    any_spec = pl.BlockSpec(memory_space=pl.ANY)
    vmem = pl.BlockSpec(memory_space=pltpu.VMEM)
    n = gathered.shape[0]
    return pl.pallas_call(
        final_kernel,
        out_shape=(
            jax.ShapeDtypeStruct(drive.shape, F32),
            jax.ShapeDtypeStruct(amps.shape, BF16),
        ),
        in_specs=[pl.BlockSpec(memory_space=pltpu.SMEM)] + [any_spec] * (1 + len(ring)) + [vmem] * 5,
        out_specs=(vmem, vmem),
        scratch_shapes=[
            pltpu.VMEM(gathered.shape, BF16),
            pltpu.VMEM((NZ, NX) + amps.shape, BF16),
            pltpu.VMEM(drive.shape, F32),
            pltpu.SemaphoreType.DMA((n,)),
            pltpu.SemaphoreType.DMA((NZ + 1,)),
        ],
        compiler_params=pltpu.CompilerParams(vmem_limit_bytes=40 << 20),
        cost_estimate=pl.CostEstimate(
            flops=2 * 256 * 256 * 12288, bytes_accessed=13 << 20, transcendentals=0
        ),
    )(where, gathered, *ring, hole, amps, drive, own_energy, pair_energy)


def body(amplitudes, drive, pair_irrep, occ_irrep, ladder_ints, hole_ints, occ_energy, pair_energy):
    z = lax.axis_index("z")
    x = lax.axis_index("x")
    row_rank = lax.axis_index("y") * NCORE + lax.axis_index("core")
    col_rank = z * NX + x
    where = jnp.stack([z, x]).astype(jnp.int32)
    occ_rows, pair_cols = amplitudes.shape
    ladder_rows = ladder_ints.shape[0]
    own_pairs = lax.dynamic_slice_in_dim(pair_irrep, col_rank * pair_cols, pair_cols)
    ladder_labels = lax.dynamic_slice_in_dim(pair_irrep, row_rank * ladder_rows, ladder_rows)
    own_occ = lax.dynamic_slice_in_dim(occ_irrep, row_rank * occ_rows, occ_rows)
    ladder_kept = jnp.where(
        ladder_labels[:, None] == own_pairs[None, :], ladder_ints, jnp.zeros_like(ladder_ints)
    )
    rows = jnp.concatenate([ladder_kept, amplitudes], axis=0)
    gathered = lax.all_gather(rows, ("y", "core"), axis=0, tiled=False)

    from_ahead = lax.ppermute(amplitudes, "x", shift(NX, -1))
    from_behind = lax.ppermute(amplitudes, "x", shift(NX, 1))
    from_opposite = lax.ppermute(amplitudes, "x", shift(NX, 2))
    own = place(where, (amplitudes, from_ahead, from_opposite, from_behind))
    f1 = lax.ppermute(own, "z", shift(NZ, 1))
    b1 = lax.ppermute(own, "z", shift(NZ, -1))
    f2 = lax.ppermute(f1, "z", shift(NZ, 1))
    b2 = lax.ppermute(b1, "z", shift(NZ, -1))
    f3 = lax.ppermute(f2, "z", shift(NZ, 1))
    b3 = lax.ppermute(b2, "z", shift(NZ, -1))
    f4 = lax.ppermute(f3[: NX // 2], "z", shift(NZ, 1))
    b4 = lax.ppermute(b3[NX // 2 :], "z", shift(NZ, -1))

    hole_kept = jnp.where(
        own_occ[:, None] == occ_irrep[None, :], hole_ints, jnp.zeros_like(hole_ints)
    )
    pair_occ = (occ_energy[:, None] + occ_energy[None, :]).reshape(-1)
    own_energy = lax.dynamic_slice_in_dim(pair_occ, row_rank * occ_rows, occ_rows)
    return final(
        where, gathered, (own, f1, f2, f3, f4, b1, b2, b3, b4), hole_kept, amplitudes, drive,
        own_energy[:, None], pair_energy[None, :],
    )


def solution(mesh):
    fine = Mesh(mesh.devices.reshape(NY, NCORE, NZ, NX), ("y", "core", "z", "x"))
    row, col = ("y", "core"), ("z", "x")
    in_specs = (
        P(row, col),
        P(row, col),
        P(),
        P(),
        P(row, col),
        P(row, None),
        P(),
        P(col),
    )
    out_specs = (P(row, col), P(row, col))
    return jax.shard_map(body, mesh=fine, in_specs=in_specs, out_specs=out_specs, check_vma=False)
```

time: 233 us -> 151 us (0.65)
  the two profiles are of different devices: /device:TPU:1 before, /device:TPU:2 now
where the time goes in v1:
time: 151 us; the launch traced here: 150 us
  starting transfers between devices  44.1 us (29%)
  Pallas kernels  36.6 us (24%)
  waiting for transfers between devices  33.9 us (22%)
  local copies, waits for them, and re-layouts  15.5 us (10%)
  between operations  14.3 us (9%)
  other arithmetic  5.59 us (4%)
    pallas_call x1, Pallas kernels, place(): pl.pallas_call(place_kernel, out_shape=jax.ShapeDtypeStruct((NX,) + piece...  27.2 us
    unnamed x42, local copies, waits for them, and re-layouts  12.1 us
    ppermute x1, waiting for transfers between devices, body(): b1 = lax.ppermute(own, 'z', shift(NZ, -1))  9.9 us
    pallas_call x1, Pallas kernels, final(): pl.pallas_call(final_kernel, out_shape=(jax.ShapeDtypeStruct(drive.shape,...  9.38 us
    ppermute x1, starting transfers between devices, body(): from_opposite = lax.ppermute(amplitudes, 'x', shift(NX, 2))  8.4 us
    ppermute x1, waiting for transfers between devices, body(): b2 = lax.ppermute(b1, 'z', shift(NZ, -1))  7.13 us
    ppermute x1, waiting for transfers between devices, body(): b3 = lax.ppermute(b2, 'z', shift(NZ, -1))  6.43 us
    ppermute x1, starting transfers between devices, body(): b1 = lax.ppermute(own, 'z', shift(NZ, -1))  5.86 us
  transfers between devices with their start and end apart: 12, of which 7 were waited for; matrix products, arithmetic and copies ran while one was open for 3% of the time, Pallas kernels for 18%

profile of v1, /device:TPU:2, one launch (start us, length us, event | category | flops | bytes accessed | tf_op | source)
XLA Modules:
  0.0 150.0 jit_solution(982413180435885802)
XLA Ops:
  7.2 0.0 copy-start.19
  7.2 0.0 all-gather.3.cloned.1.call-start
  7.2 0.8 dynamic_slice.13
  8.0 0.8 dynamic_slice.12
  8.8 1.1 compare_select_fusion.1
  9.8 1.7 %pad_maximum_fusion = bf16[768,256]{1,0:T(8,128)(2,1)} fusion(bf16[256,256]{1,0:T(8,128)(2,1)} %amps.1, bf16[512,256]{1,0:T(8,128)(2,1)S(1)} %compare_select_fusion.1), kind=kLoop, calls=%fused_computation.2 | loop fusion | flops 786432 | bytes 786432 | tf_op jit(solution)/shard_map/concatenate | solution.py:126
  11.5 0.0 all-gather.3.cloned.1.call-update
  11.6 3.4 %collective-permute-start.2 = (bf16[256,256]{1,0:T(8,128)(2,1)}, bf16[256,256]{1,0:T(8,128)(2,1)S(1)}, u32[]{:S(2)}, u32[]{:S(2)}) collective-permute-start(bf16[256,256]{1,0:T(8,128)(2,1)} %amps.1), channel_id=1, source_target_pairs={{0,1},{1,2},{2,3},{3,0},{4,5},{5,6},{6,7},{7,4},{8,9},{9,10},{10,1... | collective-permute-start | bytes 393224 | tf_op jit(solution)/shard_map/ppermute | solution.py:130
  15.0 8.4 %collective-permute-start.1 = (bf16[256,256]{1,0:T(8,128)(2,1)}, bf16[256,256]{1,0:T(8,128)(2,1)S(1)}, u32[]{:S(2)}, u32[]{:S(2)}) collective-permute-start(bf16[256,256]{1,0:T(8,128)(2,1)} %amps.1), channel_id=1, source_target_pairs={{0,2},{1,3},{2,0},{3,1},{4,6},{5,7},{6,4},{7,5},{8,10},{9,11},{10,... | collective-permute-start | bytes 393224 | tf_op jit(solution)/shard_map/ppermute | solution.py:131
  23.4 1.9 %collective-permute-start = (bf16[256,256]{1,0:T(8,128)(2,1)}, bf16[256,256]{1,0:T(8,128)(2,1)S(1)}, u32[]{:S(2)}, u32[]{:S(2)}) collective-permute-start(bf16[256,256]{1,0:T(8,128)(2,1)} %amps.1), channel_id=1, source_target_pairs={{0,3},{1,0},{2,1},{3,2},{4,7},{5,4},{6,5},{7,6},{8,11},{9,8},{10,9... | collective-permute-start | bytes 393224 | tf_op jit(solution)/shard_map/ppermute | solution.py:129
  25.3 0.6 pad_add_fusion.where_ref
  25.9 0.0 collective-permute-done.2.p3
  25.9 0.6 collective-permute-done.1.p2
  26.5 3.9 %collective-permute-done.p1 = bf16[256,256]{1,0:T(8,128)(2,1)S(1)} collective-permute-done((bf16[256,256]{1,0:T(8,128)(2,1)}, bf16[256,256]{1,0:T(8,128)(2,1)S(1)}, u32[]{:S(2)}, u32[]{:S(2)}) %collective-permute-start) | collective-permute-done | bytes 131104 | tf_op jit(solution)/shard_map/ppermute | solution.py:129
  30.4 0.0 copy-done.16
  30.4 0.0 copy-done.17
  30.4 0.7 copy-done.18
  31.1 27.2 %shard_map.95.own = bf16[4,256,256]{2,1,0:T(8,128)(2,1)} custom-call(s32[2]{0:T(128)} %pad_add_fusion.where_ref, bf16[256,256]{1,0:T(8,128)(2,1)} %amps.1, bf16[256,256]{1,0:T(8,128)(2,1)} %copy-done.18, bf16[256,256]{1,0:T(8,128)(2,1)} %copy-done.17, bf16[256,256]{1,0:T(8,128)(2,1)} %copy-done.16), custom_call_target="tpu_custom_call" | custom-call | bytes 1048576 | tf_op jit(solution)/shard_map/pallas_call | solution.py:28
  58.3 5.9 %collective-permute-start.7 = (bf16[4,256,256]{2,1,0:T(8,128)(2,1)}, bf16[4,256,256]{2,1,0:T(8,128)(2,1)S(1)}, u32[]{:S(2)}, u32[]{:S(2)}) collective-permute-start(bf16[4,256,256]{2,1,0:T(8,128)(2,1)} %shard_map.95.own), channel_id=1, source_target_pairs={{0,28},{4,0},{8,4},{12,8},{16,12},{20,16},{24,20},{28,24},{1,29},{... | collective-permute-start | bytes 1572872 | tf_op jit(solution)/shard_map/ppermute | solution.py:134
  64.2 1.9 %collective-permute-start.3 = (bf16[4,256,256]{2,1,0:T(8,128)(2,1)}, bf16[4,256,256]{2,1,0:T(8,128)(2,1)S(1)}, u32[]{:S(2)}, u32[]{:S(2)}) collective-permute-start(bf16[4,256,256]{2,1,0:T(8,128)(2,1)} %shard_map.95.own), channel_id=1, source_target_pairs={{0,4},{4,8},{8,12},{12,16},{16,20},{20,24},{24,28},{28,0},{1,5},{5... | collective-permute-start | bytes 1572872 | tf_op jit(solution)/shard_map/ppermute | solution.py:133
  66.1 9.9 %collective-permute-done.7.b1 = bf16[4,256,256]{2,1,0:T(8,128)(2,1)S(1)} collective-permute-done((bf16[4,256,256]{2,1,0:T(8,128)(2,1)}, bf16[4,256,256]{2,1,0:T(8,128)(2,1)S(1)}, u32[]{:S(2)}, u32[]{:S(2)}) %collective-permute-start.7) | collective-permute-done | bytes 524320 | tf_op jit(solution)/shard_map/ppermute | solution.py:134
  76.0 5.5 %collective-permute-start.8 = (bf16[4,256,256]{2,1,0:T(8,128)(2,1)S(1)}, bf16[4,256,256]{2,1,0:T(8,128)(2,1)S(1)}, u32[]{:S(2)}, u32[]{:S(2)}) collective-permute-start(bf16[4,256,256]{2,1,0:T(8,128)(2,1)S(1)} %collective-permute-done.7.b1), channel_id=1, source_target_pairs={{0,28},{4,0},{8,4},{12,8},{16,12},{20,16},{24,20},{28,24},{1,29},{... | collective-permute-start | bytes 1572872 | tf_op jit(solution)/shard_map/ppermute | solution.py:136
  81.5 0.0 copy-start.5
  81.5 0.8 copy-done.5
  82.3 0.0 collective-permute-done.3.f1
  82.3 1.9 %collective-permute-start.4 = (bf16[4,256,256]{2,1,0:T(8,128)(2,1)S(1)}, bf16[4,256,256]{2,1,0:T(8,128)(2,1)S(1)}, u32[]{:S(2)}, u32[]{:S(2)}) collective-permute-start(bf16[4,256,256]{2,1,0:T(8,128)(2,1)S(1)} %collective-permute-done.3.f1), channel_id=1, source_target_pairs={{0,4},{4,8},{8,12},{12,16},{16,20},{20,24},{24,28},{28,0},{1,5},{5... | collective-permute-start | bytes 1572872 | tf_op jit(solution)/shard_map/ppermute | solution.py:135
  84.3 0.0 copy-start.7
  84.3 0.8 copy-done.7
  85.1 7.1 %collective-permute-done.8.b2 = bf16[4,256,256]{2,1,0:T(8,128)(2,1)S(1)} collective-permute-done((bf16[4,256,256]{2,1,0:T(8,128)(2,1)S(1)}, bf16[4,256,256]{2,1,0:T(8,128)(2,1)S(1)}, u32[]{:S(2)}, u32[]{:S(2)}) %collective-permute-start.8) | collective-permute-done | bytes 524320 | tf_op jit(solution)/shard_map/ppermute | solution.py:136
  92.2 5.6 %collective-permute-start.9 = (bf16[4,256,256]{2,1,0:T(8,128)(2,1)S(1)}, bf16[4,256,256]{2,1,0:T(8,128)(2,1)S(1)}, u32[]{:S(2)}, u32[]{:S(2)}) collective-permute-start(bf16[4,256,256]{2,1,0:T(8,128)(2,1)S(1)} %collective-permute-done.8.b2), channel_id=1, source_target_pairs={{0,28},{4,0},{8,4},{12,8},{16,12},{20,16},{24,20},{28,24},{1,29},{... | collective-permute-start | bytes 1572872 | tf_op jit(solution)/shard_map/ppermute | solution.py:138
  97.8 0.6 collective-permute-done.4.f2
  98.4 1.9 %collective-permute-start.5 = (bf16[4,256,256]{2,1,0:T(8,128)(2,1)S(1)}, bf16[4,256,256]{2,1,0:T(8,128)(2,1)S(1)}, u32[]{:S(2)}, u32[]{:S(2)}) collective-permute-start(bf16[4,256,256]{2,1,0:T(8,128)(2,1)S(1)} %collective-permute-done.4.f2), channel_id=1, source_target_pairs={{0,4},{4,8},{8,12},{12,16},{16,20},{20,24},{24,28},{28,0},{1,5},{5... | collective-permute-start | bytes 1572872 | tf_op jit(solution)/shard_map/ppermute | solution.py:137
  100.3 0.0 copy-start.11
  100.3 0.8 copy-done.11
  101.1 0.0 copy-done.19
  101.1 0.1 dynamic_slice.14
  101.1 6.4 %collective-permute-done.9.b3 = bf16[4,256,256]{2,1,0:T(8,128)(2,1)S(1)} collective-permute-done((bf16[4,256,256]{2,1,0:T(8,128)(2,1)S(1)}, bf16[4,256,256]{2,1,0:T(8,128)(2,1)S(1)}, u32[]{:S(2)}, u32[]{:S(2)}) %collective-permute-start.9) | collective-permute-done | bytes 524320 | tf_op jit(solution)/shard_map/ppermute | solution.py:138
  107.6 0.7 slice.9
  108.3 5.6 %collective-permute-start.10 = (bf16[2,256,256]{2,1,0:T(8,128)(2,1)}, bf16[2,256,256]{2,1,0:T(8,128)(2,1)}, u32[]{:S(2)}, u32[]{:S(2)}) collective-permute-start(bf16[2,256,256]{2,1,0:T(8,128)(2,1)} %slice.9), channel_id=1, source_target_pairs={{0,28},{4,0},{8,4},{12,8},{16,12},{20,16},{24,20},{28,24},{1,29},{... | collective-permute-start | bytes 786440 | tf_op jit(solution)/shard_map/ppermute | solution.py:140
  113.9 0.0 collective-permute-done.5.f3
  113.9 0.0 copy-start.3
  113.9 0.8 slice.8
  114.7 0.0 copy-done.9
  114.7 0.1 copy-done.3
  114.8 0.0 copy-start.15
  114.8 2.1 %collective-permute-start.6 = (bf16[2,256,256]{2,1,0:T(8,128)(2,1)}, bf16[2,256,256]{2,1,0:T(8,128)(2,1)}, u32[]{:S(2)}, u32[]{:S(2)}) collective-permute-start(bf16[2,256,256]{2,1,0:T(8,128)(2,1)} %slice.8), channel_id=1, source_target_pairs={{0,4},{4,8},{8,12},{12,16},{16,20},{20,24},{24,28},{28,0},{1,5},{5... | collective-permute-start | bytes 786440 | tf_op jit(solution)/shard_map/ppermute | solution.py:139
  116.9 2.1 %compare_select_fusion.hole = bf16[256,4096]{1,0:T(8,128)(2,1)S(1)} fusion(bf16[256,4096]{1,0:T(8,128)(2,1)} %param.13, s32[4096]{0:T(1024)S(1)} %copy-done.19, s32[256]{0:T(256)S(1)} %dynamic_slice.14), kind=kLoop, calls=%fused_computation | loop fusion | flops 2097152 | bytes 4211712 | tf_op jit(solution)/shard_map/jit(_where)/select_n | solution.py:142
  119.0 0.0 copy-done.20
  119.0 0.1 broadcast_add_fusion
  119.1 0.1 add.41
  119.2 0.1 dynamic_slice.15
  119.3 0.1 copy.10.own_energy
  119.4 0.0 collective-permute-done.10.b4
  119.4 5.3 %collective-permute-done.6.f4 = bf16[2,256,256]{2,1,0:T(8,128)(2,1)} collective-permute-done((bf16[2,256,256]{2,1,0:T(8,128)(2,1)}, bf16[2,256,256]{2,1,0:T(8,128)(2,1)}, u32[]{:S(2)}, u32[]{:S(2)}) %collective-permute-start.6) | collective-permute-done | bytes 262176 | tf_op jit(solution)/shard_map/ppermute | solution.py:139
  124.8 0.0 copy-done.1
  124.8 0.0 copy-done.14
  124.8 2.8 %copy-done = bf16[12288,256]{1,0:T(8,128)(2,1)S(1)} copy-done((bf16[12288,256]{1,0:T(8,128)(2,1)S(1)}, bf16[12288,256]{1,0:T(8,128)(2,1)}, u32[]{:S(2)}) %copy-start) | copy-done | bytes 6291480
  127.6 1.0 copy-done.4
  128.6 1.0 copy-done.6
  129.6 1.0 copy-done.8
  130.7 1.0 copy-done.10
  131.7 1.0 copy-done.12
  132.8 0.9 copy-done.13
  133.7 9.4 %shard_map.96 = (f32[256,256]{1,0:T(8,128)}, bf16[256,256]{1,0:T(8,128)(2,1)}) custom-call(s32[2]{0:T(128)S(1)} %copy-done.14, bf16[16,768,256]{2,1,0:T(8,128)(2,1)S(1)} %bitcast.5, bf16[4,256,256]{2,1,0:T(8,128)(2,1)S(1)} %copy-done.1, bf16[4,256,256]{2,1,0:T(8,128)(2,1)S(1)} %copy-done.8, bf16[4,256,256]{2,1,0:T(8,128)(2,1)S(1)} %copy-done.12, ...), custom_call_target="tpu_custom_call" | custom-call | flops 1610612736 | bytes 13631488 | tf_op jit(solution)/shard_map/pallas_call | solution.py:90
  (18 shorter events, 0.0 us)
Async XLA Ops:
  7.2 93.9 %copy-start.19 = (s32[4096]{0:T(1024)S(1)}, s32[4096]{0:T(1024)}, u32[]{:S(2)}) copy-start(s32[4096]{0:T(1024)} %param.11) | copy-start | bytes 49156
  7.2 117.6 %all-gather.3.cloned.1.call-start = ((), (), s32[]{:S(2)}) async-start(), calls=%async_computation | async-start | bytes 6684672 | tf_op jit(solution)/shard_map/all_gather | solution.py:127
  11.6 14.4 %collective-permute-start.2 = (bf16[256,256]{1,0:T(8,128)(2,1)}, bf16[256,256]{1,0:T(8,128)(2,1)S(1)}, u32[]{:S(2)}, u32[]{:S(2)}) collective-permute-start(bf16[256,256]{1,0:T(8,128)(2,1)} %amps.1), channel_id=1, source_target_pairs={{0,1},{1,2},{2,3},{3,0},{4,5},{5,6},{6,7},{7,4},{8,9},{9,10},{10,1... | collective-permute-start | bytes 393224 | tf_op jit(solution)/shard_map/ppermute | solution.py:130
  15.0 11.5 %collective-permute-start.1 = (bf16[256,256]{1,0:T(8,128)(2,1)}, bf16[256,256]{1,0:T(8,128)(2,1)S(1)}, u32[]{:S(2)}, u32[]{:S(2)}) collective-permute-start(bf16[256,256]{1,0:T(8,128)(2,1)} %amps.1), channel_id=1, source_target_pairs={{0,2},{1,3},{2,0},{3,1},{4,6},{5,7},{6,4},{7,5},{8,10},{9,11},{10,... | collective-permute-start | bytes 393224 | tf_op jit(solution)/shard_map/ppermute | solution.py:131
  23.4 7.1 %collective-permute-start = (bf16[256,256]{1,0:T(8,128)(2,1)}, bf16[256,256]{1,0:T(8,128)(2,1)S(1)}, u32[]{:S(2)}, u32[]{:S(2)}) collective-permute-start(bf16[256,256]{1,0:T(8,128)(2,1)} %amps.1), channel_id=1, source_target_pairs={{0,3},{1,0},{2,1},{3,2},{4,7},{5,4},{6,5},{7,6},{8,11},{9,8},{10,9... | collective-permute-start | bytes 393224 | tf_op jit(solution)/shard_map/ppermute | solution.py:129
  25.9 4.5 %copy-start.16 = (bf16[256,256]{1,0:T(8,128)(2,1)}, bf16[256,256]{1,0:T(8,128)(2,1)S(1)}, u32[]{:S(2)}) copy-start(bf16[256,256]{1,0:T(8,128)(2,1)S(1)} %collective-permute-done.2.p3) | copy-start | bytes 393220
  26.5 3.9 %copy-start.17 = (bf16[256,256]{1,0:T(8,128)(2,1)}, bf16[256,256]{1,0:T(8,128)(2,1)S(1)}, u32[]{:S(2)}) copy-start(bf16[256,256]{1,0:T(8,128)(2,1)S(1)} %collective-permute-done.1.p2) | copy-start | bytes 393220
  30.4 0.7 copy-start.18
  58.3 17.7 %collective-permute-start.7 = (bf16[4,256,256]{2,1,0:T(8,128)(2,1)}, bf16[4,256,256]{2,1,0:T(8,128)(2,1)S(1)}, u32[]{:S(2)}, u32[]{:S(2)}) collective-permute-start(bf16[4,256,256]{2,1,0:T(8,128)(2,1)} %shard_map.95.own), channel_id=1, source_target_pairs={{0,28},{4,0},{8,4},{12,8},{16,12},{20,16},{24,20},{28,24},{1,29},{... | collective-permute-start | bytes 1572872 | tf_op jit(solution)/shard_map/ppermute | solution.py:134
  64.2 18.2 %collective-permute-start.3 = (bf16[4,256,256]{2,1,0:T(8,128)(2,1)}, bf16[4,256,256]{2,1,0:T(8,128)(2,1)S(1)}, u32[]{:S(2)}, u32[]{:S(2)}) collective-permute-start(bf16[4,256,256]{2,1,0:T(8,128)(2,1)} %shard_map.95.own), channel_id=1, source_target_pairs={{0,4},{4,8},{8,12},{12,16},{16,20},{20,24},{24,28},{28,0},{1,5},{5... | collective-permute-start | bytes 1572872 | tf_op jit(solution)/shard_map/ppermute | solution.py:133
  76.0 16.2 %collective-permute-start.8 = (bf16[4,256,256]{2,1,0:T(8,128)(2,1)S(1)}, bf16[4,256,256]{2,1,0:T(8,128)(2,1)S(1)}, u32[]{:S(2)}, u32[]{:S(2)}) collective-permute-start(bf16[4,256,256]{2,1,0:T(8,128)(2,1)S(1)} %collective-permute-done.7.b1), channel_id=1, source_target_pairs={{0,28},{4,0},{8,4},{12,8},{16,12},{20,16},{24,20},{28,24},{1,29},{... | collective-permute-start | bytes 1572872 | tf_op jit(solution)/shard_map/ppermute | solution.py:136
  81.5 0.8 copy-start.5
  82.3 16.0 %collective-permute-start.4 = (bf16[4,256,256]{2,1,0:T(8,128)(2,1)S(1)}, bf16[4,256,256]{2,1,0:T(8,128)(2,1)S(1)}, u32[]{:S(2)}, u32[]{:S(2)}) collective-permute-start(bf16[4,256,256]{2,1,0:T(8,128)(2,1)S(1)} %collective-permute-done.3.f1), channel_id=1, source_target_pairs={{0,4},{4,8},{8,12},{12,16},{16,20},{20,24},{24,28},{28,0},{1,5},{5... | collective-permute-start | bytes 1572872 | tf_op jit(solution)/shard_map/ppermute | solution.py:135
  84.3 0.8 copy-start.7
  92.2 22.5 %copy-start.9 = (bf16[4,256,256]{2,1,0:T(8,128)(2,1)}, bf16[4,256,256]{2,1,0:T(8,128)(2,1)S(1)}, u32[]{:S(2)}) copy-start(bf16[4,256,256]{2,1,0:T(8,128)(2,1)S(1)} %collective-permute-done.8.b2) | copy-start | bytes 1572868
  92.2 15.4 %collective-permute-start.9 = (bf16[4,256,256]{2,1,0:T(8,128)(2,1)S(1)}, bf16[4,256,256]{2,1,0:T(8,128)(2,1)S(1)}, u32[]{:S(2)}, u32[]{:S(2)}) collective-permute-start(bf16[4,256,256]{2,1,0:T(8,128)(2,1)S(1)} %collective-permute-done.8.b2), channel_id=1, source_target_pairs={{0,28},{4,0},{8,4},{12,8},{16,12},{20,16},{24,20},{28,24},{1,29},{... | collective-permute-start | bytes 1572872 | tf_op jit(solution)/shard_map/ppermute | solution.py:138
  98.4 15.5 %collective-permute-start.5 = (bf16[4,256,256]{2,1,0:T(8,128)(2,1)S(1)}, bf16[4,256,256]{2,1,0:T(8,128)(2,1)S(1)}, u32[]{:S(2)}, u32[]{:S(2)}) collective-permute-start(bf16[4,256,256]{2,1,0:T(8,128)(2,1)S(1)} %collective-permute-done.4.f2), channel_id=1, source_target_pairs={{0,4},{4,8},{8,12},{12,16},{16,20},{20,24},{24,28},{28,0},{1,5},{5... | collective-permute-start | bytes 1572872 | tf_op jit(solution)/shard_map/ppermute | solution.py:137
  100.3 0.8 copy-start.11
  108.3 11.1 %collective-permute-start.10 = (bf16[2,256,256]{2,1,0:T(8,128)(2,1)}, bf16[2,256,256]{2,1,0:T(8,128)(2,1)}, u32[]{:S(2)}, u32[]{:S(2)}) collective-permute-start(bf16[2,256,256]{2,1,0:T(8,128)(2,1)} %slice.9), channel_id=1, source_target_pairs={{0,28},{4,0},{8,4},{12,8},{16,12},{20,16},{24,20},{28,24},{1,29},{... | collective-permute-start | bytes 786440 | tf_op jit(solution)/shard_map/ppermute | solution.py:140
  113.9 0.9 copy-start.3
  114.8 4.2 %copy-start.20 = (f32[64]{0:T(128)S(1)}, f32[64]{0:T(128)}, u32[]{:S(2)}) copy-start(f32[64]{0:T(128)} %param.14) | copy-start | bytes 772
  114.8 10.0 %copy-start.1 = (bf16[4,256,256]{2,1,0:T(8,128)(2,1)S(1)}, bf16[4,256,256]{2,1,0:T(8,128)(2,1)}, u32[]{:S(2)}) copy-start(bf16[4,256,256]{2,1,0:T(8,128)(2,1)} %shard_map.95.own) | copy-start | bytes 1572868
  114.8 10.0 %copy-start.2 = (bf16[256,256]{1,0:T(8,128)(2,1)S(1)}, bf16[256,256]{1,0:T(8,128)(2,1)}, u32[]{:S(2)}) copy-start(bf16[256,256]{1,0:T(8,128)(2,1)} %amps.1) | copy-start | bytes 393220
  114.8 10.0 %copy-start.14 = (s32[2]{0:T(128)S(1)}, s32[2]{0:T(128)}, u32[]{:S(2)}) copy-start(s32[2]{0:T(128)} %pad_add_fusion.where_ref) | copy-start | bytes 28
  114.8 10.0 %copy-start.15 = (f32[256]{0:T(256)S(1)}, f32[256]{0:T(256)}, u32[]{:S(2)}) copy-start(f32[256]{0:T(256)} %param.15) | copy-start | bytes 3076
  114.8 9.9 %collective-permute-start.6 = (bf16[2,256,256]{2,1,0:T(8,128)(2,1)}, bf16[2,256,256]{2,1,0:T(8,128)(2,1)}, u32[]{:S(2)}, u32[]{:S(2)}) collective-permute-start(bf16[2,256,256]{2,1,0:T(8,128)(2,1)} %slice.8), channel_id=1, source_target_pairs={{0,4},{4,8},{8,12},{12,16},{16,20},{20,24},{24,28},{28,0},{1,5},{5... | collective-permute-start | bytes 786440 | tf_op jit(solution)/shard_map/ppermute | solution.py:139
  124.8 2.8 %copy-start = (bf16[12288,256]{1,0:T(8,128)(2,1)S(1)}, bf16[12288,256]{1,0:T(8,128)(2,1)}, u32[]{:S(2)}) copy-start(bf16[12288,256]{1,0:T(8,128)(2,1)} %all-gather.3.cloned.1.call-done) | copy-start | bytes 18874372
  127.6 1.0 copy-start.4
  128.6 1.0 copy-start.6
  129.6 1.0 copy-start.8
  130.7 1.0 copy-start.10
  131.7 1.0 copy-start.12
  132.8 0.9 copy-start.13
Sparse Core Ops, SparseCore 0:
  11.7 53.1 all-gather.2

commit v2 on v0

v2 whole, which is shorter than its diff:
```python
import jax
import jax.numpy as jnp
from jax import lax
from jax.experimental import pallas as pl
from jax.experimental.pallas import tpu as pltpu
from jax.sharding import Mesh, PartitionSpec as P

NY, NCORE, NZ, NX = 8, 2, 8, 4
BF16, F32 = jnp.bfloat16, jnp.float32
LANES = 128


def shift(n, by):
    return [(i, (i + by) % n) for i in range(n)]


def row_rank():
    return lax.axis_index("y") * NCORE + lax.axis_index("core")


def prep_kernel(labels, ladder, amps, rows_ref):
    r = row_rank()
    c = lax.axis_index("z") * NX + lax.axis_index("x")
    n_ladder, n_cols = ladder.shape
    col_labels = [
        labels[pl.ds(c * (n_cols // LANES) + q, 1), :].astype(F32) for q in range(n_cols // LANES)
    ]
    for k in range(n_ladder // LANES):
        line = labels[pl.ds(r * (n_ladder // LANES) + k, 1), :].astype(F32)
        row_labels = jnp.broadcast_to(line, (LANES, LANES)).T
        for q in range(n_cols // LANES):
            at = (pl.ds(k * LANES, LANES), pl.ds(q * LANES, LANES))
            kept = jnp.where(row_labels == col_labels[q], ladder[at].astype(F32), 0.0)
            rows_ref[at] = kept.astype(BF16)
    rows_ref[n_ladder:, :] = amps[...]


def prep(labels, ladder, amps):
    vmem = pl.BlockSpec(memory_space=pltpu.VMEM)
    n = ladder.shape[0] + amps.shape[0]
    return pl.pallas_call(
        prep_kernel,
        out_shape=jax.ShapeDtypeStruct((n, amps.shape[1]), BF16),
        in_specs=[vmem] * 3,
        out_specs=vmem,
        cost_estimate=pl.CostEstimate(flops=0, bytes_accessed=1 << 20, transcendentals=0),
    )(labels, ladder, amps)


def final_kernel(gathered, hole, *refs):
    parts, (amps, drive, own_energy, pair_energy, residual_ref, updated_ref) = refs[:9], refs[9:15]
    rows_v, amps_rows_v, hole_v, parts_v, acc, row_sems, amps_sems, hole_sems, part_sems = refs[15:]
    z, x = lax.axis_index("z"), lax.axis_index("x")
    n, size = gathered.shape[0], amps.shape[0]
    group = n // len(hole_v)
    hole_copies, copies, at = [], [], 0
    for g in range(len(hole_v)):
        src = hole.at[:, pl.ds(g * group * size, group * size)]
        mine = [pltpu.make_async_copy(src, hole_v[g], hole_sems.at[g])]
        for r in range(g * group, (g + 1) * group):
            src = gathered.at[r, pl.ds(2 * size, size)]
            dst = amps_rows_v.at[pl.ds(r * size, size)]
            mine.append(pltpu.make_async_copy(src, dst, amps_sems.at[r]))
        hole_copies.append(mine)
    opposite = lax.rem(z + NZ // 2, NZ)
    sources = [(lax.rem(z + NZ + away, NZ), range(NX)) for away in (0, -1, 1, -2, 2, -3, 3)]
    sources += [(opposite, range(NX // 2)), (opposite, range(NX // 2, NX))]
    for i, (slot, blocks) in enumerate(sources):
        mine = [pltpu.make_async_copy(parts[i], parts_v[i], part_sems.at[i])]
        for j in blocks:
            block = slot * NX + lax.rem(x + j, NX)
            src = gathered.at[block // 2, pl.ds(pl.multiple_of(lax.rem(block, 2) * size, size), size)]
            dst = rows_v.at[pl.ds(at, size)]
            mine.append(pltpu.make_async_copy(src, dst, row_sems.at[at // size]))
            at += size
        copies.append(mine)
    for mine in hole_copies + copies:
        for copy in mine:
            copy.start()
    acc[...] = drive[...]
    for g, mine in enumerate(hole_copies):
        for copy in mine:
            copy.wait()
        at = pl.ds(g * group * size, group * size)
        acc[...] += jnp.dot(hole_v[g][...], amps_rows_v[at], preferred_element_type=F32)
    at = 0
    for i, mine in enumerate(copies):
        for copy in mine:
            copy.wait()
        depth = size * (len(mine) - 1)
        acc[...] += jnp.dot(parts_v[i][...], rows_v[at : at + depth, :], preferred_element_type=F32)
        at += depth
    residual = acc[...]
    residual_ref[...] = residual
    denominator = pair_energy[...] - own_energy[...]
    updated_ref[...] = (amps[...].astype(F32) - residual / denominator).astype(BF16)


def final(gathered, hole, parts, amps, drive, own_energy, pair_energy):
    hbm = pl.BlockSpec(memory_space=pltpu.HBM)
    vmem = pl.BlockSpec(memory_space=pltpu.VMEM)
    n, _, cols = gathered.shape
    size, groups = amps.shape[0], 4
    in_hbm = [pltpu.with_memory_space_constraint(a, pltpu.HBM) for a in (gathered, hole, *parts)]
    return pl.pallas_call(
        final_kernel,
        out_shape=(
            jax.ShapeDtypeStruct(drive.shape, F32),
            jax.ShapeDtypeStruct(amps.shape, BF16),
        ),
        in_specs=[hbm] * len(in_hbm) + [vmem] * 4,
        out_specs=(vmem, vmem),
        scratch_shapes=[
            pltpu.VMEM((2 * n * size, cols), BF16),
            pltpu.VMEM((n * size, cols), BF16),
            [pltpu.VMEM((size, n * size // groups), BF16) for _ in range(groups)],
            [pltpu.VMEM(p.shape, BF16) for p in parts],
            pltpu.VMEM(drive.shape, F32),
            pltpu.SemaphoreType.DMA((2 * n,)),
            pltpu.SemaphoreType.DMA((n,)),
            pltpu.SemaphoreType.DMA((groups,)),
            pltpu.SemaphoreType.DMA((len(parts),)),
        ],
        compiler_params=pltpu.CompilerParams(vmem_limit_bytes=32 << 20),
        cost_estimate=pl.CostEstimate(
            flops=2 * 256 * 256 * 12288, bytes_accessed=13 << 20, transcendentals=0
        ),
    )(*in_hbm, amps, drive, own_energy, pair_energy)


def body(amplitudes, drive, pair_irrep, occ_irrep, ladder_ints, hole_ints, occ_energy, pair_energy):
    occ_rows = amplitudes.shape[0]
    rows = prep(pair_irrep.reshape(-1, LANES), ladder_ints, amplitudes)
    gathered = lax.all_gather(rows, ("y", "core"), axis=0, tiled=False)

    blocks = [lax.ppermute(amplitudes, "x", shift(NX, -j)) for j in range(1, NX)]
    own = jnp.concatenate([amplitudes] + blocks, axis=1)
    f, b = own, own
    parts = [own]
    for _ in range(NZ // 2 - 1):
        f = lax.ppermute(f, "z", shift(NZ, 1))
        b = lax.ppermute(b, "z", shift(NZ, -1))
        parts += [f, b]
    half = own.shape[1] // 2
    parts.append(lax.ppermute(f[:, :half], "z", shift(NZ, 1)))
    parts.append(lax.ppermute(b[:, half:], "z", shift(NZ, -1)))

    own_occ = lax.dynamic_slice_in_dim(occ_irrep, row_rank() * occ_rows, occ_rows)
    hole_kept = jnp.where(
        own_occ[:, None] == occ_irrep[None, :], hole_ints, jnp.zeros_like(hole_ints)
    )
    pair_occ = (occ_energy[:, None] + occ_energy[None, :]).reshape(-1)
    own_energy = lax.dynamic_slice_in_dim(pair_occ, row_rank() * occ_rows, occ_rows)
    return final(
        gathered, hole_kept, parts, amplitudes, drive, own_energy[:, None], pair_energy[None, :]
    )


def solution(mesh):
    fine = Mesh(mesh.devices.reshape(NY, NCORE, NZ, NX), ("y", "core", "z", "x"))
    row, col = ("y", "core"), ("z", "x")
    in_specs = (
        P(row, col),
        P(row, col),
        P(),
        P(),
        P(row, col),
        P(row, None),
        P(),
        P(col),
    )
    out_specs = (P(row, col), P(row, col))
    return jax.shard_map(body, mesh=fine, in_specs=in_specs, out_specs=out_specs, check_vma=False)
```

time: 233 us -> 107 us (0.46)
  the two profiles are of different devices: /device:TPU:1 before, /device:TPU:38 now
where the time goes in v2:
time: 107 us; the launch traced here: 106 us
  starting transfers between devices  44.7 us (42%)
  waiting for transfers between devices  31.3 us (29%)
  between operations  14.3 us (13%)
  Pallas kernels  11 us (10%)
  local copies, waits for them, and re-layouts  2.88 us (3%)
  other arithmetic  1.99 us (2%)
    ppermute x3, starting transfers between devices, body(): b = lax.ppermute(b, 'z', shift(NZ, -1))  22.2 us
    ppermute x3, waiting for transfers between devices, body(): b = lax.ppermute(b, 'z', shift(NZ, -1))  20.2 us
    ppermute x3, starting transfers between devices, body(): lax.ppermute(amplitudes, 'x', shift(NX, -j))  9.16 us
    pallas_call x1, Pallas kernels, final(): pl.pallas_call(final_kernel, out_shape=(jax.ShapeDtypeStruct(drive.shape,...  8.95 us
    ppermute x3, starting transfers between devices, body(): f = lax.ppermute(f, 'z', shift(NZ, 1))  5.76 us
    ppermute x1, waiting for transfers between devices, body(): parts.append(lax.ppermute(f[:, :half], 'z', shift(NZ, 1)))  5.55 us
    ppermute x3, waiting for transfers between devices, body(): lax.ppermute(amplitudes, 'x', shift(NX, -j))  5.51 us
    ppermute x1, starting transfers between devices, body(): parts.append(lax.ppermute(b[:, half:], 'z', shift(NZ, -1)))  5.5 us
  transfers between devices with their start and end apart: 12, of which 5 were waited for; matrix products, arithmetic and copies ran while one was open for 4% of the time, Pallas kernels for 0%

profile of v2, /device:TPU:38, one launch (start us, length us, event | category | flops | bytes accessed | tf_op | source)
XLA Modules:
  0.0 106.2 jit_solution(10830883861535083752)
XLA Ops:
  7.2 0.0 copy-start.9
  7.2 0.0 copy-start.3
  7.2 0.0 all-gather.3.cloned.1.call-start
  7.2 2.0 %shard_map.95 = bf16[768,256]{1,0:T(8,128)(2,1)} custom-call(s32[64,128]{1,0:T(8,128)} %bitcast.6, bf16[512,256]{1,0:T(8,128)(2,1)} %ladder.1, bf16[256,256]{1,0:T(8,128)(2,1)} %refs_9_.1), custom_call_target="tpu_custom_call" | custom-call | bytes 1048576 | tf_op jit(solution)/shard_map/pallas_call | solution.py:41
  9.3 0.0 all-gather.3.cloned.1.call-update
  9.3 2.7 %collective-permute-start = (bf16[256,256]{1,0:T(8,128)(2,1)}, bf16[256,256]{1,0:T(8,128)(2,1)S(1)}, u32[]{:S(2)}, u32[]{:S(2)}) collective-permute-start(bf16[256,256]{1,0:T(8,128)(2,1)} %refs_9_.1), channel_id=1, source_target_pairs={{0,3},{1,0},{2,1},{3,2},{4,7},{5,4},{6,5},{7,6},{8,11},{9,8},{10,9... | collective-permute-start | bytes 393224 | tf_op jit(solution)/shard_map/ppermute | solution.py:136
  12.0 4.3 %collective-permute-start.2 = (bf16[256,256]{1,0:T(8,128)(2,1)}, bf16[256,256]{1,0:T(8,128)(2,1)S(1)}, u32[]{:S(2)}, u32[]{:S(2)}) collective-permute-start(bf16[256,256]{1,0:T(8,128)(2,1)} %refs_9_.1), channel_id=1, source_target_pairs={{0,1},{1,2},{2,3},{3,0},{4,5},{5,6},{6,7},{7,4},{8,9},{9,10},{10,1... | collective-permute-start | bytes 393224 | tf_op jit(solution)/shard_map/ppermute | solution.py:136
  16.4 2.1 %collective-permute-start.1 = (bf16[256,256]{1,0:T(8,128)(2,1)}, bf16[256,256]{1,0:T(8,128)(2,1)S(1)}, u32[]{:S(2)}, u32[]{:S(2)}) collective-permute-start(bf16[256,256]{1,0:T(8,128)(2,1)} %refs_9_.1), channel_id=1, source_target_pairs={{0,2},{1,3},{2,0},{3,1},{4,6},{5,7},{6,4},{7,5},{8,10},{9,11},{10,... | collective-permute-start | bytes 393224 | tf_op jit(solution)/shard_map/ppermute | solution.py:136
  18.5 0.9 constant_dynamic-update-slice_fusion.3
  19.4 0.0 collective-permute-done
  19.4 5.5 %collective-permute-done.1 = bf16[256,256]{1,0:T(8,128)(2,1)S(1)} collective-permute-done((bf16[256,256]{1,0:T(8,128)(2,1)}, bf16[256,256]{1,0:T(8,128)(2,1)S(1)}, u32[]{:S(2)}, u32[]{:S(2)}) %collective-permute-start.1) | collective-permute-done | bytes 131104 | tf_op jit(solution)/shard_map/ppermute | solution.py:136
  25.0 0.0 collective-permute-done.2
  25.0 0.0 copy-start.6
  25.0 10.9 %collective-permute-start.4 = (bf16[256,1024]{1,0:T(8,128)(2,1)S(1)}, bf16[256,1024]{1,0:T(8,128)(2,1)S(1)}, u32[]{:S(2)}, u32[]{:S(2)}) collective-permute-start(bf16[256,1024]{1,0:T(8,128)(2,1)S(1)} %constant_dynamic-update-slice_fusion.refs_0_), channel_id=1, source_target_pairs={{0,28},{4,0},{8,4},{12,8},{16,12},{20,16},{24,20},{28,24},{1,29},{... | collective-permute-start | bytes 1572872 | tf_op jit(solution)/shard_map/ppermute | solution.py:142
  36.0 1.9 %collective-permute-start.3 = (bf16[256,1024]{1,0:T(8,128)(2,1)S(1)}, bf16[256,1024]{1,0:T(8,128)(2,1)S(1)}, u32[]{:S(2)}, u32[]{:S(2)}) collective-permute-start(bf16[256,1024]{1,0:T(8,128)(2,1)S(1)} %constant_dynamic-update-slice_fusion.refs_0_), channel_id=1, source_target_pairs={{0,4},{4,8},{8,12},{12,16},{16,20},{20,24},{24,28},{28,0},{1,5},{5... | collective-permute-start | bytes 1572872 | tf_op jit(solution)/shard_map/ppermute | solution.py:141
  37.9 7.5 %collective-permute-done.4.refs_2_ = bf16[256,1024]{1,0:T(8,128)(2,1)S(1)} collective-permute-done((bf16[256,1024]{1,0:T(8,128)(2,1)S(1)}, bf16[256,1024]{1,0:T(8,128)(2,1)S(1)}, u32[]{:S(2)}, u32[]{:S(2)}) %collective-permute-start.4) | collective-permute-done | bytes 524320 | tf_op jit(solution)/shard_map/ppermute | solution.py:142
  45.4 0.0 copy-start.7
  45.4 5.6 %collective-permute-start.6 = (bf16[256,1024]{1,0:T(8,128)(2,1)S(1)}, bf16[256,1024]{1,0:T(8,128)(2,1)}, u32[]{:S(2)}, u32[]{:S(2)}) collective-permute-start(bf16[256,1024]{1,0:T(8,128)(2,1)S(1)} %collective-permute-done.4.refs_2_), channel_id=1, source_target_pairs={{0,28},{4,0},{8,4},{12,8},{16,12},{20,16},{24,20},{28,24},{1,29},{... | collective-permute-start | bytes 1572872 | tf_op jit(solution)/shard_map/ppermute | solution.py:142
  51.0 0.0 collective-permute-done.3.refs_1_
  51.0 0.0 copy-start.8
  51.0 1.9 %collective-permute-start.5 = (bf16[256,1024]{1,0:T(8,128)(2,1)S(1)}, bf16[256,1024]{1,0:T(8,128)(2,1)}, u32[]{:S(2)}, u32[]{:S(2)}) collective-permute-start(bf16[256,1024]{1,0:T(8,128)(2,1)S(1)} %collective-permute-done.3.refs_1_), channel_id=1, source_target_pairs={{0,4},{4,8},{8,12},{12,16},{16,20},{20,24},{24,28},{28,0},{1,5},{5... | collective-permute-start | bytes 1572872 | tf_op jit(solution)/shard_map/ppermute | solution.py:141
  53.0 6.7 %collective-permute-done.6.refs_4_ = bf16[256,1024]{1,0:T(8,128)(2,1)} collective-permute-done((bf16[256,1024]{1,0:T(8,128)(2,1)S(1)}, bf16[256,1024]{1,0:T(8,128)(2,1)}, u32[]{:S(2)}, u32[]{:S(2)}) %collective-permute-start.6) | collective-permute-done | bytes 524320 | tf_op jit(solution)/shard_map/ppermute | solution.py:142
  59.6 5.7 %collective-permute-start.8 = (bf16[256,1024]{1,0:T(8,128)(2,1)}, bf16[256,1024]{1,0:T(8,128)(2,1)S(1)}, u32[]{:S(2)}, u32[]{:S(2)}) collective-permute-start(bf16[256,1024]{1,0:T(8,128)(2,1)} %collective-permute-done.6.refs_4_), channel_id=1, source_target_pairs={{0,28},{4,0},{8,4},{12,8},{16,12},{20,16},{24,20},{28,24},{1,29},{... | collective-permute-start | bytes 1572872 | tf_op jit(solution)/shard_map/ppermute | solution.py:142
  65.3 0.0 copy-done.6
  65.3 0.0 collective-permute-done.5.refs_3_
  65.4 0.0 copy-done.7
  65.4 1.9 %collective-permute-start.7 = (bf16[256,1024]{1,0:T(8,128)(2,1)}, bf16[256,1024]{1,0:T(8,128)(2,1)S(1)}, u32[]{:S(2)}, u32[]{:S(2)}) collective-permute-start(bf16[256,1024]{1,0:T(8,128)(2,1)} %collective-permute-done.5.refs_3_), channel_id=1, source_target_pairs={{0,4},{4,8},{8,12},{12,16},{16,20},{20,24},{24,28},{28,0},{1,5},{5... | collective-permute-start | bytes 1572872 | tf_op jit(solution)/shard_map/ppermute | solution.py:141
  67.3 0.0 copy-done.8
  67.3 0.0 copy-done.9
  67.3 0.1 dynamic_slice.6
  67.4 6.0 %collective-permute-done.8.refs_6_ = bf16[256,1024]{1,0:T(8,128)(2,1)S(1)} collective-permute-done((bf16[256,1024]{1,0:T(8,128)(2,1)}, bf16[256,1024]{1,0:T(8,128)(2,1)S(1)}, u32[]{:S(2)}, u32[]{:S(2)}) %collective-permute-start.8) | collective-permute-done | bytes 524320 | tf_op jit(solution)/shard_map/ppermute | solution.py:142
  73.4 0.0 copy-start.4
  73.4 5.5 %collective-permute-start.10 = (bf16[256,512]{1,0:T(8,128)(2,1)S(1)}, bf16[256,512]{1,0:T(8,128)(2,1)}, u32[]{:S(2)}, u32[]{:S(2)}) collective-permute-start(bf16[256,512]{1,0:T(8,128)(2,1)S(1)} %slice.9), channel_id=1, source_target_pairs={{0,28},{4,0},{8,4},{12,8},{16,12},{20,16},{24,20},{28,24},{1,29},{... | collective-permute-start | bytes 786440 | tf_op jit(solution)/shard_map/ppermute | solution.py:146
  78.9 0.0 collective-permute-done.7.refs_5_
  78.9 0.0 copy-start.5
  78.9 0.8 copy-done.5
  79.7 0.7 slice.8
  80.4 0.0 copy-start.10
  80.4 0.0 copy-start
  80.4 0.0 copy-start.1
  80.4 0.0 copy-start.2
  80.4 2.1 %collective-permute-start.9 = (bf16[256,512]{1,0:T(8,128)(2,1)}, bf16[256,512]{1,0:T(8,128)(2,1)}, u32[]{:S(2)}, u32[]{:S(2)}) collective-permute-start(bf16[256,512]{1,0:T(8,128)(2,1)} %slice.8), channel_id=1, source_target_pairs={{0,4},{4,8},{8,12},{12,16},{16,20},{20,24},{24,28},{28,0},{1,5},{5... | collective-permute-start | bytes 786440 | tf_op jit(solution)/shard_map/ppermute | solution.py:145
  82.5 0.0 copy-done.3
  82.5 1.9 %compare_select_fusion.hole = bf16[256,4096]{1,0:T(8,128)(2,1)} fusion(bf16[256,4096]{1,0:T(8,128)(2,1)S(1)} %copy-done.3, s32[4096]{0:T(1024)S(1)} %copy-done.9, s32[256]{0:T(256)S(1)} %dynamic_slice.6), kind=kLoop, calls=%fused_computation | loop fusion | flops 2097152 | bytes 4211712 | tf_op jit(solution)/shard_map/jit(_where)/select_n | solution.py:149
  84.4 0.0 copy-done.4
  84.4 0.0 copy-done.10
  84.4 0.1 broadcast_add_fusion
  84.5 0.1 add.30
  84.6 0.1 dynamic_slice.7
  84.6 0.1 copy.10.refs_11_
  84.8 0.0 collective-permute-done.10.refs_8_
  84.8 5.6 %collective-permute-done.9.refs_7_ = bf16[256,512]{1,0:T(8,128)(2,1)} collective-permute-done((bf16[256,512]{1,0:T(8,128)(2,1)}, bf16[256,512]{1,0:T(8,128)(2,1)}, u32[]{:S(2)}, u32[]{:S(2)}) %collective-permute-start.9) | collective-permute-done | bytes 262176 | tf_op jit(solution)/shard_map/ppermute | solution.py:145
  90.3 0.0 all-gather.3.cloned.1.call-done
  90.4 0.0 copy-done
  90.4 0.0 copy-done.1
  90.4 0.0 copy-done.2
  90.4 8.9 %shard_map.96 = (f32[256,256]{1,0:T(8,128)}, bf16[256,256]{1,0:T(8,128)(2,1)}) custom-call(bf16[16,768,256]{2,1,0:T(8,128)(2,1)} %bitcast.5, bf16[256,4096]{1,0:T(8,128)(2,1)} %compare_select_fusion.hole, bf16[256,1024]{1,0:T(8,128)(2,1)} %copy-done.6, bf16[256,1024]{1,0:T(8,128)(2,1)} %copy-done.8, bf16[256,1024]{1,0:T(8,128)(2,1)} %copy-done.7, ...), custom_call_target="tpu_custom_call" | custom-call | flops 1610612736 | bytes 13631488 | tf_op jit(solution)/shard_map/pallas_call | solution.py:105
  (4 shorter events, 0.0 us)
Async XLA Ops:
  7.2 60.1 %copy-start.9 = (s32[4096]{0:T(1024)S(1)}, s32[4096]{0:T(1024)}, u32[]{:S(2)}) copy-start(s32[4096]{0:T(1024)} %param.11) | copy-start | bytes 49156
  7.2 75.3 %copy-start.3 = (bf16[256,4096]{1,0:T(8,128)(2,1)S(1)}, bf16[256,4096]{1,0:T(8,128)(2,1)}, u32[]{:S(2)}) copy-start(bf16[256,4096]{1,0:T(8,128)(2,1)} %param.13) | copy-start | bytes 6291460
  7.2 83.2 %all-gather.3.cloned.1.call-start = ((), (), s32[]{:S(2)}) async-start(), calls=%async_computation | async-start | bytes 6684672 | tf_op jit(solution)/shard_map/all_gather | solution.py:134
  9.3 10.1 %collective-permute-start = (bf16[256,256]{1,0:T(8,128)(2,1)}, bf16[256,256]{1,0:T(8,128)(2,1)S(1)}, u32[]{:S(2)}, u32[]{:S(2)}) collective-permute-start(bf16[256,256]{1,0:T(8,128)(2,1)} %refs_9_.1), channel_id=1, source_target_pairs={{0,3},{1,0},{2,1},{3,2},{4,7},{5,4},{6,5},{7,6},{8,11},{9,8},{10,9... | collective-permute-start | bytes 393224 | tf_op jit(solution)/shard_map/ppermute | solution.py:136
  12.0 12.9 %collective-permute-start.2 = (bf16[256,256]{1,0:T(8,128)(2,1)}, bf16[256,256]{1,0:T(8,128)(2,1)S(1)}, u32[]{:S(2)}, u32[]{:S(2)}) collective-permute-start(bf16[256,256]{1,0:T(8,128)(2,1)} %refs_9_.1), channel_id=1, source_target_pairs={{0,1},{1,2},{2,3},{3,0},{4,5},{5,6},{6,7},{7,4},{8,9},{9,10},{10,1... | collective-permute-start | bytes 393224 | tf_op jit(solution)/shard_map/ppermute | solution.py:136
  16.4 8.6 %collective-permute-start.1 = (bf16[256,256]{1,0:T(8,128)(2,1)}, bf16[256,256]{1,0:T(8,128)(2,1)S(1)}, u32[]{:S(2)}, u32[]{:S(2)}) collective-permute-start(bf16[256,256]{1,0:T(8,128)(2,1)} %refs_9_.1), channel_id=1, source_target_pairs={{0,2},{1,3},{2,0},{3,1},{4,6},{5,7},{6,4},{7,5},{8,10},{9,11},{10,... | collective-permute-start | bytes 393224 | tf_op jit(solution)/shard_map/ppermute | solution.py:136
  25.0 40.4 %copy-start.6 = (bf16[256,1024]{1,0:T(8,128)(2,1)}, bf16[256,1024]{1,0:T(8,128)(2,1)S(1)}, u32[]{:S(2)}) copy-start(bf16[256,1024]{1,0:T(8,128)(2,1)S(1)} %constant_dynamic-update-slice_fusion.refs_0_) | copy-start | bytes 1572868
  25.0 20.4 %collective-permute-start.4 = (bf16[256,1024]{1,0:T(8,128)(2,1)S(1)}, bf16[256,1024]{1,0:T(8,128)(2,1)S(1)}, u32[]{:S(2)}, u32[]{:S(2)}) collective-permute-start(bf16[256,1024]{1,0:T(8,128)(2,1)S(1)} %constant_dynamic-update-slice_fusion.refs_0_), channel_id=1, source_target_pairs={{0,28},{4,0},{8,4},{12,8},{16,12},{20,16},{24,20},{28,24},{1,29},{... | collective-permute-start | bytes 1572872 | tf_op jit(solution)/shard_map/ppermute | solution.py:142
  36.0 15.1 %collective-permute-start.3 = (bf16[256,1024]{1,0:T(8,128)(2,1)S(1)}, bf16[256,1024]{1,0:T(8,128)(2,1)S(1)}, u32[]{:S(2)}, u32[]{:S(2)}) collective-permute-start(bf16[256,1024]{1,0:T(8,128)(2,1)S(1)} %constant_dynamic-update-slice_fusion.refs_0_), channel_id=1, source_target_pairs={{0,4},{4,8},{8,12},{12,16},{16,20},{20,24},{24,28},{28,0},{1,5},{5... | collective-permute-start | bytes 1572872 | tf_op jit(solution)/shard_map/ppermute | solution.py:141
  45.4 20.0 %copy-start.7 = (bf16[256,1024]{1,0:T(8,128)(2,1)}, bf16[256,1024]{1,0:T(8,128)(2,1)S(1)}, u32[]{:S(2)}) copy-start(bf16[256,1024]{1,0:T(8,128)(2,1)S(1)} %collective-permute-done.4.refs_2_) | copy-start | bytes 1572868
  45.4 14.2 %collective-permute-start.6 = (bf16[256,1024]{1,0:T(8,128)(2,1)S(1)}, bf16[256,1024]{1,0:T(8,128)(2,1)}, u32[]{:S(2)}, u32[]{:S(2)}) collective-permute-start(bf16[256,1024]{1,0:T(8,128)(2,1)S(1)} %collective-permute-done.4.refs_2_), channel_id=1, source_target_pairs={{0,28},{4,0},{8,4},{12,8},{16,12},{20,16},{24,20},{28,24},{1,29},{... | collective-permute-start | bytes 1572872 | tf_op jit(solution)/shard_map/ppermute | solution.py:142
  51.0 16.3 %copy-start.8 = (bf16[256,1024]{1,0:T(8,128)(2,1)}, bf16[256,1024]{1,0:T(8,128)(2,1)S(1)}, u32[]{:S(2)}) copy-start(bf16[256,1024]{1,0:T(8,128)(2,1)S(1)} %collective-permute-done.3.refs_1_) | copy-start | bytes 1572868
  51.0 14.3 %collective-permute-start.5 = (bf16[256,1024]{1,0:T(8,128)(2,1)S(1)}, bf16[256,1024]{1,0:T(8,128)(2,1)}, u32[]{:S(2)}, u32[]{:S(2)}) collective-permute-start(bf16[256,1024]{1,0:T(8,128)(2,1)S(1)} %collective-permute-done.3.refs_1_), channel_id=1, source_target_pairs={{0,4},{4,8},{8,12},{12,16},{16,20},{20,24},{24,28},{28,0},{1,5},{5... | collective-permute-start | bytes 1572872 | tf_op jit(solution)/shard_map/ppermute | solution.py:141
  59.6 13.7 %collective-permute-start.8 = (bf16[256,1024]{1,0:T(8,128)(2,1)}, bf16[256,1024]{1,0:T(8,128)(2,1)S(1)}, u32[]{:S(2)}, u32[]{:S(2)}) collective-permute-start(bf16[256,1024]{1,0:T(8,128)(2,1)} %collective-permute-done.6.refs_4_), channel_id=1, source_target_pairs={{0,28},{4,0},{8,4},{12,8},{16,12},{20,16},{24,20},{28,24},{1,29},{... | collective-permute-start | bytes 1572872 | tf_op jit(solution)/shard_map/ppermute | solution.py:142
  65.4 13.5 %collective-permute-start.7 = (bf16[256,1024]{1,0:T(8,128)(2,1)}, bf16[256,1024]{1,0:T(8,128)(2,1)S(1)}, u32[]{:S(2)}, u32[]{:S(2)}) collective-permute-start(bf16[256,1024]{1,0:T(8,128)(2,1)} %collective-permute-done.5.refs_3_), channel_id=1, source_target_pairs={{0,4},{4,8},{8,12},{12,16},{16,20},{20,24},{24,28},{28,0},{1,5},{5... | collective-permute-start | bytes 1572872 | tf_op jit(solution)/shard_map/ppermute | solution.py:141
  73.4 11.1 %copy-start.4 = (bf16[256,1024]{1,0:T(8,128)(2,1)}, bf16[256,1024]{1,0:T(8,128)(2,1)S(1)}, u32[]{:S(2)}) copy-start(bf16[256,1024]{1,0:T(8,128)(2,1)S(1)} %collective-permute-done.8.refs_6_) | copy-start | bytes 1572868
  73.4 11.4 %collective-permute-start.10 = (bf16[256,512]{1,0:T(8,128)(2,1)S(1)}, bf16[256,512]{1,0:T(8,128)(2,1)}, u32[]{:S(2)}, u32[]{:S(2)}) collective-permute-start(bf16[256,512]{1,0:T(8,128)(2,1)S(1)} %slice.9), channel_id=1, source_target_pairs={{0,28},{4,0},{8,4},{12,8},{16,12},{20,16},{24,20},{28,24},{1,29},{... | collective-permute-start | bytes 786440 | tf_op jit(solution)/shard_map/ppermute | solution.py:146
  78.9 0.8 copy-start.5
  80.4 4.0 %copy-start.10 = (f32[64]{0:T(128)S(1)}, f32[64]{0:T(128)}, u32[]{:S(2)}) copy-start(f32[64]{0:T(128)} %param.14) | copy-start | bytes 772
  80.4 9.9 %copy-start = (bf16[256,256]{1,0:T(8,128)(2,1)S(1)}, bf16[256,256]{1,0:T(8,128)(2,1)}, u32[]{:S(2)}) copy-start(bf16[256,256]{1,0:T(8,128)(2,1)} %refs_9_.1) | copy-start | bytes 393220
  80.4 9.9 %copy-start.1 = (f32[256,256]{1,0:T(8,128)S(1)}, f32[256,256]{1,0:T(8,128)}, u32[]{:S(2)}) copy-start(f32[256,256]{1,0:T(8,128)} %refs_10_.1) | copy-start | bytes 786436
  80.4 9.9 %copy-start.2 = (f32[256]{0:T(256)S(1)}, f32[256]{0:T(256)}, u32[]{:S(2)}) copy-start(f32[256]{0:T(256)} %param.15) | copy-start | bytes 3076
  80.4 9.9 %collective-permute-start.9 = (bf16[256,512]{1,0:T(8,128)(2,1)}, bf16[256,512]{1,0:T(8,128)(2,1)}, u32[]{:S(2)}, u32[]{:S(2)}) collective-permute-start(bf16[256,512]{1,0:T(8,128)(2,1)} %slice.8), channel_id=1, source_target_pairs={{0,4},{4,8},{8,12},{12,16},{16,20},{20,24},{24,28},{28,0},{1,5},{5... | collective-permute-start | bytes 786440 | tf_op jit(solution)/shard_map/ppermute | solution.py:145
Sparse Core Ops, SparseCore 0:
  10.1 50.3 all-gather.2

commit v3 on v2

v3 whole, which is shorter than its diff:
```python
import jax
import jax.numpy as jnp
from jax import lax
from jax.experimental import pallas as pl
from jax.experimental.pallas import tpu as pltpu
from jax.sharding import Mesh, PartitionSpec as P

NY, NCORE, NZ, NX = 8, 2, 8, 4
BF16, F32 = jnp.bfloat16, jnp.float32
LANES = 128


def shift(n, by):
    return [(i, (i + by) % n) for i in range(n)]


def row_rank():
    return lax.axis_index("y") * NCORE + lax.axis_index("core")


def kept_block():
    x = lax.axis_index("x")
    inner = jnp.logical_or(x == 1, x == 2).astype(jnp.int32)
    return lax.rem(inner + lax.axis_index("core"), 2)


def masked_block(labels, ladder, block, write):
    r = row_rank()
    c = lax.axis_index("z") * NX + lax.axis_index("x")
    size = ladder.shape[0] // 2
    lines, cols = size // LANES, ladder.shape[1] // LANES
    col_labels = [labels[pl.ds(c * cols + q, 1), :].astype(F32) for q in range(cols)]
    for k in range(lines):
        line = labels[pl.ds((2 * r + block) * lines + k, 1), :].astype(F32)
        row_labels = jnp.broadcast_to(line, (LANES, LANES)).T
        at = pl.ds(pl.multiple_of(block * size + k * LANES, LANES), LANES)
        for q in range(cols):
            lanes = slice(q * LANES, (q + 1) * LANES)
            values = ladder[at, lanes].astype(F32)
            kept = jnp.where(row_labels == col_labels[q], values, 0.0)
            write(slice(k * LANES, (k + 1) * LANES), lanes, kept.astype(BF16))


def send_kernel(labels, ladder, out_ref):
    def write(rows, lanes, values):
        out_ref[rows, lanes] = values

    masked_block(labels, ladder, 1 - kept_block(), write)


def rows_kernel(labels, ladder, amps, out_ref):
    def write(rows, lanes, values):
        out_ref[rows, lanes] = values

    masked_block(labels, ladder, kept_block(), write)
    size = amps.shape[0]
    out_ref[size : 2 * size, :] = amps[...]
    out_ref[2 * size :, :] = jnp.zeros_like(amps)


def prepare(kernel, rows, *args):
    vmem = pl.BlockSpec(memory_space=pltpu.VMEM)
    return pl.pallas_call(
        kernel,
        out_shape=jax.ShapeDtypeStruct((rows, args[1].shape[1]), BF16),
        in_specs=[vmem] * len(args),
        out_specs=vmem,
        cost_estimate=pl.CostEstimate(flops=0, bytes_accessed=1 << 20, transcendentals=0),
    )(*args)


def ladder_copies(gathered, first_row, parts, parts_v, part_sems, rows_v, row_sems, size):
    z, x = lax.axis_index("z"), lax.axis_index("x")
    upper = (x >= NX // 2).astype(jnp.int32)
    opposite = lax.rem(z + NZ // 2, NZ)
    sources = [(lax.rem(z + NZ + away, NZ), (0, 1)) for away in (0, -1, 1, -2, 2, -3, 3)]
    sources += [(opposite, (0,)), (opposite, (1,))]
    copies, at = [], 0
    for i, (slot, blocks) in enumerate(sources):
        mine = [pltpu.make_async_copy(parts[i], parts_v[i], part_sems.at[i])]
        for j in blocks:
            r = 2 * slot + (upper if j == 0 else 1 - upper)
            src = gathered.at[r, pl.ds(first_row, size)]
            dst = rows_v.at[pl.ds(at, size)]
            mine.append(pltpu.make_async_copy(src, dst, row_sems.at[at // size]))
            at += size
        copies.append(mine)
    return copies


def add_ladder(copies, parts_v, rows_v, acc, size):
    at = 0
    for i, mine in enumerate(copies):
        for copy in mine:
            copy.wait()
        depth = size * (len(mine) - 1)
        acc[...] += jnp.dot(parts_v[i][...], rows_v[at : at + depth, :], preferred_element_type=F32)
        at += depth


def partner_kernel(gathered, *refs):
    parts, out_ref = refs[:9], refs[9]
    rows_v, parts_v, row_sems, part_sems = refs[10:]
    size = out_ref.shape[0]
    copies = ladder_copies(gathered, 2 * size, parts, parts_v, part_sems, rows_v, row_sems, size)
    for mine in copies:
        for copy in mine:
            copy.start()
    out_ref[...] = jnp.zeros_like(out_ref)
    add_ladder(copies, parts_v, rows_v, out_ref, size)


def own_kernel(gathered, hole, *refs):
    parts, drive, out_ref = refs[:9], refs[9], refs[10]
    rows_v, amps_rows_v, hole_v, parts_v, row_sems, amps_sems, hole_sems, part_sems = refs[11:]
    n, size = gathered.shape[0], out_ref.shape[0]
    group = n // len(hole_v)
    hole_copies = []
    for g in range(len(hole_v)):
        src = hole.at[:, pl.ds(g * group * size, group * size)]
        mine = [pltpu.make_async_copy(src, hole_v[g], hole_sems.at[g])]
        for r in range(g * group, (g + 1) * group):
            src = gathered.at[r, pl.ds(size, size)]
            dst = amps_rows_v.at[pl.ds(r * size, size)]
            mine.append(pltpu.make_async_copy(src, dst, amps_sems.at[r]))
        hole_copies.append(mine)
    copies = ladder_copies(gathered, 0, parts, parts_v, part_sems, rows_v, row_sems, size)
    for mine in hole_copies + copies:
        for copy in mine:
            copy.start()
    out_ref[...] = drive[...]
    for g, mine in enumerate(hole_copies):
        for copy in mine:
            copy.wait()
        at = pl.ds(g * group * size, group * size)
        out_ref[...] += jnp.dot(hole_v[g][...], amps_rows_v[at], preferred_element_type=F32)
    add_ladder(copies, parts_v, rows_v, out_ref, size)


def products(kernel, gathered, hole, parts, drive):
    hbm = pl.BlockSpec(memory_space=pltpu.HBM)
    vmem = pl.BlockSpec(memory_space=pltpu.VMEM)
    n, _, cols = gathered.shape
    size, groups = drive.shape[0], 4
    with_hole = hole is not None
    arrays = (gathered, hole, *parts) if with_hole else (gathered, *parts)
    in_hbm = [pltpu.with_memory_space_constraint(a, pltpu.HBM) for a in arrays]
    scratch = [pltpu.VMEM((n * size, cols), BF16)]
    sems = [pltpu.SemaphoreType.DMA((n,))]
    if with_hole:
        scratch.append(pltpu.VMEM((n * size, cols), BF16))
        scratch.append([pltpu.VMEM((size, n * size // groups), BF16) for _ in range(groups)])
        sems += [pltpu.SemaphoreType.DMA((n,)), pltpu.SemaphoreType.DMA((groups,))]
    scratch.append([pltpu.VMEM(p.shape, BF16) for p in parts])
    sems.append(pltpu.SemaphoreType.DMA((len(parts),)))
    depth = (2 if with_hole else 1) * n * size
    return pl.pallas_call(
        kernel,
        out_shape=jax.ShapeDtypeStruct(drive.shape, F32),
        in_specs=[hbm] * len(in_hbm) + ([vmem] if with_hole else []),
        out_specs=vmem,
        scratch_shapes=scratch + sems,
        compiler_params=pltpu.CompilerParams(vmem_limit_bytes=32 << 20),
        cost_estimate=pl.CostEstimate(
            flops=2 * size * cols * depth, bytes_accessed=4 * size * depth, transcendentals=0
        ),
    )(*in_hbm, *([drive] if with_hole else []))


def body(amplitudes, drive, pair_irrep, occ_irrep, ladder_ints, hole_ints, occ_energy, pair_energy):
    size = amplitudes.shape[0]
    labels = pair_irrep.reshape(-1, LANES)
    partner = [(i, i ^ 1) for i in range(NX)]
    lent = lax.ppermute(prepare(send_kernel, size, labels, ladder_ints), "x", partner)
    rows = prepare(rows_kernel, 3 * size, labels, ladder_ints, amplitudes)
    rows = lax.dynamic_update_slice(rows, lent, (2 * size, 0))
    gathered = lax.all_gather(rows, ("y", "core"), axis=0, tiled=False)

    other = lax.ppermute(amplitudes, "x", [(i, NX - 1 - i) for i in range(NX)])
    own = jnp.concatenate([amplitudes, other], axis=1)
    f, b = own, own
    parts = [own]
    for _ in range(NZ // 2 - 1):
        f = lax.ppermute(f, "z", shift(NZ, 1))
        b = lax.ppermute(b, "z", shift(NZ, -1))
        parts += [f, b]
    parts.append(lax.ppermute(f[:, :size], "z", shift(NZ, 1)))
    parts.append(lax.ppermute(b[:, size:], "z", shift(NZ, -1)))

    own_occ = lax.dynamic_slice_in_dim(occ_irrep, row_rank() * size, size)
    hole_kept = jnp.where(
        own_occ[:, None] == occ_irrep[None, :], hole_ints, jnp.zeros_like(hole_ints)
    )
    pair_occ = (occ_energy[:, None] + occ_energy[None, :]).reshape(-1)
    own_energy = lax.dynamic_slice_in_dim(pair_occ, row_rank() * size, size)
    denominator = pair_energy[None, :] - own_energy[:, None]
    for_partner = products(partner_kernel, gathered, None, parts, drive)
    from_partner = lax.ppermute(for_partner, "x", partner)
    residual = products(own_kernel, gathered, hole_kept, parts, drive) + from_partner
    updated = (amplitudes.astype(F32) - residual / denominator).astype(BF16)
    return residual, updated


def solution(mesh):
    fine = Mesh(mesh.devices.reshape(NY, NCORE, NZ, NX), ("y", "core", "z", "x"))
    row, col = ("y", "core"), ("z", "x")
    in_specs = (
        P(row, col),
        P(row, col),
        P(),
        P(),
        P(row, col),
        P(row, None),
        P(),
        P(col),
    )
    out_specs = (P(row, col), P(row, col))
    return jax.shard_map(body, mesh=fine, in_specs=in_specs, out_specs=out_specs, check_vma=False)
```

time: 107 us -> 92.5 us (0.86)
  the two profiles are of different devices: /device:TPU:38 before, /device:TPU:1 now
where the time goes in v3:
time: 92.5 us; the launch traced here: 92 us
  starting transfers between devices  44.5 us (48%)
  waiting for transfers between devices  15.7 us (17%)
  between operations  14.3 us (15%)
  Pallas kernels  12.8 us (14%)
  other arithmetic  2.8 us (3%)
  local copies, waits for them, and re-layouts  1.9 us (2%)
    ppermute x3, starting transfers between devices, body(): b = lax.ppermute(b, 'z', shift(NZ, -1))  17.7 us
    pallas_call x2, Pallas kernels, products(): pl.pallas_call(kernel, out_shape=jax.ShapeDtypeStruct(drive.shape, F32),...  9.01 us
    ppermute x3, starting transfers between devices, body(): f = lax.ppermute(f, 'z', shift(NZ, 1))  8 us
    all_gather x1, waiting for transfers between devices, body(): gathered = lax.all_gather(rows, ('y', 'core'), axis=0, tiled=False)  6.78 us
    ppermute x3, waiting for transfers between devices, body(): f = lax.ppermute(f, 'z', shift(NZ, 1))  6.33 us
    ppermute x1, starting transfers between devices, body(): other = lax.ppermute(amplitudes, 'x', [(i, NX - 1 - i) for i in range(NX)])  5.18 us
    ppermute x1, starting transfers between devices, body(): parts.append(lax.ppermute(b[:, size:], 'z', shift(NZ, -1)))  4.57 us
    ppermute x1, starting transfers between devices, body(): lax.ppermute(prepare(send_kernel, size, labels, ladder_ints), 'x', partner)  3.94 us
  transfers between devices with their start and end apart: 12, of which 7 were waited for; matrix products, arithmetic and copies ran while one was open for 3% of the time, Pallas kernels for 8%

profile of v3, /device:TPU:1, one launch (start us, length us, event | category | flops | bytes accessed | tf_op | source)
XLA Modules:
  0.0 92.0 jit_solution(8981092885675538509)
XLA Ops:
  7.2 0.0 copy-start.9
  7.2 0.0 copy-start.1
  7.2 0.0 all-gather.2.cloned.1.call-start
  7.2 1.9 %shard_map.96 = bf16[256,256]{1,0:T(8,128)(2,1)} custom-call(s32[64,128]{1,0:T(8,128)} %bitcast.5, bf16[512,256]{1,0:T(8,128)(2,1)} %ladder.3), custom_call_target="tpu_custom_call" | custom-call | bytes 1048576 | tf_op jit(solution)/shard_map/pallas_call | solution.py:63
  9.1 3.9 %collective-permute-start = (bf16[256,256]{1,0:T(8,128)(2,1)}, bf16[256,256]{1,0:T(8,128)(2,1)S(1)}, u32[]{:S(2)}, u32[]{:S(2)}) collective-permute-start(bf16[256,256]{1,0:T(8,128)(2,1)} %shard_map.96), channel_id=1, source_target_pairs={{0,1},{1,0},{2,3},{3,2},{4,5},{5,4},{6,7},{7,6},{8,9},{9,8},{10,11... | collective-permute-start | bytes 393224 | tf_op jit(solution)/shard_map/ppermute | solution.py:174
  13.0 1.9 %shard_map.95 = bf16[768,256]{1,0:T(8,128)(2,1)} custom-call(s32[64,128]{1,0:T(8,128)} %bitcast.6, bf16[512,256]{1,0:T(8,128)(2,1)} %ladder.3, bf16[256,256]{1,0:T(8,128)(2,1)} %amps.1), custom_call_target="tpu_custom_call" | custom-call | bytes 1048576 | tf_op jit(solution)/shard_map/pallas_call | solution.py:63
  15.0 0.6 collective-permute-done
  15.6 0.7 bitcast_dynamic-update-slice_fusion
  16.3 0.0 all-gather.2.cloned.1.call-update
  16.3 5.2 %collective-permute-start.1 = (bf16[256,256]{1,0:T(8,128)(2,1)}, bf16[256,256]{1,0:T(8,128)(2,1)S(1)}, u32[]{:S(2)}, u32[]{:S(2)}) collective-permute-start(bf16[256,256]{1,0:T(8,128)(2,1)} %amps.1), channel_id=1, source_target_pairs={{0,3},{1,2},{2,1},{3,0},{4,7},{5,6},{6,5},{7,4},{8,11},{9,10},{10,... | collective-permute-start | bytes 393224 | tf_op jit(solution)/shard_map/ppermute | solution.py:179
  21.5 0.9 %constant_dynamic-update-slice_fusion.1 = bf16[256,512]{1,0:T(8,128)(2,1)S(1)} fusion(bf16[256,256]{1,0:T(8,128)(2,1)} %amps.1), kind=kLoop, calls=%fused_computation.5 | loop fusion | bytes 262144
  22.4 1.6 %collective-permute-done.1 = bf16[256,256]{1,0:T(8,128)(2,1)S(1)} collective-permute-done((bf16[256,256]{1,0:T(8,128)(2,1)}, bf16[256,256]{1,0:T(8,128)(2,1)S(1)}, u32[]{:S(2)}, u32[]{:S(2)}) %collective-permute-start.1) | collective-permute-done | bytes 131104 | tf_op jit(solution)/shard_map/ppermute | solution.py:179
  24.0 0.0 copy-start.4
  24.0 4.2 %collective-permute-start.2 = (bf16[256,512]{1,0:T(8,128)(2,1)S(1)}, bf16[256,512]{1,0:T(8,128)(2,1)S(1)}, u32[]{:S(2)}, u32[]{:S(2)}) collective-permute-start(bf16[256,512]{1,0:T(8,128)(2,1)S(1)} %constant_dynamic-update-slice_fusion.refs_0_), channel_id=1, source_target_pairs={{0,4},{4,8},{8,12},{12,16},{16,20},{20,24},{24,28},{28,0},{1,5},{5... | collective-permute-start | bytes 786440 | tf_op jit(solution)/shard_map/ppermute | solution.py:184
  28.2 8.6 %collective-permute-start.3 = (bf16[256,512]{1,0:T(8,128)(2,1)S(1)}, bf16[256,512]{1,0:T(8,128)(2,1)S(1)}, u32[]{:S(2)}, u32[]{:S(2)}) collective-permute-start(bf16[256,512]{1,0:T(8,128)(2,1)S(1)} %constant_dynamic-update-slice_fusion.refs_0_), channel_id=1, source_target_pairs={{0,28},{4,0},{8,4},{12,8},{16,12},{20,16},{24,20},{28,24},{1,29},{... | collective-permute-start | bytes 786440 | tf_op jit(solution)/shard_map/ppermute | solution.py:185
  36.8 1.8 %collective-permute-done.2.refs_1_ = bf16[256,512]{1,0:T(8,128)(2,1)S(1)} collective-permute-done((bf16[256,512]{1,0:T(8,128)(2,1)S(1)}, bf16[256,512]{1,0:T(8,128)(2,1)S(1)}, u32[]{:S(2)}, u32[]{:S(2)}) %collective-permute-start.2) | collective-permute-done | bytes 262176 | tf_op jit(solution)/shard_map/ppermute | solution.py:184
  38.7 0.0 copy-start.6
  38.7 1.9 %collective-permute-start.4 = (bf16[256,512]{1,0:T(8,128)(2,1)S(1)}, bf16[256,512]{1,0:T(8,128)(2,1)}, u32[]{:S(2)}, u32[]{:S(2)}) collective-permute-start(bf16[256,512]{1,0:T(8,128)(2,1)S(1)} %collective-permute-done.2.refs_1_), channel_id=1, source_target_pairs={{0,4},{4,8},{8,12},{12,16},{16,20},{20,24},{24,28},{28,0},{1,5},{5... | collective-permute-start | bytes 786440 | tf_op jit(solution)/shard_map/ppermute | solution.py:184
  40.6 0.0 collective-permute-done.3.refs_2_
  40.6 0.0 copy-start.7
  40.6 4.6 %collective-permute-start.5 = (bf16[256,512]{1,0:T(8,128)(2,1)S(1)}, bf16[256,512]{1,0:T(8,128)(2,1)}, u32[]{:S(2)}, u32[]{:S(2)}) collective-permute-start(bf16[256,512]{1,0:T(8,128)(2,1)S(1)} %collective-permute-done.3.refs_2_), channel_id=1, source_target_pairs={{0,28},{4,0},{8,4},{12,8},{16,12},{20,16},{24,20},{28,24},{1,29},{... | collective-permute-start | bytes 786440 | tf_op jit(solution)/shard_map/ppermute | solution.py:185
  45.2 2.2 %collective-permute-done.4.refs_3_ = bf16[256,512]{1,0:T(8,128)(2,1)} collective-permute-done((bf16[256,512]{1,0:T(8,128)(2,1)S(1)}, bf16[256,512]{1,0:T(8,128)(2,1)}, u32[]{:S(2)}, u32[]{:S(2)}) %collective-permute-start.4) | collective-permute-done | bytes 262176 | tf_op jit(solution)/shard_map/ppermute | solution.py:184
  47.4 1.9 %collective-permute-start.6 = (bf16[256,512]{1,0:T(8,128)(2,1)}, bf16[256,512]{1,0:T(8,128)(2,1)S(1)}, u32[]{:S(2)}, u32[]{:S(2)}) collective-permute-start(bf16[256,512]{1,0:T(8,128)(2,1)} %collective-permute-done.4.refs_3_), channel_id=1, source_target_pairs={{0,4},{4,8},{8,12},{12,16},{16,20},{20,24},{24,28},{28,0},{1,5},{5... | collective-permute-start | bytes 786440 | tf_op jit(solution)/shard_map/ppermute | solution.py:184
  49.3 0.0 collective-permute-done.5.refs_4_
  49.3 4.6 %collective-permute-start.7 = (bf16[256,512]{1,0:T(8,128)(2,1)}, bf16[256,512]{1,0:T(8,128)(2,1)S(1)}, u32[]{:S(2)}, u32[]{:S(2)}) collective-permute-start(bf16[256,512]{1,0:T(8,128)(2,1)} %collective-permute-done.5.refs_4_), channel_id=1, source_target_pairs={{0,28},{4,0},{8,4},{12,8},{16,12},{20,16},{24,20},{28,24},{1,29},{... | collective-permute-start | bytes 786440 | tf_op jit(solution)/shard_map/ppermute | solution.py:185
  53.9 0.0 copy-done.9
  53.9 0.1 dynamic_slice.6
  54.0 2.3 %collective-permute-done.6.refs_5_ = bf16[256,512]{1,0:T(8,128)(2,1)S(1)} collective-permute-done((bf16[256,512]{1,0:T(8,128)(2,1)}, bf16[256,512]{1,0:T(8,128)(2,1)S(1)}, u32[]{:S(2)}, u32[]{:S(2)}) %collective-permute-start.6) | collective-permute-done | bytes 262176 | tf_op jit(solution)/shard_map/ppermute | solution.py:184
  56.3 0.0 copy-start.2
  56.3 1.9 %collective-permute-start.8 = (bf16[256,256]{1,0:T(8,128)(2,1)S(1)}, bf16[256,256]{1,0:T(8,128)(2,1)S(1)}, u32[]{:S(2)}, u32[]{:S(2)}) collective-permute-start(bf16[256,256]{1,0:T(8,128)(2,1)S(1)} %slice.8), channel_id=1, source_target_pairs={{0,4},{4,8},{8,12},{12,16},{16,20},{20,24},{24,28},{28,0},{1,5},{5... | collective-permute-start | bytes 393224 | tf_op jit(solution)/shard_map/ppermute | solution.py:187
  58.2 0.0 collective-permute-done.7.refs_6_
  58.3 0.0 copy-start.3
  58.3 4.6 %collective-permute-start.9 = (bf16[256,256]{1,0:T(8,128)(2,1)S(1)}, bf16[256,256]{1,0:T(8,128)(2,1)}, u32[]{:S(2)}, u32[]{:S(2)}) collective-permute-start(bf16[256,256]{1,0:T(8,128)(2,1)S(1)} %slice.9), channel_id=1, source_target_pairs={{0,28},{4,0},{8,4},{12,8},{16,12},{20,16},{24,20},{28,24},{1,29},{... | collective-permute-start | bytes 393224 | tf_op jit(solution)/shard_map/ppermute | solution.py:188
  62.9 0.0 copy-done.1
  62.9 1.9 %compare_select_fusion.hole = bf16[256,4096]{1,0:T(8,128)(2,1)} fusion(bf16[256,4096]{1,0:T(8,128)(2,1)S(1)} %copy-done.1, s32[4096]{0:T(1024)S(1)} %copy-done.9, s32[256]{0:T(256)S(1)} %dynamic_slice.6), kind=kLoop, calls=%fused_computation | loop fusion | flops 2097152 | bytes 4211712 | tf_op jit(solution)/shard_map/jit(_where)/select_n | solution.py:191
  64.8 0.0 copy-done.4
  64.8 0.0 copy-done.6
  64.8 0.0 copy-done.7
  64.8 0.0 copy-done.2
  64.8 0.0 copy-done.3
  64.8 0.0 copy-start.10
  64.9 0.0 copy-start
  64.9 0.0 collective-permute-done.8.refs_7_
  64.9 0.0 copy-start.8
  64.9 0.0 collective-permute-done.9.refs_8_
  64.9 6.8 %all-gather.2.cloned.1.call-done.gathered = bf16[16,768,256]{2,1,0:T(8,128)(2,1)} async-done(((bf16[1,768,256]{2,1,0:T(8,128)(2,1)}), bf16[16,768,256]{2,1,0:T(8,128)(2,1)}) %all-gather.2.cloned.1.call-update) | async-done | bytes 6291472 | tf_op jit(solution)/shard_map/all_gather | solution.py:177
  71.7 0.0 copy-done.8
  71.7 3.2 %shard_map.98 = f32[256,256]{1,0:T(8,128)S(1)} custom-call(bf16[16,768,256]{2,1,0:T(8,128)(2,1)} %all-gather.2.cloned.1.call-done.gathered, bf16[256,512]{1,0:T(8,128)(2,1)} %copy-done.4, bf16[256,512]{1,0:T(8,128)(2,1)} %copy-done.6, bf16[256,512]{1,0:T(8,128)(2,1)} %copy-done.7, bf16[256,512]{1,0:T(8,128)(2,1)} %collective-permute-done.4.refs_3_, ...), custom_call_target="tpu_custom_call" | custom-call | flops 536870912 | bytes 4194304 | tf_op jit(solution)/shard_map/pallas_call | solution.py:157
  74.9 3.1 %collective-permute-start.10 = (f32[256,256]{1,0:T(8,128)S(1)}, f32[256,256]{1,0:T(8,128)S(1)}, u32[]{:S(2)}, u32[]{:S(2)}) collective-permute-start(f32[256,256]{1,0:T(8,128)S(1)} %shard_map.98), channel_id=1, source_target_pairs={{0,1},{1,0},{2,3},{3,2},{4,5},{5,4},{6,7},{7,6},{8,9},{9,8},{10,11... | collective-permute-start | bytes 786440 | tf_op jit(solution)/shard_map/ppermute | solution.py:198
  78.0 0.0 copy-done.10
  78.0 0.1 broadcast_add_fusion
  78.0 0.1 add.34
  78.1 0.1 dynamic_slice.7
  78.2 0.0 copy-done
  78.2 0.0 copy-start.5
  78.2 0.0 copy-start.11
  78.2 5.8 %shard_map.97 = f32[256,256]{1,0:T(8,128)S(1)} custom-call(bf16[16,768,256]{2,1,0:T(8,128)(2,1)} %all-gather.2.cloned.1.call-done.gathered, bf16[256,4096]{1,0:T(8,128)(2,1)} %compare_select_fusion.hole, bf16[256,512]{1,0:T(8,128)(2,1)} %copy-done.4, bf16[256,512]{1,0:T(8,128)(2,1)} %copy-done.6, bf16[256,512]{1,0:T(8,128)(2,1)} %copy-done.7, ...), custom_call_target="tpu_custom_call" | custom-call | flops 1073741824 | bytes 8388608 | tf_op jit(solution)/shard_map/pallas_call | solution.py:157
  84.1 0.3 collective-permute-done.10
  84.4 0.0 copy-done.5
  84.4 0.0 copy-done.11
  84.4 0.8 subtract_convert_fusion
  (3 shorter events, 0.0 us)
Async XLA Ops:
  7.2 46.7 %copy-start.9 = (s32[4096]{0:T(1024)S(1)}, s32[4096]{0:T(1024)}, u32[]{:S(2)}) copy-start(s32[4096]{0:T(1024)} %param.11) | copy-start | bytes 49156
  7.2 55.7 %copy-start.1 = (bf16[256,4096]{1,0:T(8,128)(2,1)S(1)}, bf16[256,4096]{1,0:T(8,128)(2,1)}, u32[]{:S(2)}) copy-start(bf16[256,4096]{1,0:T(8,128)(2,1)} %param.13) | copy-start | bytes 6291460
  7.2 64.5 %all-gather.2.cloned.1.call-start = ((), (), s32[]{:S(2)}) async-start(), calls=%async_computation | async-start | bytes 6684672 | tf_op jit(solution)/shard_map/all_gather | solution.py:177
  9.1 6.5 %collective-permute-start = (bf16[256,256]{1,0:T(8,128)(2,1)}, bf16[256,256]{1,0:T(8,128)(2,1)S(1)}, u32[]{:S(2)}, u32[]{:S(2)}) collective-permute-start(bf16[256,256]{1,0:T(8,128)(2,1)} %shard_map.96), channel_id=1, source_target_pairs={{0,1},{1,0},{2,3},{3,2},{4,5},{5,4},{6,7},{7,6},{8,9},{9,8},{10,11... | collective-permute-start | bytes 393224 | tf_op jit(solution)/shard_map/ppermute | solution.py:174
  16.3 7.7 %collective-permute-start.1 = (bf16[256,256]{1,0:T(8,128)(2,1)}, bf16[256,256]{1,0:T(8,128)(2,1)S(1)}, u32[]{:S(2)}, u32[]{:S(2)}) collective-permute-start(bf16[256,256]{1,0:T(8,128)(2,1)} %amps.1), channel_id=1, source_target_pairs={{0,3},{1,2},{2,1},{3,0},{4,7},{5,6},{6,5},{7,4},{8,11},{9,10},{10,... | collective-permute-start | bytes 393224 | tf_op jit(solution)/shard_map/ppermute | solution.py:179
  24.0 40.8 %copy-start.4 = (bf16[256,512]{1,0:T(8,128)(2,1)}, bf16[256,512]{1,0:T(8,128)(2,1)S(1)}, u32[]{:S(2)}) copy-start(bf16[256,512]{1,0:T(8,128)(2,1)S(1)} %constant_dynamic-update-slice_fusion.refs_0_) | copy-start | bytes 786436
  24.0 14.6 %collective-permute-start.2 = (bf16[256,512]{1,0:T(8,128)(2,1)S(1)}, bf16[256,512]{1,0:T(8,128)(2,1)S(1)}, u32[]{:S(2)}, u32[]{:S(2)}) collective-permute-start(bf16[256,512]{1,0:T(8,128)(2,1)S(1)} %constant_dynamic-update-slice_fusion.refs_0_), channel_id=1, source_target_pairs={{0,4},{4,8},{8,12},{12,16},{16,20},{20,24},{24,28},{28,0},{1,5},{5... | collective-permute-start | bytes 786440 | tf_op jit(solution)/shard_map/ppermute | solution.py:184
  28.2 12.3 %collective-permute-start.3 = (bf16[256,512]{1,0:T(8,128)(2,1)S(1)}, bf16[256,512]{1,0:T(8,128)(2,1)S(1)}, u32[]{:S(2)}, u32[]{:S(2)}) collective-permute-start(bf16[256,512]{1,0:T(8,128)(2,1)S(1)} %constant_dynamic-update-slice_fusion.refs_0_), channel_id=1, source_target_pairs={{0,28},{4,0},{8,4},{12,8},{16,12},{20,16},{24,20},{28,24},{1,29},{... | collective-permute-start | bytes 786440 | tf_op jit(solution)/shard_map/ppermute | solution.py:185
  38.7 26.2 %copy-start.6 = (bf16[256,512]{1,0:T(8,128)(2,1)}, bf16[256,512]{1,0:T(8,128)(2,1)S(1)}, u32[]{:S(2)}) copy-start(bf16[256,512]{1,0:T(8,128)(2,1)S(1)} %collective-permute-done.2.refs_1_) | copy-start | bytes 786436
  38.7 8.7 %collective-permute-start.4 = (bf16[256,512]{1,0:T(8,128)(2,1)S(1)}, bf16[256,512]{1,0:T(8,128)(2,1)}, u32[]{:S(2)}, u32[]{:S(2)}) collective-permute-start(bf16[256,512]{1,0:T(8,128)(2,1)S(1)} %collective-permute-done.2.refs_1_), channel_id=1, source_target_pairs={{0,4},{4,8},{8,12},{12,16},{16,20},{20,24},{24,28},{28,0},{1,5},{5... | collective-permute-start | bytes 786440 | tf_op jit(solution)/shard_map/ppermute | solution.py:184
  40.6 24.2 %copy-start.7 = (bf16[256,512]{1,0:T(8,128)(2,1)}, bf16[256,512]{1,0:T(8,128)(2,1)S(1)}, u32[]{:S(2)}) copy-start(bf16[256,512]{1,0:T(8,128)(2,1)S(1)} %collective-permute-done.3.refs_2_) | copy-start | bytes 786436
  40.6 8.7 %collective-permute-start.5 = (bf16[256,512]{1,0:T(8,128)(2,1)S(1)}, bf16[256,512]{1,0:T(8,128)(2,1)}, u32[]{:S(2)}, u32[]{:S(2)}) collective-permute-start(bf16[256,512]{1,0:T(8,128)(2,1)S(1)} %collective-permute-done.3.refs_2_), channel_id=1, source_target_pairs={{0,28},{4,0},{8,4},{12,8},{16,12},{20,16},{24,20},{28,24},{1,29},{... | collective-permute-start | bytes 786440 | tf_op jit(solution)/shard_map/ppermute | solution.py:185
  47.4 8.9 %collective-permute-start.6 = (bf16[256,512]{1,0:T(8,128)(2,1)}, bf16[256,512]{1,0:T(8,128)(2,1)S(1)}, u32[]{:S(2)}, u32[]{:S(2)}) collective-permute-start(bf16[256,512]{1,0:T(8,128)(2,1)} %collective-permute-done.4.refs_3_), channel_id=1, source_target_pairs={{0,4},{4,8},{8,12},{12,16},{16,20},{20,24},{24,28},{28,0},{1,5},{5... | collective-permute-start | bytes 786440 | tf_op jit(solution)/shard_map/ppermute | solution.py:184
  49.3 8.9 %collective-permute-start.7 = (bf16[256,512]{1,0:T(8,128)(2,1)}, bf16[256,512]{1,0:T(8,128)(2,1)S(1)}, u32[]{:S(2)}, u32[]{:S(2)}) collective-permute-start(bf16[256,512]{1,0:T(8,128)(2,1)} %collective-permute-done.5.refs_4_), channel_id=1, source_target_pairs={{0,28},{4,0},{8,4},{12,8},{16,12},{20,16},{24,20},{28,24},{1,29},{... | collective-permute-start | bytes 786440 | tf_op jit(solution)/shard_map/ppermute | solution.py:185
  56.3 8.5 %copy-start.2 = (bf16[256,512]{1,0:T(8,128)(2,1)}, bf16[256,512]{1,0:T(8,128)(2,1)S(1)}, u32[]{:S(2)}) copy-start(bf16[256,512]{1,0:T(8,128)(2,1)S(1)} %collective-permute-done.6.refs_5_) | copy-start | bytes 786436
  56.3 8.5 %collective-permute-start.8 = (bf16[256,256]{1,0:T(8,128)(2,1)S(1)}, bf16[256,256]{1,0:T(8,128)(2,1)S(1)}, u32[]{:S(2)}, u32[]{:S(2)}) collective-permute-start(bf16[256,256]{1,0:T(8,128)(2,1)S(1)} %slice.8), channel_id=1, source_target_pairs={{0,4},{4,8},{8,12},{12,16},{16,20},{20,24},{24,28},{28,0},{1,5},{5... | collective-permute-start | bytes 393224 | tf_op jit(solution)/shard_map/ppermute | solution.py:187
  58.3 6.6 %copy-start.3 = (bf16[256,512]{1,0:T(8,128)(2,1)}, bf16[256,512]{1,0:T(8,128)(2,1)S(1)}, u32[]{:S(2)}) copy-start(bf16[256,512]{1,0:T(8,128)(2,1)S(1)} %collective-permute-done.7.refs_6_) | copy-start | bytes 786436
  58.3 6.6 %collective-permute-start.9 = (bf16[256,256]{1,0:T(8,128)(2,1)S(1)}, bf16[256,256]{1,0:T(8,128)(2,1)}, u32[]{:S(2)}, u32[]{:S(2)}) collective-permute-start(bf16[256,256]{1,0:T(8,128)(2,1)S(1)} %slice.9), channel_id=1, source_target_pairs={{0,28},{4,0},{8,4},{12,8},{16,12},{20,16},{24,20},{28,24},{1,29},{... | collective-permute-start | bytes 393224 | tf_op jit(solution)/shard_map/ppermute | solution.py:188
  64.8 13.1 %copy-start.10 = (f32[64]{0:T(128)S(1)}, f32[64]{0:T(128)}, u32[]{:S(2)}) copy-start(f32[64]{0:T(128)} %param.14) | copy-start | bytes 772
  64.9 13.3 %copy-start = (f32[256,256]{1,0:T(8,128)S(1)}, f32[256,256]{1,0:T(8,128)}, u32[]{:S(2)}) copy-start(f32[256,256]{1,0:T(8,128)} %refs_9_.1) | copy-start | bytes 786436
  64.9 6.8 %copy-start.8 = (bf16[256,256]{1,0:T(8,128)(2,1)}, bf16[256,256]{1,0:T(8,128)(2,1)S(1)}, u32[]{:S(2)}) copy-start(bf16[256,256]{1,0:T(8,128)(2,1)S(1)} %collective-permute-done.8.refs_7_) | copy-start | bytes 393220
  74.9 9.5 %collective-permute-start.10 = (f32[256,256]{1,0:T(8,128)S(1)}, f32[256,256]{1,0:T(8,128)S(1)}, u32[]{:S(2)}, u32[]{:S(2)}) collective-permute-start(f32[256,256]{1,0:T(8,128)S(1)} %shard_map.98), channel_id=1, source_target_pairs={{0,1},{1,0},{2,3},{3,2},{4,5},{5,4},{6,7},{7,6},{8,9},{9,8},{10,11... | collective-permute-start | bytes 786440 | tf_op jit(solution)/shard_map/ppermute | solution.py:198
  78.2 6.2 %copy-start.5 = (bf16[256,256]{1,0:T(8,128)(2,1)S(1)}, bf16[256,256]{1,0:T(8,128)(2,1)}, u32[]{:S(2)}) copy-start(bf16[256,256]{1,0:T(8,128)(2,1)} %amps.1) | copy-start | bytes 393220
  78.2 6.2 %copy-start.11 = (f32[256]{0:T(256)S(1)}, f32[256]{0:T(256)}, u32[]{:S(2)}) copy-start(f32[256]{0:T(256)} %param.15) | copy-start | bytes 3076
Sparse Core Ops, SparseCore 0:
  16.4 55.2 all-gather.1

commit v4 on v3

--- a/solution.py
+++ b/solution.py
@@ -8,6 +8,8 @@
 NY, NCORE, NZ, NX = 8, 2, 8, 4
 BF16, F32 = jnp.bfloat16, jnp.float32
 LANES = 128
+FIXED_BITS = 14
+EXPONENT_ROWS = 16
 
 
 def shift(n, by):
@@ -69,15 +71,15 @@
     )(*args)
 
 
-def ladder_copies(gathered, first_row, parts, parts_v, part_sems, rows_v, row_sems, size):
+def ladder_copies(gathered, first_row, parts, rows_v, row_sems, size):
     z, x = lax.axis_index("z"), lax.axis_index("x")
     upper = (x >= NX // 2).astype(jnp.int32)
     opposite = lax.rem(z + NZ // 2, NZ)
     sources = [(lax.rem(z + NZ + away, NZ), (0, 1)) for away in (0, -1, 1, -2, 2, -3, 3)]
     sources += [(opposite, (0,)), (opposite, (1,))]
     copies, at = [], 0
-    for i, (slot, blocks) in enumerate(sources):
-        mine = [pltpu.make_async_copy(parts[i], parts_v[i], part_sems.at[i])]
+    for slot, blocks in sources:
+        mine = []
         for j in blocks:
             r = 2 * slot + (upper if j == 0 else 1 - upper)
             src = gathered.at[r, pl.ds(first_row, size)]
@@ -88,31 +90,37 @@
     return copies
 
 
-def add_ladder(copies, parts_v, rows_v, acc, size):
+def add_ladder(copies, parts, rows_v, acc, size):
     at = 0
-    for i, mine in enumerate(copies):
+    for part, mine in zip(parts, copies):
         for copy in mine:
             copy.wait()
-        depth = size * (len(mine) - 1)
-        acc[...] += jnp.dot(parts_v[i][...], rows_v[at : at + depth, :], preferred_element_type=F32)
+        depth = size * len(mine)
+        acc[...] += jnp.dot(part[...], rows_v[at : at + depth, :], preferred_element_type=F32)
         at += depth
 
 
 def partner_kernel(gathered, *refs):
-    parts, out_ref = refs[:9], refs[9]
-    rows_v, parts_v, row_sems, part_sems = refs[10:]
-    size = out_ref.shape[0]
-    copies = ladder_copies(gathered, 2 * size, parts, parts_v, part_sems, rows_v, row_sems, size)
+    parts, out_ref, rows_v, acc, row_sems = refs[:9], *refs[9:]
+    size = acc.shape[0]
+    copies = ladder_copies(gathered, 2 * size, parts, rows_v, row_sems, size)
     for mine in copies:
         for copy in mine:
             copy.start()
-    out_ref[...] = jnp.zeros_like(out_ref)
-    add_ladder(copies, parts_v, rows_v, out_ref, size)
+    acc[...] = jnp.zeros_like(acc)
+    add_ladder(copies, parts, rows_v, acc, size)
+    largest = jnp.max(jnp.abs(acc[...]), axis=0, keepdims=True)
+    exponent = jnp.ceil(jnp.log2(jnp.maximum(largest, 2.0**-100)))
+    fixed = jnp.round(acc[...] * jnp.exp2(FIXED_BITS - exponent))
+    out_ref[:size, :] = fixed.astype(jnp.int32).astype(jnp.int16)
+    rows = out_ref.shape[0] - size
+    line = jnp.broadcast_to(exponent, (rows, exponent.shape[1]))
+    out_ref[size:, :] = line.astype(jnp.int32).astype(jnp.int16)
 
 
 def own_kernel(gathered, hole, *refs):
     parts, drive, out_ref = refs[:9], refs[9], refs[10]
-    rows_v, amps_rows_v, hole_v, parts_v, row_sems, amps_sems, hole_sems, part_sems = refs[11:]
+    rows_v, amps_rows_v, hole_v, row_sems, amps_sems, hole_sems = refs[11:]
     n, size = gathered.shape[0], out_ref.shape[0]
     group = n // len(hole_v)
     hole_copies = []
@@ -124,17 +132,17 @@
             dst = amps_rows_v.at[pl.ds(r * size, size)]
             mine.append(pltpu.make_async_copy(src, dst, amps_sems.at[r]))
         hole_copies.append(mine)
-    copies = ladder_copies(gathered, 0, parts, parts_v, part_sems, rows_v, row_sems, size)
-    for mine in hole_copies + copies:
+    copies = ladder_copies(gathered, 0, parts, rows_v, row_sems, size)
+    for mine in copies + hole_copies:
         for copy in mine:
             copy.start()
     out_ref[...] = drive[...]
+    add_ladder(copies, parts, rows_v, out_ref, size)
     for g, mine in enumerate(hole_copies):
         for copy in mine:
             copy.wait()
         at = pl.ds(g * group * size, group * size)
         out_ref[...] += jnp.dot(hole_v[g][...], amps_rows_v[at], preferred_element_type=F32)
-    add_ladder(copies, parts_v, rows_v, out_ref, size)
 
 
 def products(kernel, gathered, hole, parts, drive):
@@ -143,28 +151,31 @@
     n, _, cols = gathered.shape
     size, groups = drive.shape[0], 4
     with_hole = hole is not None
-    arrays = (gathered, hole, *parts) if with_hole else (gathered, *parts)
+    arrays = (gathered, hole) if with_hole else (gathered,)
     in_hbm = [pltpu.with_memory_space_constraint(a, pltpu.HBM) for a in arrays]
+    in_vmem = (*parts, drive) if with_hole else parts
+    out = jax.ShapeDtypeStruct(drive.shape, F32)
     scratch = [pltpu.VMEM((n * size, cols), BF16)]
+    if not with_hole:
+        out = jax.ShapeDtypeStruct((size + EXPONENT_ROWS, cols), jnp.int16)
+        scratch.append(pltpu.VMEM(drive.shape, F32))
     sems = [pltpu.SemaphoreType.DMA((n,))]
     if with_hole:
         scratch.append(pltpu.VMEM((n * size, cols), BF16))
         scratch.append([pltpu.VMEM((size, n * size // groups), BF16) for _ in range(groups)])
         sems += [pltpu.SemaphoreType.DMA((n,)), pltpu.SemaphoreType.DMA((groups,))]
-    scratch.append([pltpu.VMEM(p.shape, BF16) for p in parts])
-    sems.append(pltpu.SemaphoreType.DMA((len(parts),)))
     depth = (2 if with_hole else 1) * n * size
     return pl.pallas_call(
         kernel,
-        out_shape=jax.ShapeDtypeStruct(drive.shape, F32),
-        in_specs=[hbm] * len(in_hbm) + ([vmem] if with_hole else []),
+        out_shape=out,
+        in_specs=[hbm] * len(in_hbm) + [vmem] * len(in_vmem),
         out_specs=vmem,
         scratch_shapes=scratch + sems,
-        compiler_params=pltpu.CompilerParams(vmem_limit_bytes=32 << 20),
+        compiler_params=pltpu.CompilerParams(vmem_limit_bytes=24 << 20),
         cost_estimate=pl.CostEstimate(
             flops=2 * size * cols * depth, bytes_accessed=4 * size * depth, transcendentals=0
         ),
-    )(*in_hbm, *([drive] if with_hole else []))
+    )(*in_hbm, *in_vmem)
 
 
 def body(amplitudes, drive, pair_irrep, occ_irrep, ladder_ints, hole_ints, occ_energy, pair_energy):
@@ -196,7 +207,9 @@
     denominator = pair_energy[None, :] - own_energy[:, None]
     for_partner = products(partner_kernel, gathered, None, parts, drive)
     from_partner = lax.ppermute(for_partner, "x", partner)
-    residual = products(own_kernel, gathered, hole_kept, parts, drive) + from_partner
+    scale = jnp.exp2(from_partner[size : size + 1].astype(F32) - FIXED_BITS)
+    residual = products(own_kernel, gathered, hole_kept, parts, drive)
+    residual = residual + from_partner[:size].astype(F32) * scale
     updated = (amplitudes.astype(F32) - residual / denominator).astype(BF16)
     return residual, updated
 

time: 92.5 us -> 90.5 us (0.978)
  Pallas kernels: 12.8 us -> 11 us
  waiting for transfers between devices: 15.7 us -> 13.9 us
  other arithmetic: 2.8 us -> 4.43 us
    pallas_call x2, Pallas kernels: 9.01 us -> 7.4 us  [products(): pl.pallas_call(kernel, out_shape=out, in_specs=[hbm] * len(in_hbm) + [vme...]
    select_n x1, other arithmetic: 1.94 us -> 3.54 us  [body(): jnp.where(own_occ[:, None] == occ_irrep[None, :], hole_ints, jnp.zeros_li...]
    all_gather x1, waiting for transfers between devices: 6.78 us -> 5.5 us  [body(): gathered = lax.all_gather(rows, ('y', 'core'), axis=0, tiled=False)]
  transfers between devices with their start and end apart: 12 -> 12, of which waited for: 7 -> 6; matrix products, arithmetic and copies ran while one was open for 3% -> 5% of each run, Pallas kernels for 8% -> 7%
where the time goes in v4:
time: 90.5 us; the launch traced here: 90 us
  starting transfers between devices  44.5 us (49%)
  between operations  14.2 us (16%)
  waiting for transfers between devices  13.9 us (15%)
  Pallas kernels  11 us (12%)
  other arithmetic  4.43 us (5%)
  local copies, waits for them, and re-layouts  1.85 us (2%)
    ppermute x3, starting transfers between devices, body(): b = lax.ppermute(b, 'z', shift(NZ, -1))  17.7 us
    ppermute x3, starting transfers between devices, body(): f = lax.ppermute(f, 'z', shift(NZ, 1))  8 us
    pallas_call x2, Pallas kernels, products(): pl.pallas_call(kernel, out_shape=out, in_specs=[hbm] * len(in_hbm) + [vme...  7.4 us
    ppermute x3, waiting for transfers between devices, body(): f = lax.ppermute(f, 'z', shift(NZ, 1))  6.14 us
    all_gather x1, waiting for transfers between devices, body(): gathered = lax.all_gather(rows, ('y', 'core'), axis=0, tiled=False)  5.5 us
    ppermute x1, starting transfers between devices, body(): other = lax.ppermute(amplitudes, 'x', [(i, NX - 1 - i) for i in range(NX)])  5.18 us
    ppermute x1, starting transfers between devices, body(): parts.append(lax.ppermute(b[:, size:], 'z', shift(NZ, -1)))  4.57 us
    ppermute x1, starting transfers between devices, body(): lax.ppermute(prepare(send_kernel, size, labels, ladder_ints), 'x', partner)  3.94 us
  transfers between devices with their start and end apart: 12, of which 6 were waited for; matrix products, arithmetic and copies ran while one was open for 5% of the time, Pallas kernels for 7%

profile of v4, /device:TPU:1, one launch (start us, length us, event | category | flops | bytes accessed | tf_op | source)
XLA Modules:
  0.0 90.0 jit_solution(3454969696767537199)
XLA Ops:
  7.2 0.0 copy-start.2
  7.2 0.0 all-gather.2.cloned.1.call-start
  7.2 1.7 %shard_map.96 = bf16[256,256]{1,0:T(8,128)(2,1)} custom-call(s32[64,128]{1,0:T(8,128)} %bitcast.6, bf16[512,256]{1,0:T(8,128)(2,1)} %ladder.3), custom_call_target="tpu_custom_call" | custom-call | bytes 1048576 | tf_op jit(solution)/shard_map/pallas_call | solution.py:65
  9.0 3.9 %collective-permute-start = (bf16[256,256]{1,0:T(8,128)(2,1)}, bf16[256,256]{1,0:T(8,128)(2,1)S(1)}, u32[]{:S(2)}, u32[]{:S(2)}) collective-permute-start(bf16[256,256]{1,0:T(8,128)(2,1)} %shard_map.96), channel_id=1, source_target_pairs={{0,1},{1,0},{2,3},{3,2},{4,5},{5,4},{6,7},{7,6},{8,9},{9,8},{10,11... | collective-permute-start | bytes 393224 | tf_op jit(solution)/shard_map/ppermute | solution.py:185
  12.9 1.9 %shard_map.95 = bf16[768,256]{1,0:T(8,128)(2,1)} custom-call(s32[64,128]{1,0:T(8,128)} %bitcast.7, bf16[512,256]{1,0:T(8,128)(2,1)} %ladder.3, bf16[256,256]{1,0:T(8,128)(2,1)} %amps.1), custom_call_target="tpu_custom_call" | custom-call | bytes 1048576 | tf_op jit(solution)/shard_map/pallas_call | solution.py:65
  14.8 0.6 collective-permute-done
  15.4 0.7 bitcast_dynamic-update-slice_fusion
  16.1 0.0 all-gather.2.cloned.1.call-update
  16.1 5.2 %collective-permute-start.1 = (bf16[256,256]{1,0:T(8,128)(2,1)}, bf16[256,256]{1,0:T(8,128)(2,1)S(1)}, u32[]{:S(2)}, u32[]{:S(2)}) collective-permute-start(bf16[256,256]{1,0:T(8,128)(2,1)} %amps.1), channel_id=1, source_target_pairs={{0,3},{1,2},{2,1},{3,0},{4,7},{5,6},{6,5},{7,4},{8,11},{9,10},{10,... | collective-permute-start | bytes 393224 | tf_op jit(solution)/shard_map/ppermute | solution.py:190
  21.3 0.9 %constant_dynamic-update-slice_fusion.1 = bf16[256,512]{1,0:T(8,128)(2,1)S(1)} fusion(bf16[256,256]{1,0:T(8,128)(2,1)} %amps.1), kind=kLoop, calls=%fused_computation.6 | loop fusion | bytes 262144
  22.2 1.6 %collective-permute-done.1 = bf16[256,256]{1,0:T(8,128)(2,1)S(1)} collective-permute-done((bf16[256,256]{1,0:T(8,128)(2,1)}, bf16[256,256]{1,0:T(8,128)(2,1)S(1)}, u32[]{:S(2)}, u32[]{:S(2)}) %collective-permute-start.1) | collective-permute-done | bytes 131104 | tf_op jit(solution)/shard_map/ppermute | solution.py:190
  23.9 4.2 %collective-permute-start.2 = (bf16[256,512]{1,0:T(8,128)(2,1)S(1)}, bf16[256,512]{1,0:T(8,128)(2,1)S(1)}, u32[]{:S(2)}, u32[]{:S(2)}) collective-permute-start(bf16[256,512]{1,0:T(8,128)(2,1)S(1)} %constant_dynamic-update-slice_fusion.refs_0_), channel_id=1, source_target_pairs={{0,4},{4,8},{8,12},{12,16},{16,20},{20,24},{24,28},{28,0},{1,5},{5... | collective-permute-start | bytes 786440 | tf_op jit(solution)/shard_map/ppermute | solution.py:195
  28.1 8.6 %collective-permute-start.3 = (bf16[256,512]{1,0:T(8,128)(2,1)S(1)}, bf16[256,512]{1,0:T(8,128)(2,1)S(1)}, u32[]{:S(2)}, u32[]{:S(2)}) collective-permute-start(bf16[256,512]{1,0:T(8,128)(2,1)S(1)} %constant_dynamic-update-slice_fusion.refs_0_), channel_id=1, source_target_pairs={{0,28},{4,0},{8,4},{12,8},{16,12},{20,16},{24,20},{28,24},{1,29},{... | collective-permute-start | bytes 786440 | tf_op jit(solution)/shard_map/ppermute | solution.py:196
  36.7 1.8 %collective-permute-done.2.refs_1_ = bf16[256,512]{1,0:T(8,128)(2,1)S(1)} collective-permute-done((bf16[256,512]{1,0:T(8,128)(2,1)S(1)}, bf16[256,512]{1,0:T(8,128)(2,1)S(1)}, u32[]{:S(2)}, u32[]{:S(2)}) %collective-permute-start.2) | collective-permute-done | bytes 262176 | tf_op jit(solution)/shard_map/ppermute | solution.py:195
  38.5 1.9 %collective-permute-start.4 = (bf16[256,512]{1,0:T(8,128)(2,1)S(1)}, bf16[256,512]{1,0:T(8,128)(2,1)S(1)}, u32[]{:S(2)}, u32[]{:S(2)}) collective-permute-start(bf16[256,512]{1,0:T(8,128)(2,1)S(1)} %collective-permute-done.2.refs_1_), channel_id=1, source_target_pairs={{0,4},{4,8},{8,12},{12,16},{16,20},{20,24},{24,28},{28,0},{1,5},{5... | collective-permute-start | bytes 786440 | tf_op jit(solution)/shard_map/ppermute | solution.py:195
  40.4 0.0 collective-permute-done.3.refs_2_
  40.4 4.6 %collective-permute-start.5 = (bf16[256,512]{1,0:T(8,128)(2,1)S(1)}, bf16[256,512]{1,0:T(8,128)(2,1)S(1)}, u32[]{:S(2)}, u32[]{:S(2)}) collective-permute-start(bf16[256,512]{1,0:T(8,128)(2,1)S(1)} %collective-permute-done.3.refs_2_), channel_id=1, source_target_pairs={{0,28},{4,0},{8,4},{12,8},{16,12},{20,16},{24,20},{28,24},{1,29},{... | collective-permute-start | bytes 786440 | tf_op jit(solution)/shard_map/ppermute | solution.py:196
  45.0 2.2 %collective-permute-done.4.refs_3_ = bf16[256,512]{1,0:T(8,128)(2,1)S(1)} collective-permute-done((bf16[256,512]{1,0:T(8,128)(2,1)S(1)}, bf16[256,512]{1,0:T(8,128)(2,1)S(1)}, u32[]{:S(2)}, u32[]{:S(2)}) %collective-permute-start.4) | collective-permute-done | bytes 262176 | tf_op jit(solution)/shard_map/ppermute | solution.py:195
  47.2 1.9 %collective-permute-start.6 = (bf16[256,512]{1,0:T(8,128)(2,1)S(1)}, bf16[256,512]{1,0:T(8,128)(2,1)S(1)}, u32[]{:S(2)}, u32[]{:S(2)}) collective-permute-start(bf16[256,512]{1,0:T(8,128)(2,1)S(1)} %collective-permute-done.4.refs_3_), channel_id=1, source_target_pairs={{0,4},{4,8},{8,12},{12,16},{16,20},{20,24},{24,28},{28,0},{1,5},{5... | collective-permute-start | bytes 786440 | tf_op jit(solution)/shard_map/ppermute | solution.py:195
  49.1 0.0 collective-permute-done.5.refs_4_
  49.1 4.6 %collective-permute-start.7 = (bf16[256,512]{1,0:T(8,128)(2,1)S(1)}, bf16[256,512]{1,0:T(8,128)(2,1)S(1)}, u32[]{:S(2)}, u32[]{:S(2)}) collective-permute-start(bf16[256,512]{1,0:T(8,128)(2,1)S(1)} %collective-permute-done.5.refs_4_), channel_id=1, source_target_pairs={{0,28},{4,0},{8,4},{12,8},{16,12},{20,16},{24,20},{28,24},{1,29},{... | collective-permute-start | bytes 786440 | tf_op jit(solution)/shard_map/ppermute | solution.py:196
  53.7 0.0 copy-done.2
  53.7 0.1 dynamic_slice.6
  53.8 2.1 %collective-permute-done.6.refs_5_ = bf16[256,512]{1,0:T(8,128)(2,1)S(1)} collective-permute-done((bf16[256,512]{1,0:T(8,128)(2,1)S(1)}, bf16[256,512]{1,0:T(8,128)(2,1)S(1)}, u32[]{:S(2)}, u32[]{:S(2)}) %collective-permute-start.6) | collective-permute-done | bytes 262176 | tf_op jit(solution)/shard_map/ppermute | solution.py:195
  55.9 1.9 %collective-permute-start.8 = (bf16[256,256]{1,0:T(8,128)(2,1)S(1)}, bf16[256,256]{1,0:T(8,128)(2,1)S(1)}, u32[]{:S(2)}, u32[]{:S(2)}) collective-permute-start(bf16[256,256]{1,0:T(8,128)(2,1)S(1)} %slice.16), channel_id=1, source_target_pairs={{0,4},{4,8},{8,12},{12,16},{16,20},{20,24},{24,28},{28,0},{1,5},{5... | collective-permute-start | bytes 393224 | tf_op jit(solution)/shard_map/ppermute | solution.py:198
  57.9 0.0 collective-permute-done.7.refs_6_
  57.9 4.6 %collective-permute-start.9 = (bf16[256,256]{1,0:T(8,128)(2,1)S(1)}, bf16[256,256]{1,0:T(8,128)(2,1)S(1)}, u32[]{:S(2)}, u32[]{:S(2)}) collective-permute-start(bf16[256,256]{1,0:T(8,128)(2,1)S(1)} %slice.17), channel_id=1, source_target_pairs={{0,28},{4,0},{8,4},{12,8},{16,12},{20,16},{24,20},{28,24},{1,29},{... | collective-permute-start | bytes 393224 | tf_op jit(solution)/shard_map/ppermute | solution.py:199
  62.5 3.5 %compare_select_fusion.hole = bf16[256,4096]{1,0:T(8,128)(2,1)} fusion(bf16[256,4096]{1,0:T(8,128)(2,1)} %param.13, s32[4096]{0:T(1024)S(1)} %copy-done.2, s32[256]{0:T(256)S(1)} %dynamic_slice.6), kind=kLoop, calls=%fused_computation | loop fusion | flops 2097152 | bytes 4211712 | tf_op jit(solution)/shard_map/jit(_where)/select_n | solution.py:202
  66.0 0.0 copy-start.3
  66.0 0.0 copy-start
  66.0 0.0 collective-permute-done.8.refs_7_
  66.0 0.0 collective-permute-done.9.refs_8_
  66.0 5.5 %all-gather.2.cloned.1.call-done.gathered = bf16[16,768,256]{2,1,0:T(8,128)(2,1)} async-done(((bf16[1,768,256]{2,1,0:T(8,128)(2,1)}), bf16[16,768,256]{2,1,0:T(8,128)(2,1)}) %all-gather.2.cloned.1.call-update) | async-done | bytes 6291472 | tf_op jit(solution)/shard_map/all_gather | solution.py:188
  71.5 2.8 %shard_map.98 = s16[272,256]{1,0:T(8,128)(2,1)S(1)} custom-call(bf16[16,768,256]{2,1,0:T(8,128)(2,1)} %all-gather.2.cloned.1.call-done.gathered, bf16[256,512]{1,0:T(8,128)(2,1)S(1)} %constant_dynamic-update-slice_fusion.refs_0_, bf16[256,512]{1,0:T(8,128)(2,1)S(1)} %collective-permute-done.2.refs_1_, bf16[256,512]{1,0:T(8,128)(2,1)S(1)} %collective-permute-done.3.refs_2_, ...), custom_call_target="tpu_custom_call" | custom-call | flops 536870912 | bytes 4194304 | tf_op jit(solution)/shard_map/pallas_call | solution.py:168
  74.3 3.1 %collective-permute-start.10 = (s16[272,256]{1,0:T(8,128)(2,1)S(1)}, s16[272,256]{1,0:T(8,128)(2,1)S(1)}, u32[]{:S(2)}, u32[]{:S(2)}) collective-permute-start(s16[272,256]{1,0:T(8,128)(2,1)S(1)} %shard_map.98), channel_id=1, source_target_pairs={{0,1},{1,0},{2,3},{3,2},{4,5},{5,4},{6,7},{7,6},{8,9},{9,8},{10,11... | collective-permute-start | bytes 417800 | tf_op jit(solution)/shard_map/ppermute | solution.py:209
  77.4 0.0 copy-done.3
  77.4 0.1 broadcast_add_fusion
  77.5 0.1 add.35
  77.6 0.1 dynamic_slice.7
  77.6 0.0 copy-done
  77.7 0.0 copy-start.1
  77.7 0.0 copy-start.4
  77.7 4.6 %shard_map.97 = f32[256,256]{1,0:T(8,128)S(1)} custom-call(bf16[16,768,256]{2,1,0:T(8,128)(2,1)} %all-gather.2.cloned.1.call-done.gathered, bf16[256,4096]{1,0:T(8,128)(2,1)} %compare_select_fusion.hole, bf16[256,512]{1,0:T(8,128)(2,1)S(1)} %constant_dynamic-update-slice_fusion.refs_0_, bf16[256,512]{1,0:T(8,128)(2,1)S(1)} %collective-permute-done.2.refs_1_, ...), custom_call_target="tpu_custom_call" | custom-call | flops 1073741824 | bytes 8388608 | tf_op jit(solution)/shard_map/pallas_call | solution.py:168
  82.3 0.0 collective-permute-done.10
  82.3 0.0 copy-done.1
  82.3 0.0 copy-done.4
  82.3 0.8 subtract_convert_fusion
  (4 shorter events, 0.0 us)
Async XLA Ops:
  7.2 46.6 %copy-start.2 = (s32[4096]{0:T(1024)S(1)}, s32[4096]{0:T(1024)}, u32[]{:S(2)}) copy-start(s32[4096]{0:T(1024)} %param.11) | copy-start | bytes 49156
  7.2 64.3 %all-gather.2.cloned.1.call-start = ((), (), s32[]{:S(2)}) async-start(), calls=%async_computation | async-start | bytes 6684672 | tf_op jit(solution)/shard_map/all_gather | solution.py:188
  9.0 6.5 %collective-permute-start = (bf16[256,256]{1,0:T(8,128)(2,1)}, bf16[256,256]{1,0:T(8,128)(2,1)S(1)}, u32[]{:S(2)}, u32[]{:S(2)}) collective-permute-start(bf16[256,256]{1,0:T(8,128)(2,1)} %shard_map.96), channel_id=1, source_target_pairs={{0,1},{1,0},{2,3},{3,2},{4,5},{5,4},{6,7},{7,6},{8,9},{9,8},{10,11... | collective-permute-start | bytes 393224 | tf_op jit(solution)/shard_map/ppermute | solution.py:185
  16.1 7.7 %collective-permute-start.1 = (bf16[256,256]{1,0:T(8,128)(2,1)}, bf16[256,256]{1,0:T(8,128)(2,1)S(1)}, u32[]{:S(2)}, u32[]{:S(2)}) collective-permute-start(bf16[256,256]{1,0:T(8,128)(2,1)} %amps.1), channel_id=1, source_target_pairs={{0,3},{1,2},{2,1},{3,0},{4,7},{5,6},{6,5},{7,4},{8,11},{9,10},{10,... | collective-permute-start | bytes 393224 | tf_op jit(solution)/shard_map/ppermute | solution.py:190
  23.9 14.6 %collective-permute-start.2 = (bf16[256,512]{1,0:T(8,128)(2,1)S(1)}, bf16[256,512]{1,0:T(8,128)(2,1)S(1)}, u32[]{:S(2)}, u32[]{:S(2)}) collective-permute-start(bf16[256,512]{1,0:T(8,128)(2,1)S(1)} %constant_dynamic-update-slice_fusion.refs_0_), channel_id=1, source_target_pairs={{0,4},{4,8},{8,12},{12,16},{16,20},{20,24},{24,28},{28,0},{1,5},{5... | collective-permute-start | bytes 786440 | tf_op jit(solution)/shard_map/ppermute | solution.py:195
  28.1 12.3 %collective-permute-start.3 = (bf16[256,512]{1,0:T(8,128)(2,1)S(1)}, bf16[256,512]{1,0:T(8,128)(2,1)S(1)}, u32[]{:S(2)}, u32[]{:S(2)}) collective-permute-start(bf16[256,512]{1,0:T(8,128)(2,1)S(1)} %constant_dynamic-update-slice_fusion.refs_0_), channel_id=1, source_target_pairs={{0,28},{4,0},{8,4},{12,8},{16,12},{20,16},{24,20},{28,24},{1,29},{... | collective-permute-start | bytes 786440 | tf_op jit(solution)/shard_map/ppermute | solution.py:196
  38.5 8.7 %collective-permute-start.4 = (bf16[256,512]{1,0:T(8,128)(2,1)S(1)}, bf16[256,512]{1,0:T(8,128)(2,1)S(1)}, u32[]{:S(2)}, u32[]{:S(2)}) collective-permute-start(bf16[256,512]{1,0:T(8,128)(2,1)S(1)} %collective-permute-done.2.refs_1_), channel_id=1, source_target_pairs={{0,4},{4,8},{8,12},{12,16},{16,20},{20,24},{24,28},{28,0},{1,5},{5... | collective-permute-start | bytes 786440 | tf_op jit(solution)/shard_map/ppermute | solution.py:195
  40.4 8.7 %collective-permute-start.5 = (bf16[256,512]{1,0:T(8,128)(2,1)S(1)}, bf16[256,512]{1,0:T(8,128)(2,1)S(1)}, u32[]{:S(2)}, u32[]{:S(2)}) collective-permute-start(bf16[256,512]{1,0:T(8,128)(2,1)S(1)} %collective-permute-done.3.refs_2_), channel_id=1, source_target_pairs={{0,28},{4,0},{8,4},{12,8},{16,12},{20,16},{24,20},{28,24},{1,29},{... | collective-permute-start | bytes 786440 | tf_op jit(solution)/shard_map/ppermute | solution.py:196
  47.2 8.7 %collective-permute-start.6 = (bf16[256,512]{1,0:T(8,128)(2,1)S(1)}, bf16[256,512]{1,0:T(8,128)(2,1)S(1)}, u32[]{:S(2)}, u32[]{:S(2)}) collective-permute-start(bf16[256,512]{1,0:T(8,128)(2,1)S(1)} %collective-permute-done.4.refs_3_), channel_id=1, source_target_pairs={{0,4},{4,8},{8,12},{12,16},{16,20},{20,24},{24,28},{28,0},{1,5},{5... | collective-permute-start | bytes 786440 | tf_op jit(solution)/shard_map/ppermute | solution.py:195
  49.1 8.7 %collective-permute-start.7 = (bf16[256,512]{1,0:T(8,128)(2,1)S(1)}, bf16[256,512]{1,0:T(8,128)(2,1)S(1)}, u32[]{:S(2)}, u32[]{:S(2)}) collective-permute-start(bf16[256,512]{1,0:T(8,128)(2,1)S(1)} %collective-permute-done.5.refs_4_), channel_id=1, source_target_pairs={{0,28},{4,0},{8,4},{12,8},{16,12},{20,16},{24,20},{28,24},{1,29},{... | collective-permute-start | bytes 786440 | tf_op jit(solution)/shard_map/ppermute | solution.py:196
  55.9 10.1 %collective-permute-start.8 = (bf16[256,256]{1,0:T(8,128)(2,1)S(1)}, bf16[256,256]{1,0:T(8,128)(2,1)S(1)}, u32[]{:S(2)}, u32[]{:S(2)}) collective-permute-start(bf16[256,256]{1,0:T(8,128)(2,1)S(1)} %slice.16), channel_id=1, source_target_pairs={{0,4},{4,8},{8,12},{12,16},{16,20},{20,24},{24,28},{28,0},{1,5},{5... | collective-permute-start | bytes 393224 | tf_op jit(solution)/shard_map/ppermute | solution.py:198
  57.9 8.1 %collective-permute-start.9 = (bf16[256,256]{1,0:T(8,128)(2,1)S(1)}, bf16[256,256]{1,0:T(8,128)(2,1)S(1)}, u32[]{:S(2)}, u32[]{:S(2)}) collective-permute-start(bf16[256,256]{1,0:T(8,128)(2,1)S(1)} %slice.17), channel_id=1, source_target_pairs={{0,28},{4,0},{8,4},{12,8},{16,12},{20,16},{24,20},{28,24},{1,29},{... | collective-permute-start | bytes 393224 | tf_op jit(solution)/shard_map/ppermute | solution.py:199
  66.0 11.4 %copy-start.3 = (f32[64]{0:T(128)S(1)}, f32[64]{0:T(128)}, u32[]{:S(2)}) copy-start(f32[64]{0:T(128)} %param.14) | copy-start | bytes 772
  66.0 11.6 %copy-start = (f32[256,256]{1,0:T(8,128)S(1)}, f32[256,256]{1,0:T(8,128)}, u32[]{:S(2)}) copy-start(f32[256,256]{1,0:T(8,128)} %refs_9_.1) | copy-start | bytes 786436
  74.3 8.0 %collective-permute-start.10 = (s16[272,256]{1,0:T(8,128)(2,1)S(1)}, s16[272,256]{1,0:T(8,128)(2,1)S(1)}, u32[]{:S(2)}, u32[]{:S(2)}) collective-permute-start(s16[272,256]{1,0:T(8,128)(2,1)S(1)} %shard_map.98), channel_id=1, source_target_pairs={{0,1},{1,0},{2,3},{3,2},{4,5},{5,4},{6,7},{7,6},{8,9},{9,8},{10,11... | collective-permute-start | bytes 417800 | tf_op jit(solution)/shard_map/ppermute | solution.py:209
  77.7 4.7 %copy-start.1 = (bf16[256,256]{1,0:T(8,128)(2,1)S(1)}, bf16[256,256]{1,0:T(8,128)(2,1)}, u32[]{:S(2)}) copy-start(bf16[256,256]{1,0:T(8,128)(2,1)} %amps.1) | copy-start | bytes 393220
  77.7 4.7 %copy-start.4 = (f32[256]{0:T(256)S(1)}, f32[256]{0:T(256)}, u32[]{:S(2)}) copy-start(f32[256]{0:T(256)} %param.15) | copy-start | bytes 3076
Sparse Core Ops, SparseCore 0:
  16.2 55.2 all-gather.1

commit v5 on v4

--- a/solution.py
+++ b/solution.py
@@ -26,49 +26,41 @@
     return lax.rem(inner + lax.axis_index("core"), 2)
 
 
-def masked_block(labels, ladder, block, write):
-    r = row_rank()
+def masked(values, row_labels, col_labels):
+    return jnp.where(row_labels == col_labels, values.astype(F32), 0.0).astype(BF16)
+
+
+def down(line):
+    return jnp.broadcast_to(line.astype(F32), (LANES, LANES)).T
+
+
+def rows_kernel(labels, ladder, amps, out_ref):
+    size, cols = amps.shape
+    block = kept_block()
     c = lax.axis_index("z") * NX + lax.axis_index("x")
-    size = ladder.shape[0] // 2
-    lines, cols = size // LANES, ladder.shape[1] // LANES
-    col_labels = [labels[pl.ds(c * cols + q, 1), :].astype(F32) for q in range(cols)]
-    for k in range(lines):
-        line = labels[pl.ds((2 * r + block) * lines + k, 1), :].astype(F32)
-        row_labels = jnp.broadcast_to(line, (LANES, LANES)).T
+    lines = cols // LANES
+    first = (2 * row_rank() + block) * (size // LANES)
+    for k in range(size // LANES):
+        row_labels = down(labels[pl.ds(first + k, 1), :])
         at = pl.ds(pl.multiple_of(block * size + k * LANES, LANES), LANES)
-        for q in range(cols):
+        for q in range(lines):
             lanes = slice(q * LANES, (q + 1) * LANES)
-            values = ladder[at, lanes].astype(F32)
-            kept = jnp.where(row_labels == col_labels[q], values, 0.0)
-            write(slice(k * LANES, (k + 1) * LANES), lanes, kept.astype(BF16))
-
-
-def send_kernel(labels, ladder, out_ref):
-    def write(rows, lanes, values):
-        out_ref[rows, lanes] = values
-
-    masked_block(labels, ladder, 1 - kept_block(), write)
-
-
-def rows_kernel(labels, ladder, amps, out_ref):
-    def write(rows, lanes, values):
-        out_ref[rows, lanes] = values
-
-    masked_block(labels, ladder, kept_block(), write)
-    size = amps.shape[0]
+            col_labels = labels[pl.ds(c * lines + q, 1), :].astype(F32)
+            out_ref[k * LANES : (k + 1) * LANES, lanes] = masked(ladder[at, lanes], row_labels, col_labels)
     out_ref[size : 2 * size, :] = amps[...]
     out_ref[2 * size :, :] = jnp.zeros_like(amps)
 
 
-def prepare(kernel, rows, *args):
+def gather_rows(labels, ladder, amps):
     vmem = pl.BlockSpec(memory_space=pltpu.VMEM)
+    size, cols = amps.shape
     return pl.pallas_call(
-        kernel,
-        out_shape=jax.ShapeDtypeStruct((rows, args[1].shape[1]), BF16),
-        in_specs=[vmem] * len(args),
+        rows_kernel,
+        out_shape=jax.ShapeDtypeStruct((3 * size, cols), BF16),
+        in_specs=[vmem] * 3,
         out_specs=vmem,
         cost_estimate=pl.CostEstimate(flops=0, bytes_accessed=1 << 20, transcendentals=0),
-    )(*args)
+    )(labels, ladder, amps)
 
 
 def ladder_copies(gathered, first_row, parts, rows_v, row_sems, size):
@@ -182,8 +174,14 @@
     size = amplitudes.shape[0]
     labels = pair_irrep.reshape(-1, LANES)
     partner = [(i, i ^ 1) for i in range(NX)]
-    lent = lax.ppermute(prepare(send_kernel, size, labels, ladder_ints), "x", partner)
-    rows = prepare(rows_kernel, 3 * size, labels, ladder_ints, amplitudes)
+    kept = kept_block()
+    lent = lax.dynamic_slice_in_dim(ladder_ints, (1 - kept) * size, size)
+    lent = lax.ppermute(lent, "x", partner)
+    rows = gather_rows(labels, ladder_ints, amplitudes)
+    lent_rows = lax.dynamic_slice_in_dim(pair_irrep, (2 * row_rank() + kept) * size, size)
+    partner_rank = lax.axis_index("z") * NX + (lax.axis_index("x") ^ 1)
+    lent_cols = lax.dynamic_slice_in_dim(pair_irrep, partner_rank * size, size)
+    lent = jnp.where(lent_rows[:, None] == lent_cols[None, :], lent, jnp.zeros_like(lent))
     rows = lax.dynamic_update_slice(rows, lent, (2 * size, 0))
     gathered = lax.all_gather(rows, ("y", "core"), axis=0, tiled=False)
 

time: 90.5 us -> 89.6 us (0.990)
  Pallas kernels: 11 us -> 9.31 us
  local copies, waits for them, and re-layouts: 1.85 us -> 2.95 us
    dynamic_slice x0 -> x2, local copies, waits for them, and re-layouts: none -> 1.75 us  [the longest x1 0.92 us: body(): lent = lax.dynamic_slice_in_dim(ladder_ints, (1 - kept) * size, size)]
    pallas_call x2 -> x1, Pallas kernels: 3.64 us -> 1.91 us  [gather_rows(): pl.pallas_call(rows_kernel, out_shape=jax.ShapeDtypeStruct((3 * size, col...]
  transfers between devices with their start and end apart: 12 -> 12, of which waited for: 6 -> 5; matrix products, arithmetic and copies ran while one was open for 5% -> 6% of each run, Pallas kernels for 7% -> 7%
where the time goes in v5:
time: 89.6 us; the launch traced here: 89.1 us
  starting transfers between devices  44.1 us (49%)
  between operations  14.3 us (16%)
  waiting for transfers between devices  13.3 us (15%)
  Pallas kernels  9.31 us (10%)
  other arithmetic  5.19 us (6%)
  local copies, waits for them, and re-layouts  2.95 us (3%)
    ppermute x3, starting transfers between devices, body(): b = lax.ppermute(b, 'z', shift(NZ, -1))  17.7 us
    ppermute x3, starting transfers between devices, body(): f = lax.ppermute(f, 'z', shift(NZ, 1))  8 us
    pallas_call x2, Pallas kernels, products(): pl.pallas_call(kernel, out_shape=out, in_specs=[hbm] * len(in_hbm) + [vme...  7.4 us
    ppermute x3, waiting for transfers between devices, body(): f = lax.ppermute(f, 'z', shift(NZ, 1))  6.14 us
    all_gather x1, waiting for transfers between devices, body(): gathered = lax.all_gather(rows, ('y', 'core'), axis=0, tiled=False)  5.5 us
    ppermute x1, starting transfers between devices, body(): other = lax.ppermute(amplitudes, 'x', [(i, NX - 1 - i) for i in range(NX)])  4.74 us
    ppermute x1, starting transfers between devices, body(): parts.append(lax.ppermute(b[:, size:], 'z', shift(NZ, -1)))  4.57 us
    ppermute x1, starting transfers between devices, body(): lent = lax.ppermute(lent, 'x', partner)  3.95 us
  transfers between devices with their start and end apart: 12, of which 5 were waited for; matrix products, arithmetic and copies ran while one was open for 6% of the time, Pallas kernels for 7%

profile of v5, /device:TPU:1, one launch (start us, length us, event | category | flops | bytes accessed | tf_op | source)
XLA Modules:
  0.0 89.1 jit_solution(7587372980940172503)
XLA Ops:
  7.2 0.0 copy-start.2
  7.2 0.0 all-gather.2.cloned.1.call-start
  7.2 0.9 %constant_dynamic-slice_fusion = bf16[256,256]{1,0:T(8,128)(2,1)S(1)} fusion(bf16[512,256]{1,0:T(8,128)(2,1)} %ladder.1, s32[]{:T(128)S(6)} %select_n.23), kind=kLoop, calls=%fused_computation.13 | loop fusion | bytes 262148 | tf_op jit(solution)/shard_map/dynamic_slice | solution.py:178
  8.2 3.9 %collective-permute-start = (bf16[256,256]{1,0:T(8,128)(2,1)S(1)}, bf16[256,256]{1,0:T(8,128)(2,1)S(1)}, u32[]{:S(2)}, u32[]{:S(2)}) collective-permute-start(bf16[256,256]{1,0:T(8,128)(2,1)S(1)} %constant_dynamic-slice_fusion), channel_id=1, source_target_pairs={{0,1},{1,0},{2,3},{3,2},{4,5},{5,4},{6,7},{7,6},{8,9},{9,8},{10,11... | collective-permute-start | bytes 393224 | tf_op jit(solution)/shard_map/ppermute | solution.py:179
  12.1 1.9 %shard_map.95 = bf16[768,256]{1,0:T(8,128)(2,1)} custom-call(s32[64,128]{1,0:T(8,128)} %bitcast.8, bf16[512,256]{1,0:T(8,128)(2,1)} %ladder.1, bf16[256,256]{1,0:T(8,128)(2,1)} %amps.1), custom_call_target="tpu_custom_call" | custom-call | bytes 1048576 | tf_op jit(solution)/shard_map/pallas_call | solution.py:57
  14.1 0.8 fusion.5
  14.9 0.0 collective-permute-done
  14.9 0.8 fusion.1
  15.7 0.0 all-gather.2.cloned.1.call-update
  15.7 4.7 %collective-permute-start.1 = (bf16[256,256]{1,0:T(8,128)(2,1)}, bf16[256,256]{1,0:T(8,128)(2,1)S(1)}, u32[]{:S(2)}, u32[]{:S(2)}) collective-permute-start(bf16[256,256]{1,0:T(8,128)(2,1)} %amps.1), channel_id=1, source_target_pairs={{0,3},{1,2},{2,1},{3,0},{4,7},{5,6},{6,5},{7,4},{8,11},{9,10},{10,... | collective-permute-start | bytes 393224 | tf_op jit(solution)/shard_map/ppermute | solution.py:188
  20.4 0.9 %constant_dynamic-update-slice_fusion.1 = bf16[256,512]{1,0:T(8,128)(2,1)S(1)} fusion(bf16[256,256]{1,0:T(8,128)(2,1)} %amps.1), kind=kLoop, calls=%fused_computation.8 | loop fusion | bytes 262144
  21.4 1.6 %collective-permute-done.1 = bf16[256,256]{1,0:T(8,128)(2,1)S(1)} collective-permute-done((bf16[256,256]{1,0:T(8,128)(2,1)}, bf16[256,256]{1,0:T(8,128)(2,1)S(1)}, u32[]{:S(2)}, u32[]{:S(2)}) %collective-permute-start.1) | collective-permute-done | bytes 131104 | tf_op jit(solution)/shard_map/ppermute | solution.py:188
  23.0 4.2 %collective-permute-start.2 = (bf16[256,512]{1,0:T(8,128)(2,1)S(1)}, bf16[256,512]{1,0:T(8,128)(2,1)S(1)}, u32[]{:S(2)}, u32[]{:S(2)}) collective-permute-start(bf16[256,512]{1,0:T(8,128)(2,1)S(1)} %constant_dynamic-update-slice_fusion.refs_0_), channel_id=1, source_target_pairs={{0,4},{4,8},{8,12},{12,16},{16,20},{20,24},{24,28},{28,0},{1,5},{5... | collective-permute-start | bytes 786440 | tf_op jit(solution)/shard_map/ppermute | solution.py:193
  27.2 8.6 %collective-permute-start.3 = (bf16[256,512]{1,0:T(8,128)(2,1)S(1)}, bf16[256,512]{1,0:T(8,128)(2,1)S(1)}, u32[]{:S(2)}, u32[]{:S(2)}) collective-permute-start(bf16[256,512]{1,0:T(8,128)(2,1)S(1)} %constant_dynamic-update-slice_fusion.refs_0_), channel_id=1, source_target_pairs={{0,28},{4,0},{8,4},{12,8},{16,12},{20,16},{24,20},{28,24},{1,29},{... | collective-permute-start | bytes 786440 | tf_op jit(solution)/shard_map/ppermute | solution.py:194
  35.8 1.8 %collective-permute-done.2.refs_1_ = bf16[256,512]{1,0:T(8,128)(2,1)S(1)} collective-permute-done((bf16[256,512]{1,0:T(8,128)(2,1)S(1)}, bf16[256,512]{1,0:T(8,128)(2,1)S(1)}, u32[]{:S(2)}, u32[]{:S(2)}) %collective-permute-start.2) | collective-permute-done | bytes 262176 | tf_op jit(solution)/shard_map/ppermute | solution.py:193
  37.6 1.9 %collective-permute-start.4 = (bf16[256,512]{1,0:T(8,128)(2,1)S(1)}, bf16[256,512]{1,0:T(8,128)(2,1)S(1)}, u32[]{:S(2)}, u32[]{:S(2)}) collective-permute-start(bf16[256,512]{1,0:T(8,128)(2,1)S(1)} %collective-permute-done.2.refs_1_), channel_id=1, source_target_pairs={{0,4},{4,8},{8,12},{12,16},{16,20},{20,24},{24,28},{28,0},{1,5},{5... | collective-permute-start | bytes 786440 | tf_op jit(solution)/shard_map/ppermute | solution.py:193
  39.5 0.0 collective-permute-done.3.refs_2_
  39.5 4.6 %collective-permute-start.5 = (bf16[256,512]{1,0:T(8,128)(2,1)S(1)}, bf16[256,512]{1,0:T(8,128)(2,1)S(1)}, u32[]{:S(2)}, u32[]{:S(2)}) collective-permute-start(bf16[256,512]{1,0:T(8,128)(2,1)S(1)} %collective-permute-done.3.refs_2_), channel_id=1, source_target_pairs={{0,28},{4,0},{8,4},{12,8},{16,12},{20,16},{24,20},{28,24},{1,29},{... | collective-permute-start | bytes 786440 | tf_op jit(solution)/shard_map/ppermute | solution.py:194
  44.1 2.2 %collective-permute-done.4.refs_3_ = bf16[256,512]{1,0:T(8,128)(2,1)S(1)} collective-permute-done((bf16[256,512]{1,0:T(8,128)(2,1)S(1)}, bf16[256,512]{1,0:T(8,128)(2,1)S(1)}, u32[]{:S(2)}, u32[]{:S(2)}) %collective-permute-start.4) | collective-permute-done | bytes 262176 | tf_op jit(solution)/shard_map/ppermute | solution.py:193
  46.3 1.9 %collective-permute-start.6 = (bf16[256,512]{1,0:T(8,128)(2,1)S(1)}, bf16[256,512]{1,0:T(8,128)(2,1)S(1)}, u32[]{:S(2)}, u32[]{:S(2)}) collective-permute-start(bf16[256,512]{1,0:T(8,128)(2,1)S(1)} %collective-permute-done.4.refs_3_), channel_id=1, source_target_pairs={{0,4},{4,8},{8,12},{12,16},{16,20},{20,24},{24,28},{28,0},{1,5},{5... | collective-permute-start | bytes 786440 | tf_op jit(solution)/shard_map/ppermute | solution.py:193
  48.2 0.0 collective-permute-done.5.refs_4_
  48.2 4.6 %collective-permute-start.7 = (bf16[256,512]{1,0:T(8,128)(2,1)S(1)}, bf16[256,512]{1,0:T(8,128)(2,1)S(1)}, u32[]{:S(2)}, u32[]{:S(2)}) collective-permute-start(bf16[256,512]{1,0:T(8,128)(2,1)S(1)} %collective-permute-done.5.refs_4_), channel_id=1, source_target_pairs={{0,28},{4,0},{8,4},{12,8},{16,12},{20,16},{24,20},{28,24},{1,29},{... | collective-permute-start | bytes 786440 | tf_op jit(solution)/shard_map/ppermute | solution.py:194
  52.8 0.0 copy-done.2
  52.8 0.1 dynamic_slice.18
  52.9 2.1 %collective-permute-done.6.refs_5_ = bf16[256,512]{1,0:T(8,128)(2,1)S(1)} collective-permute-done((bf16[256,512]{1,0:T(8,128)(2,1)S(1)}, bf16[256,512]{1,0:T(8,128)(2,1)S(1)}, u32[]{:S(2)}, u32[]{:S(2)}) %collective-permute-start.6) | collective-permute-done | bytes 262176 | tf_op jit(solution)/shard_map/ppermute | solution.py:193
  55.0 1.9 %collective-permute-start.8 = (bf16[256,256]{1,0:T(8,128)(2,1)S(1)}, bf16[256,256]{1,0:T(8,128)(2,1)S(1)}, u32[]{:S(2)}, u32[]{:S(2)}) collective-permute-start(bf16[256,256]{1,0:T(8,128)(2,1)S(1)} %slice.16), channel_id=1, source_target_pairs={{0,4},{4,8},{8,12},{12,16},{16,20},{20,24},{24,28},{28,0},{1,5},{5... | collective-permute-start | bytes 393224 | tf_op jit(solution)/shard_map/ppermute | solution.py:196
  57.0 0.0 collective-permute-done.7.refs_6_
  57.0 4.6 %collective-permute-start.9 = (bf16[256,256]{1,0:T(8,128)(2,1)S(1)}, bf16[256,256]{1,0:T(8,128)(2,1)S(1)}, u32[]{:S(2)}, u32[]{:S(2)}) collective-permute-start(bf16[256,256]{1,0:T(8,128)(2,1)S(1)} %slice.17), channel_id=1, source_target_pairs={{0,28},{4,0},{8,4},{12,8},{16,12},{20,16},{24,20},{28,24},{1,29},{... | collective-permute-start | bytes 393224 | tf_op jit(solution)/shard_map/ppermute | solution.py:197
  61.6 3.5 %compare_select_fusion.hole = bf16[256,4096]{1,0:T(8,128)(2,1)} fusion(bf16[256,4096]{1,0:T(8,128)(2,1)} %param.13, s32[4096]{0:T(1024)S(1)} %copy-done.2, s32[256]{0:T(256)S(1)} %dynamic_slice.18), kind=kLoop, calls=%fused_computation | loop fusion | flops 2097152 | bytes 4211712 | tf_op jit(solution)/shard_map/jit(_where)/select_n | solution.py:200
  65.1 0.0 copy-start.3
  65.1 0.0 copy-start
  65.1 0.0 collective-permute-done.8.refs_7_
  65.1 0.0 collective-permute-done.9.refs_8_
  65.1 5.5 %all-gather.2.cloned.1.call-done.gathered = bf16[16,768,256]{2,1,0:T(8,128)(2,1)} async-done(((bf16[1,768,256]{2,1,0:T(8,128)(2,1)}), bf16[16,768,256]{2,1,0:T(8,128)(2,1)}) %all-gather.2.cloned.1.call-update) | async-done | bytes 6291472 | tf_op jit(solution)/shard_map/all_gather | solution.py:186
  70.6 2.8 %shard_map.97 = s16[272,256]{1,0:T(8,128)(2,1)S(1)} custom-call(bf16[16,768,256]{2,1,0:T(8,128)(2,1)} %all-gather.2.cloned.1.call-done.gathered, bf16[256,512]{1,0:T(8,128)(2,1)S(1)} %constant_dynamic-update-slice_fusion.refs_0_, bf16[256,512]{1,0:T(8,128)(2,1)S(1)} %collective-permute-done.2.refs_1_, bf16[256,512]{1,0:T(8,128)(2,1)S(1)} %collective-permute-done.3.refs_2_, ...), custom_call_target="tpu_custom_call" | custom-call | flops 536870912 | bytes 4194304 | tf_op jit(solution)/shard_map/pallas_call | solution.py:160
  73.4 3.1 %collective-permute-start.10 = (s16[272,256]{1,0:T(8,128)(2,1)S(1)}, s16[272,256]{1,0:T(8,128)(2,1)S(1)}, u32[]{:S(2)}, u32[]{:S(2)}) collective-permute-start(s16[272,256]{1,0:T(8,128)(2,1)S(1)} %shard_map.97), channel_id=1, source_target_pairs={{0,1},{1,0},{2,3},{3,2},{4,5},{5,4},{6,7},{7,6},{8,9},{9,8},{10,11... | collective-permute-start | bytes 417800 | tf_op jit(solution)/shard_map/ppermute | solution.py:207
  76.5 0.0 copy-done.3
  76.5 0.1 broadcast_add_fusion
  76.6 0.1 add.60
  76.7 0.1 dynamic_slice.19
  76.8 0.0 copy-done
  76.8 0.0 copy-start.1
  76.8 0.0 copy-start.4
  76.8 4.6 %shard_map.96 = f32[256,256]{1,0:T(8,128)S(1)} custom-call(bf16[16,768,256]{2,1,0:T(8,128)(2,1)} %all-gather.2.cloned.1.call-done.gathered, bf16[256,4096]{1,0:T(8,128)(2,1)} %compare_select_fusion.hole, bf16[256,512]{1,0:T(8,128)(2,1)S(1)} %constant_dynamic-update-slice_fusion.refs_0_, bf16[256,512]{1,0:T(8,128)(2,1)S(1)} %collective-permute-done.2.refs_1_, ...), custom_call_target="tpu_custom_call" | custom-call | flops 1073741824 | bytes 8388608 | tf_op jit(solution)/shard_map/pallas_call | solution.py:160
  81.4 0.0 collective-permute-done.10
  81.4 0.0 copy-done.1
  81.4 0.0 copy-done.4
  81.4 0.8 subtract_convert_fusion
  (4 shorter events, 0.0 us)
Async XLA Ops:
  7.2 45.7 %copy-start.2 = (s32[4096]{0:T(1024)S(1)}, s32[4096]{0:T(1024)}, u32[]{:S(2)}) copy-start(s32[4096]{0:T(1024)} %param.11) | copy-start | bytes 49156
  7.2 63.5 %all-gather.2.cloned.1.call-start = ((), (), s32[]{:S(2)}) async-start(), calls=%async_computation | async-start | bytes 6684672 | tf_op jit(solution)/shard_map/all_gather | solution.py:186
  8.2 6.7 %collective-permute-start = (bf16[256,256]{1,0:T(8,128)(2,1)S(1)}, bf16[256,256]{1,0:T(8,128)(2,1)S(1)}, u32[]{:S(2)}, u32[]{:S(2)}) collective-permute-start(bf16[256,256]{1,0:T(8,128)(2,1)S(1)} %constant_dynamic-slice_fusion), channel_id=1, source_target_pairs={{0,1},{1,0},{2,3},{3,2},{4,5},{5,4},{6,7},{7,6},{8,9},{9,8},{10,11... | collective-permute-start | bytes 393224 | tf_op jit(solution)/shard_map/ppermute | solution.py:179
  15.7 7.3 %collective-permute-start.1 = (bf16[256,256]{1,0:T(8,128)(2,1)}, bf16[256,256]{1,0:T(8,128)(2,1)S(1)}, u32[]{:S(2)}, u32[]{:S(2)}) collective-permute-start(bf16[256,256]{1,0:T(8,128)(2,1)} %amps.1), channel_id=1, source_target_pairs={{0,3},{1,2},{2,1},{3,0},{4,7},{5,6},{6,5},{7,4},{8,11},{9,10},{10,... | collective-permute-start | bytes 393224 | tf_op jit(solution)/shard_map/ppermute | solution.py:188
  23.0 14.6 %collective-permute-start.2 = (bf16[256,512]{1,0:T(8,128)(2,1)S(1)}, bf16[256,512]{1,0:T(8,128)(2,1)S(1)}, u32[]{:S(2)}, u32[]{:S(2)}) collective-permute-start(bf16[256,512]{1,0:T(8,128)(2,1)S(1)} %constant_dynamic-update-slice_fusion.refs_0_), channel_id=1, source_target_pairs={{0,4},{4,8},{8,12},{12,16},{16,20},{20,24},{24,28},{28,0},{1,5},{5... | collective-permute-start | bytes 786440 | tf_op jit(solution)/shard_map/ppermute | solution.py:193
  27.2 12.3 %collective-permute-start.3 = (bf16[256,512]{1,0:T(8,128)(2,1)S(1)}, bf16[256,512]{1,0:T(8,128)(2,1)S(1)}, u32[]{:S(2)}, u32[]{:S(2)}) collective-permute-start(bf16[256,512]{1,0:T(8,128)(2,1)S(1)} %constant_dynamic-update-slice_fusion.refs_0_), channel_id=1, source_target_pairs={{0,28},{4,0},{8,4},{12,8},{16,12},{20,16},{24,20},{28,24},{1,29},{... | collective-permute-start | bytes 786440 | tf_op jit(solution)/shard_map/ppermute | solution.py:194
  37.6 8.7 %collective-permute-start.4 = (bf16[256,512]{1,0:T(8,128)(2,1)S(1)}, bf16[256,512]{1,0:T(8,128)(2,1)S(1)}, u32[]{:S(2)}, u32[]{:S(2)}) collective-permute-start(bf16[256,512]{1,0:T(8,128)(2,1)S(1)} %collective-permute-done.2.refs_1_), channel_id=1, source_target_pairs={{0,4},{4,8},{8,12},{12,16},{16,20},{20,24},{24,28},{28,0},{1,5},{5... | collective-permute-start | bytes 786440 | tf_op jit(solution)/shard_map/ppermute | solution.py:193
  39.5 8.7 %collective-permute-start.5 = (bf16[256,512]{1,0:T(8,128)(2,1)S(1)}, bf16[256,512]{1,0:T(8,128)(2,1)S(1)}, u32[]{:S(2)}, u32[]{:S(2)}) collective-permute-start(bf16[256,512]{1,0:T(8,128)(2,1)S(1)} %collective-permute-done.3.refs_2_), channel_id=1, source_target_pairs={{0,28},{4,0},{8,4},{12,8},{16,12},{20,16},{24,20},{28,24},{1,29},{... | collective-permute-start | bytes 786440 | tf_op jit(solution)/shard_map/ppermute | solution.py:194
  46.3 8.7 %collective-permute-start.6 = (bf16[256,512]{1,0:T(8,128)(2,1)S(1)}, bf16[256,512]{1,0:T(8,128)(2,1)S(1)}, u32[]{:S(2)}, u32[]{:S(2)}) collective-permute-start(bf16[256,512]{1,0:T(8,128)(2,1)S(1)} %collective-permute-done.4.refs_3_), channel_id=1, source_target_pairs={{0,4},{4,8},{8,12},{12,16},{16,20},{20,24},{24,28},{28,0},{1,5},{5... | collective-permute-start | bytes 786440 | tf_op jit(solution)/shard_map/ppermute | solution.py:193
  48.2 8.7 %collective-permute-start.7 = (bf16[256,512]{1,0:T(8,128)(2,1)S(1)}, bf16[256,512]{1,0:T(8,128)(2,1)S(1)}, u32[]{:S(2)}, u32[]{:S(2)}) collective-permute-start(bf16[256,512]{1,0:T(8,128)(2,1)S(1)} %collective-permute-done.5.refs_4_), channel_id=1, source_target_pairs={{0,28},{4,0},{8,4},{12,8},{16,12},{20,16},{24,20},{28,24},{1,29},{... | collective-permute-start | bytes 786440 | tf_op jit(solution)/shard_map/ppermute | solution.py:194
  55.0 10.1 %collective-permute-start.8 = (bf16[256,256]{1,0:T(8,128)(2,1)S(1)}, bf16[256,256]{1,0:T(8,128)(2,1)S(1)}, u32[]{:S(2)}, u32[]{:S(2)}) collective-permute-start(bf16[256,256]{1,0:T(8,128)(2,1)S(1)} %slice.16), channel_id=1, source_target_pairs={{0,4},{4,8},{8,12},{12,16},{16,20},{20,24},{24,28},{28,0},{1,5},{5... | collective-permute-start | bytes 393224 | tf_op jit(solution)/shard_map/ppermute | solution.py:196
  57.0 8.1 %collective-permute-start.9 = (bf16[256,256]{1,0:T(8,128)(2,1)S(1)}, bf16[256,256]{1,0:T(8,128)(2,1)S(1)}, u32[]{:S(2)}, u32[]{:S(2)}) collective-permute-start(bf16[256,256]{1,0:T(8,128)(2,1)S(1)} %slice.17), channel_id=1, source_target_pairs={{0,28},{4,0},{8,4},{12,8},{16,12},{20,16},{24,20},{28,24},{1,29},{... | collective-permute-start | bytes 393224 | tf_op jit(solution)/shard_map/ppermute | solution.py:197
  65.1 11.4 %copy-start.3 = (f32[64]{0:T(128)S(1)}, f32[64]{0:T(128)}, u32[]{:S(2)}) copy-start(f32[64]{0:T(128)} %param.14) | copy-start | bytes 772
  65.1 11.6 %copy-start = (f32[256,256]{1,0:T(8,128)S(1)}, f32[256,256]{1,0:T(8,128)}, u32[]{:S(2)}) copy-start(f32[256,256]{1,0:T(8,128)} %refs_9_.1) | copy-start | bytes 786436
  73.4 8.0 %collective-permute-start.10 = (s16[272,256]{1,0:T(8,128)(2,1)S(1)}, s16[272,256]{1,0:T(8,128)(2,1)S(1)}, u32[]{:S(2)}, u32[]{:S(2)}) collective-permute-start(s16[272,256]{1,0:T(8,128)(2,1)S(1)} %shard_map.97), channel_id=1, source_target_pairs={{0,1},{1,0},{2,3},{3,2},{4,5},{5,4},{6,7},{7,6},{8,9},{9,8},{10,11... | collective-permute-start | bytes 417800 | tf_op jit(solution)/shard_map/ppermute | solution.py:207
  76.8 4.7 %copy-start.1 = (bf16[256,256]{1,0:T(8,128)(2,1)S(1)}, bf16[256,256]{1,0:T(8,128)(2,1)}, u32[]{:S(2)}) copy-start(bf16[256,256]{1,0:T(8,128)(2,1)} %amps.1) | copy-start | bytes 393220
  76.8 4.7 %copy-start.4 = (f32[256]{0:T(256)S(1)}, f32[256]{0:T(256)}, u32[]{:S(2)}) copy-start(f32[256]{0:T(256)} %param.15) | copy-start | bytes 3076
Sparse Core Ops, SparseCore 0:
  15.8 54.7 all-gather.1

commit v6 on v5

--- a/solution.py
+++ b/solution.py
@@ -8,7 +8,8 @@
 NY, NCORE, NZ, NX = 8, 2, 8, 4
 BF16, F32 = jnp.bfloat16, jnp.float32
 LANES = 128
-FIXED_BITS = 14
+FIXED_BITS = 15
+FIXED_MOST = 2.0**15 - 1
 EXPONENT_ROWS = 16
 
 
@@ -104,6 +105,7 @@
     largest = jnp.max(jnp.abs(acc[...]), axis=0, keepdims=True)
     exponent = jnp.ceil(jnp.log2(jnp.maximum(largest, 2.0**-100)))
     fixed = jnp.round(acc[...] * jnp.exp2(FIXED_BITS - exponent))
+    fixed = jnp.clip(fixed, -FIXED_MOST, FIXED_MOST)
     out_ref[:size, :] = fixed.astype(jnp.int32).astype(jnp.int16)
     rows = out_ref.shape[0] - size
     line = jnp.broadcast_to(exponent, (rows, exponent.shape[1]))

time: 89.6 us -> 89.6 us (level)
  no operation moved by 1% of the time
where the time goes in v6:
time: 89.6 us; the launch traced here: 89.1 us
  starting transfers between devices  44.1 us (49%)
  between operations  14.3 us (16%)
  waiting for transfers between devices  13.3 us (15%)
  Pallas kernels  9.32 us (10%)
  other arithmetic  5.19 us (6%)
  local copies, waits for them, and re-layouts  2.95 us (3%)
    ppermute x3, starting transfers between devices, body(): b = lax.ppermute(b, 'z', shift(NZ, -1))  17.7 us
    ppermute x3, starting transfers between devices, body(): f = lax.ppermute(f, 'z', shift(NZ, 1))  8 us
    pallas_call x2, Pallas kernels, products(): pl.pallas_call(kernel, out_shape=out, in_specs=[hbm] * len(in_hbm) + [vme...  7.41 us
    ppermute x3, waiting for transfers between devices, body(): f = lax.ppermute(f, 'z', shift(NZ, 1))  6.14 us
    all_gather x1, waiting for transfers between devices, body(): gathered = lax.all_gather(rows, ('y', 'core'), axis=0, tiled=False)  5.5 us
    ppermute x1, starting transfers between devices, body(): other = lax.ppermute(amplitudes, 'x', [(i, NX - 1 - i) for i in range(NX)])  4.74 us
    ppermute x1, starting transfers between devices, body(): parts.append(lax.ppermute(b[:, size:], 'z', shift(NZ, -1)))  4.57 us
    ppermute x1, starting transfers between devices, body(): lent = lax.ppermute(lent, 'x', partner)  3.95 us
  transfers between devices with their start and end apart: 12, of which 5 were waited for; matrix products, arithmetic and copies ran while one was open for 6% of the time, Pallas kernels for 7%

profile of v6, /device:TPU:1, one launch (start us, length us, event | category | flops | bytes accessed | tf_op | source)
XLA Modules:
  0.0 89.1 jit_solution(15638005267169897567)
XLA Ops:
  7.2 0.0 copy-start.2
  7.2 0.0 all-gather.2.cloned.1.call-start
  7.2 0.9 %constant_dynamic-slice_fusion = bf16[256,256]{1,0:T(8,128)(2,1)S(1)} fusion(bf16[512,256]{1,0:T(8,128)(2,1)} %ladder.1, s32[]{:T(128)S(6)} %select_n.23), kind=kLoop, calls=%fused_computation.13 | loop fusion | bytes 262148 | tf_op jit(solution)/shard_map/dynamic_slice | solution.py:180
  8.2 3.9 %collective-permute-start = (bf16[256,256]{1,0:T(8,128)(2,1)S(1)}, bf16[256,256]{1,0:T(8,128)(2,1)S(1)}, u32[]{:S(2)}, u32[]{:S(2)}) collective-permute-start(bf16[256,256]{1,0:T(8,128)(2,1)S(1)} %constant_dynamic-slice_fusion), channel_id=1, source_target_pairs={{0,1},{1,0},{2,3},{3,2},{4,5},{5,4},{6,7},{7,6},{8,9},{9,8},{10,11... | collective-permute-start | bytes 393224 | tf_op jit(solution)/shard_map/ppermute | solution.py:181
  12.1 1.9 %shard_map.95 = bf16[768,256]{1,0:T(8,128)(2,1)} custom-call(s32[64,128]{1,0:T(8,128)} %bitcast.8, bf16[512,256]{1,0:T(8,128)(2,1)} %ladder.1, bf16[256,256]{1,0:T(8,128)(2,1)} %amps.1), custom_call_target="tpu_custom_call" | custom-call | bytes 1048576 | tf_op jit(solution)/shard_map/pallas_call | solution.py:58
  14.1 0.8 fusion.5
  14.9 0.0 collective-permute-done
  14.9 0.8 fusion.1
  15.7 0.0 all-gather.2.cloned.1.call-update
  15.7 4.7 %collective-permute-start.1 = (bf16[256,256]{1,0:T(8,128)(2,1)}, bf16[256,256]{1,0:T(8,128)(2,1)S(1)}, u32[]{:S(2)}, u32[]{:S(2)}) collective-permute-start(bf16[256,256]{1,0:T(8,128)(2,1)} %amps.1), channel_id=1, source_target_pairs={{0,3},{1,2},{2,1},{3,0},{4,7},{5,6},{6,5},{7,4},{8,11},{9,10},{10,... | collective-permute-start | bytes 393224 | tf_op jit(solution)/shard_map/ppermute | solution.py:190
  20.4 0.9 %constant_dynamic-update-slice_fusion.1 = bf16[256,512]{1,0:T(8,128)(2,1)S(1)} fusion(bf16[256,256]{1,0:T(8,128)(2,1)} %amps.1), kind=kLoop, calls=%fused_computation.8 | loop fusion | bytes 262144
  21.4 1.6 %collective-permute-done.1 = bf16[256,256]{1,0:T(8,128)(2,1)S(1)} collective-permute-done((bf16[256,256]{1,0:T(8,128)(2,1)}, bf16[256,256]{1,0:T(8,128)(2,1)S(1)}, u32[]{:S(2)}, u32[]{:S(2)}) %collective-permute-start.1) | collective-permute-done | bytes 131104 | tf_op jit(solution)/shard_map/ppermute | solution.py:190
  23.0 4.2 %collective-permute-start.2 = (bf16[256,512]{1,0:T(8,128)(2,1)S(1)}, bf16[256,512]{1,0:T(8,128)(2,1)S(1)}, u32[]{:S(2)}, u32[]{:S(2)}) collective-permute-start(bf16[256,512]{1,0:T(8,128)(2,1)S(1)} %constant_dynamic-update-slice_fusion.refs_0_), channel_id=1, source_target_pairs={{0,4},{4,8},{8,12},{12,16},{16,20},{20,24},{24,28},{28,0},{1,5},{5... | collective-permute-start | bytes 786440 | tf_op jit(solution)/shard_map/ppermute | solution.py:195
  27.2 8.6 %collective-permute-start.3 = (bf16[256,512]{1,0:T(8,128)(2,1)S(1)}, bf16[256,512]{1,0:T(8,128)(2,1)S(1)}, u32[]{:S(2)}, u32[]{:S(2)}) collective-permute-start(bf16[256,512]{1,0:T(8,128)(2,1)S(1)} %constant_dynamic-update-slice_fusion.refs_0_), channel_id=1, source_target_pairs={{0,28},{4,0},{8,4},{12,8},{16,12},{20,16},{24,20},{28,24},{1,29},{... | collective-permute-start | bytes 786440 | tf_op jit(solution)/shard_map/ppermute | solution.py:196
  35.8 1.8 %collective-permute-done.2.refs_1_ = bf16[256,512]{1,0:T(8,128)(2,1)S(1)} collective-permute-done((bf16[256,512]{1,0:T(8,128)(2,1)S(1)}, bf16[256,512]{1,0:T(8,128)(2,1)S(1)}, u32[]{:S(2)}, u32[]{:S(2)}) %collective-permute-start.2) | collective-permute-done | bytes 262176 | tf_op jit(solution)/shard_map/ppermute | solution.py:195
  37.6 1.9 %collective-permute-start.4 = (bf16[256,512]{1,0:T(8,128)(2,1)S(1)}, bf16[256,512]{1,0:T(8,128)(2,1)S(1)}, u32[]{:S(2)}, u32[]{:S(2)}) collective-permute-start(bf16[256,512]{1,0:T(8,128)(2,1)S(1)} %collective-permute-done.2.refs_1_), channel_id=1, source_target_pairs={{0,4},{4,8},{8,12},{12,16},{16,20},{20,24},{24,28},{28,0},{1,5},{5... | collective-permute-start | bytes 786440 | tf_op jit(solution)/shard_map/ppermute | solution.py:195
  39.5 0.0 collective-permute-done.3.refs_2_
  39.5 4.6 %collective-permute-start.5 = (bf16[256,512]{1,0:T(8,128)(2,1)S(1)}, bf16[256,512]{1,0:T(8,128)(2,1)S(1)}, u32[]{:S(2)}, u32[]{:S(2)}) collective-permute-start(bf16[256,512]{1,0:T(8,128)(2,1)S(1)} %collective-permute-done.3.refs_2_), channel_id=1, source_target_pairs={{0,28},{4,0},{8,4},{12,8},{16,12},{20,16},{24,20},{28,24},{1,29},{... | collective-permute-start | bytes 786440 | tf_op jit(solution)/shard_map/ppermute | solution.py:196
  44.1 2.2 %collective-permute-done.4.refs_3_ = bf16[256,512]{1,0:T(8,128)(2,1)S(1)} collective-permute-done((bf16[256,512]{1,0:T(8,128)(2,1)S(1)}, bf16[256,512]{1,0:T(8,128)(2,1)S(1)}, u32[]{:S(2)}, u32[]{:S(2)}) %collective-permute-start.4) | collective-permute-done | bytes 262176 | tf_op jit(solution)/shard_map/ppermute | solution.py:195
  46.3 1.9 %collective-permute-start.6 = (bf16[256,512]{1,0:T(8,128)(2,1)S(1)}, bf16[256,512]{1,0:T(8,128)(2,1)S(1)}, u32[]{:S(2)}, u32[]{:S(2)}) collective-permute-start(bf16[256,512]{1,0:T(8,128)(2,1)S(1)} %collective-permute-done.4.refs_3_), channel_id=1, source_target_pairs={{0,4},{4,8},{8,12},{12,16},{16,20},{20,24},{24,28},{28,0},{1,5},{5... | collective-permute-start | bytes 786440 | tf_op jit(solution)/shard_map/ppermute | solution.py:195
  48.2 0.0 collective-permute-done.5.refs_4_
  48.2 4.6 %collective-permute-start.7 = (bf16[256,512]{1,0:T(8,128)(2,1)S(1)}, bf16[256,512]{1,0:T(8,128)(2,1)S(1)}, u32[]{:S(2)}, u32[]{:S(2)}) collective-permute-start(bf16[256,512]{1,0:T(8,128)(2,1)S(1)} %collective-permute-done.5.refs_4_), channel_id=1, source_target_pairs={{0,28},{4,0},{8,4},{12,8},{16,12},{20,16},{24,20},{28,24},{1,29},{... | collective-permute-start | bytes 786440 | tf_op jit(solution)/shard_map/ppermute | solution.py:196
  52.8 0.0 copy-done.2
  52.8 0.1 dynamic_slice.18
  52.9 2.1 %collective-permute-done.6.refs_5_ = bf16[256,512]{1,0:T(8,128)(2,1)S(1)} collective-permute-done((bf16[256,512]{1,0:T(8,128)(2,1)S(1)}, bf16[256,512]{1,0:T(8,128)(2,1)S(1)}, u32[]{:S(2)}, u32[]{:S(2)}) %collective-permute-start.6) | collective-permute-done | bytes 262176 | tf_op jit(solution)/shard_map/ppermute | solution.py:195
  55.0 1.9 %collective-permute-start.8 = (bf16[256,256]{1,0:T(8,128)(2,1)S(1)}, bf16[256,256]{1,0:T(8,128)(2,1)S(1)}, u32[]{:S(2)}, u32[]{:S(2)}) collective-permute-start(bf16[256,256]{1,0:T(8,128)(2,1)S(1)} %slice.16), channel_id=1, source_target_pairs={{0,4},{4,8},{8,12},{12,16},{16,20},{20,24},{24,28},{28,0},{1,5},{5... | collective-permute-start | bytes 393224 | tf_op jit(solution)/shard_map/ppermute | solution.py:198
  57.0 0.0 collective-permute-done.7.refs_6_
  57.0 4.6 %collective-permute-start.9 = (bf16[256,256]{1,0:T(8,128)(2,1)S(1)}, bf16[256,256]{1,0:T(8,128)(2,1)S(1)}, u32[]{:S(2)}, u32[]{:S(2)}) collective-permute-start(bf16[256,256]{1,0:T(8,128)(2,1)S(1)} %slice.17), channel_id=1, source_target_pairs={{0,28},{4,0},{8,4},{12,8},{16,12},{20,16},{24,20},{28,24},{1,29},{... | collective-permute-start | bytes 393224 | tf_op jit(solution)/shard_map/ppermute | solution.py:199
  61.6 3.5 %compare_select_fusion.hole = bf16[256,4096]{1,0:T(8,128)(2,1)} fusion(bf16[256,4096]{1,0:T(8,128)(2,1)} %param.13, s32[4096]{0:T(1024)S(1)} %copy-done.2, s32[256]{0:T(256)S(1)} %dynamic_slice.18), kind=kLoop, calls=%fused_computation | loop fusion | flops 2097152 | bytes 4211712 | tf_op jit(solution)/shard_map/jit(_where)/select_n | solution.py:202
  65.1 0.0 copy-start.3
  65.1 0.0 copy-start
  65.1 0.0 collective-permute-done.8.refs_7_
  65.1 0.0 collective-permute-done.9.refs_8_
  65.1 5.5 %all-gather.2.cloned.1.call-done.gathered = bf16[16,768,256]{2,1,0:T(8,128)(2,1)} async-done(((bf16[1,768,256]{2,1,0:T(8,128)(2,1)}), bf16[16,768,256]{2,1,0:T(8,128)(2,1)}) %all-gather.2.cloned.1.call-update) | async-done | bytes 6291472 | tf_op jit(solution)/shard_map/all_gather | solution.py:188
  70.6 2.8 %shard_map.97 = s16[272,256]{1,0:T(8,128)(2,1)S(1)} custom-call(bf16[16,768,256]{2,1,0:T(8,128)(2,1)} %all-gather.2.cloned.1.call-done.gathered, bf16[256,512]{1,0:T(8,128)(2,1)S(1)} %constant_dynamic-update-slice_fusion.refs_0_, bf16[256,512]{1,0:T(8,128)(2,1)S(1)} %collective-permute-done.2.refs_1_, bf16[256,512]{1,0:T(8,128)(2,1)S(1)} %collective-permute-done.3.refs_2_, ...), custom_call_target="tpu_custom_call" | custom-call | flops 536870912 | bytes 4194304 | tf_op jit(solution)/shard_map/pallas_call | solution.py:162
  73.4 3.1 %collective-permute-start.10 = (s16[272,256]{1,0:T(8,128)(2,1)S(1)}, s16[272,256]{1,0:T(8,128)(2,1)S(1)}, u32[]{:S(2)}, u32[]{:S(2)}) collective-permute-start(s16[272,256]{1,0:T(8,128)(2,1)S(1)} %shard_map.97), channel_id=1, source_target_pairs={{0,1},{1,0},{2,3},{3,2},{4,5},{5,4},{6,7},{7,6},{8,9},{9,8},{10,11... | collective-permute-start | bytes 417800 | tf_op jit(solution)/shard_map/ppermute | solution.py:209
  76.5 0.0 copy-done.3
  76.5 0.1 broadcast_add_fusion
  76.6 0.1 add.60
  76.7 0.1 dynamic_slice.19
  76.8 0.0 copy-done
  76.8 0.0 copy-start.1
  76.8 0.0 copy-start.4
  76.8 4.6 %shard_map.96 = f32[256,256]{1,0:T(8,128)S(1)} custom-call(bf16[16,768,256]{2,1,0:T(8,128)(2,1)} %all-gather.2.cloned.1.call-done.gathered, bf16[256,4096]{1,0:T(8,128)(2,1)} %compare_select_fusion.hole, bf16[256,512]{1,0:T(8,128)(2,1)S(1)} %constant_dynamic-update-slice_fusion.refs_0_, bf16[256,512]{1,0:T(8,128)(2,1)S(1)} %collective-permute-done.2.refs_1_, ...), custom_call_target="tpu_custom_call" | custom-call | flops 1073741824 | bytes 8388608 | tf_op jit(solution)/shard_map/pallas_call | solution.py:162
  81.4 0.0 collective-permute-done.10
  81.4 0.0 copy-done.1
  81.4 0.0 copy-done.4
  81.4 0.8 subtract_convert_fusion
  (4 shorter events, 0.0 us)
Async XLA Ops:
  7.2 45.7 %copy-start.2 = (s32[4096]{0:T(1024)S(1)}, s32[4096]{0:T(1024)}, u32[]{:S(2)}) copy-start(s32[4096]{0:T(1024)} %param.11) | copy-start | bytes 49156
  7.2 63.5 %all-gather.2.cloned.1.call-start = ((), (), s32[]{:S(2)}) async-start(), calls=%async_computation | async-start | bytes 6684672 | tf_op jit(solution)/shard_map/all_gather | solution.py:188
  8.2 6.7 %collective-permute-start = (bf16[256,256]{1,0:T(8,128)(2,1)S(1)}, bf16[256,256]{1,0:T(8,128)(2,1)S(1)}, u32[]{:S(2)}, u32[]{:S(2)}) collective-permute-start(bf16[256,256]{1,0:T(8,128)(2,1)S(1)} %constant_dynamic-slice_fusion), channel_id=1, source_target_pairs={{0,1},{1,0},{2,3},{3,2},{4,5},{5,4},{6,7},{7,6},{8,9},{9,8},{10,11... | collective-permute-start | bytes 393224 | tf_op jit(solution)/shard_map/ppermute | solution.py:181
  15.7 7.3 %collective-permute-start.1 = (bf16[256,256]{1,0:T(8,128)(2,1)}, bf16[256,256]{1,0:T(8,128)(2,1)S(1)}, u32[]{:S(2)}, u32[]{:S(2)}) collective-permute-start(bf16[256,256]{1,0:T(8,128)(2,1)} %amps.1), channel_id=1, source_target_pairs={{0,3},{1,2},{2,1},{3,0},{4,7},{5,6},{6,5},{7,4},{8,11},{9,10},{10,... | collective-permute-start | bytes 393224 | tf_op jit(solution)/shard_map/ppermute | solution.py:190
  23.0 14.6 %collective-permute-start.2 = (bf16[256,512]{1,0:T(8,128)(2,1)S(1)}, bf16[256,512]{1,0:T(8,128)(2,1)S(1)}, u32[]{:S(2)}, u32[]{:S(2)}) collective-permute-start(bf16[256,512]{1,0:T(8,128)(2,1)S(1)} %constant_dynamic-update-slice_fusion.refs_0_), channel_id=1, source_target_pairs={{0,4},{4,8},{8,12},{12,16},{16,20},{20,24},{24,28},{28,0},{1,5},{5... | collective-permute-start | bytes 786440 | tf_op jit(solution)/shard_map/ppermute | solution.py:195
  27.2 12.3 %collective-permute-start.3 = (bf16[256,512]{1,0:T(8,128)(2,1)S(1)}, bf16[256,512]{1,0:T(8,128)(2,1)S(1)}, u32[]{:S(2)}, u32[]{:S(2)}) collective-permute-start(bf16[256,512]{1,0:T(8,128)(2,1)S(1)} %constant_dynamic-update-slice_fusion.refs_0_), channel_id=1, source_target_pairs={{0,28},{4,0},{8,4},{12,8},{16,12},{20,16},{24,20},{28,24},{1,29},{... | collective-permute-start | bytes 786440 | tf_op jit(solution)/shard_map/ppermute | solution.py:196
  37.6 8.7 %collective-permute-start.4 = (bf16[256,512]{1,0:T(8,128)(2,1)S(1)}, bf16[256,512]{1,0:T(8,128)(2,1)S(1)}, u32[]{:S(2)}, u32[]{:S(2)}) collective-permute-start(bf16[256,512]{1,0:T(8,128)(2,1)S(1)} %collective-permute-done.2.refs_1_), channel_id=1, source_target_pairs={{0,4},{4,8},{8,12},{12,16},{16,20},{20,24},{24,28},{28,0},{1,5},{5... | collective-permute-start | bytes 786440 | tf_op jit(solution)/shard_map/ppermute | solution.py:195
  39.5 8.7 %collective-permute-start.5 = (bf16[256,512]{1,0:T(8,128)(2,1)S(1)}, bf16[256,512]{1,0:T(8,128)(2,1)S(1)}, u32[]{:S(2)}, u32[]{:S(2)}) collective-permute-start(bf16[256,512]{1,0:T(8,128)(2,1)S(1)} %collective-permute-done.3.refs_2_), channel_id=1, source_target_pairs={{0,28},{4,0},{8,4},{12,8},{16,12},{20,16},{24,20},{28,24},{1,29},{... | collective-permute-start | bytes 786440 | tf_op jit(solution)/shard_map/ppermute | solution.py:196
  46.3 8.7 %collective-permute-start.6 = (bf16[256,512]{1,0:T(8,128)(2,1)S(1)}, bf16[256,512]{1,0:T(8,128)(2,1)S(1)}, u32[]{:S(2)}, u32[]{:S(2)}) collective-permute-start(bf16[256,512]{1,0:T(8,128)(2,1)S(1)} %collective-permute-done.4.refs_3_), channel_id=1, source_target_pairs={{0,4},{4,8},{8,12},{12,16},{16,20},{20,24},{24,28},{28,0},{1,5},{5... | collective-permute-start | bytes 786440 | tf_op jit(solution)/shard_map/ppermute | solution.py:195
  48.2 8.7 %collective-permute-start.7 = (bf16[256,512]{1,0:T(8,128)(2,1)S(1)}, bf16[256,512]{1,0:T(8,128)(2,1)S(1)}, u32[]{:S(2)}, u32[]{:S(2)}) collective-permute-start(bf16[256,512]{1,0:T(8,128)(2,1)S(1)} %collective-permute-done.5.refs_4_), channel_id=1, source_target_pairs={{0,28},{4,0},{8,4},{12,8},{16,12},{20,16},{24,20},{28,24},{1,29},{... | collective-permute-start | bytes 786440 | tf_op jit(solution)/shard_map/ppermute | solution.py:196
  55.0 10.1 %collective-permute-start.8 = (bf16[256,256]{1,0:T(8,128)(2,1)S(1)}, bf16[256,256]{1,0:T(8,128)(2,1)S(1)}, u32[]{:S(2)}, u32[]{:S(2)}) collective-permute-start(bf16[256,256]{1,0:T(8,128)(2,1)S(1)} %slice.16), channel_id=1, source_target_pairs={{0,4},{4,8},{8,12},{12,16},{16,20},{20,24},{24,28},{28,0},{1,5},{5... | collective-permute-start | bytes 393224 | tf_op jit(solution)/shard_map/ppermute | solution.py:198
  57.0 8.1 %collective-permute-start.9 = (bf16[256,256]{1,0:T(8,128)(2,1)S(1)}, bf16[256,256]{1,0:T(8,128)(2,1)S(1)}, u32[]{:S(2)}, u32[]{:S(2)}) collective-permute-start(bf16[256,256]{1,0:T(8,128)(2,1)S(1)} %slice.17), channel_id=1, source_target_pairs={{0,28},{4,0},{8,4},{12,8},{16,12},{20,16},{24,20},{28,24},{1,29},{... | collective-permute-start | bytes 393224 | tf_op jit(solution)/shard_map/ppermute | solution.py:199
  65.1 11.4 %copy-start.3 = (f32[64]{0:T(128)S(1)}, f32[64]{0:T(128)}, u32[]{:S(2)}) copy-start(f32[64]{0:T(128)} %param.14) | copy-start | bytes 772
  65.1 11.7 %copy-start = (f32[256,256]{1,0:T(8,128)S(1)}, f32[256,256]{1,0:T(8,128)}, u32[]{:S(2)}) copy-start(f32[256,256]{1,0:T(8,128)} %refs_9_.1) | copy-start | bytes 786436
  73.4 8.0 %collective-permute-start.10 = (s16[272,256]{1,0:T(8,128)(2,1)S(1)}, s16[272,256]{1,0:T(8,128)(2,1)S(1)}, u32[]{:S(2)}, u32[]{:S(2)}) collective-permute-start(s16[272,256]{1,0:T(8,128)(2,1)S(1)} %shard_map.97), channel_id=1, source_target_pairs={{0,1},{1,0},{2,3},{3,2},{4,5},{5,4},{6,7},{7,6},{8,9},{9,8},{10,11... | collective-permute-start | bytes 417800 | tf_op jit(solution)/shard_map/ppermute | solution.py:209
  76.8 4.7 %copy-start.1 = (bf16[256,256]{1,0:T(8,128)(2,1)S(1)}, bf16[256,256]{1,0:T(8,128)(2,1)}, u32[]{:S(2)}) copy-start(bf16[256,256]{1,0:T(8,128)(2,1)} %amps.1) | copy-start | bytes 393220
  76.8 4.7 %copy-start.4 = (f32[256]{0:T(256)S(1)}, f32[256]{0:T(256)}, u32[]{:S(2)}) copy-start(f32[256]{0:T(256)} %param.15) | copy-start | bytes 3076
Sparse Core Ops, SparseCore 0:
  15.8 54.7 all-gather.1

commit v7 on v6

--- a/solution.py
+++ b/solution.py
@@ -11,6 +11,7 @@
 FIXED_BITS = 15
 FIXED_MOST = 2.0**15 - 1
 EXPONENT_ROWS = 16
+NEAR = 1024
 
 
 def shift(n, by):
@@ -93,13 +94,15 @@
         at += depth
 
 
-def partner_kernel(gathered, *refs):
-    parts, out_ref, rows_v, acc, row_sems = refs[:9], *refs[9:]
+def partner_kernel(gathered, hole, *refs):
+    parts, out_ref, near_hole, rows_v, acc, row_sems, hole_sem = refs[:9], *refs[9:]
     size = acc.shape[0]
     copies = ladder_copies(gathered, 2 * size, parts, rows_v, row_sems, size)
     for mine in copies:
         for copy in mine:
             copy.start()
+    hole_copy = pltpu.make_async_copy(hole.at[:, pl.ds(0, near_hole.shape[1])], near_hole, hole_sem)
+    hole_copy.start()
     acc[...] = jnp.zeros_like(acc)
     add_ladder(copies, parts, rows_v, acc, size)
     largest = jnp.max(jnp.abs(acc[...]), axis=0, keepdims=True)
@@ -110,18 +113,24 @@
     rows = out_ref.shape[0] - size
     line = jnp.broadcast_to(exponent, (rows, exponent.shape[1]))
     out_ref[size:, :] = line.astype(jnp.int32).astype(jnp.int16)
-
-
-def own_kernel(gathered, hole, *refs):
+    hole_copy.wait()
+
+
+def own_kernel(gathered, hole, near_hole, *refs):
     parts, drive, out_ref = refs[:9], refs[9], refs[10]
     rows_v, amps_rows_v, hole_v, row_sems, amps_sems, hole_sems = refs[11:]
     n, size = gathered.shape[0], out_ref.shape[0]
-    group = n // len(hole_v)
+    near, width = near_hole.shape[1], hole_v[0].shape[1]
+    groups = [near_hole.at[:, pl.ds(at, width)] for at in range(0, near, width)] + list(hole_v)
+    per_group = width // size
     hole_copies = []
-    for g in range(len(hole_v)):
-        src = hole.at[:, pl.ds(g * group * size, group * size)]
-        mine = [pltpu.make_async_copy(src, hole_v[g], hole_sems.at[g])]
-        for r in range(g * group, (g + 1) * group):
+    for g in range(len(groups)):
+        at, mine = g * width, []
+        if at >= near:
+            i = (at - near) // width
+            src = hole.at[:, pl.ds(at, width)]
+            mine = [pltpu.make_async_copy(src, groups[g], hole_sems.at[i])]
+        for r in range(g * per_group, (g + 1) * per_group):
             src = gathered.at[r, pl.ds(size, size)]
             dst = amps_rows_v.at[pl.ds(r * size, size)]
             mine.append(pltpu.make_async_copy(src, dst, amps_sems.at[r]))
@@ -135,41 +144,64 @@
     for g, mine in enumerate(hole_copies):
         for copy in mine:
             copy.wait()
-        at = pl.ds(g * group * size, group * size)
-        out_ref[...] += jnp.dot(hole_v[g][...], amps_rows_v[at], preferred_element_type=F32)
-
-
-def products(kernel, gathered, hole, parts, drive):
+        at = pl.ds(g * width, width)
+        out_ref[...] += jnp.dot(groups[g][...], amps_rows_v[at], preferred_element_type=F32)
+
+
+def in_hbm(*arrays):
+    return [pltpu.with_memory_space_constraint(a, pltpu.HBM) for a in arrays]
+
+
+def partner_product(gathered, hole, parts):
     hbm = pl.BlockSpec(memory_space=pltpu.HBM)
     vmem = pl.BlockSpec(memory_space=pltpu.VMEM)
     n, _, cols = gathered.shape
-    size, groups = drive.shape[0], 4
-    with_hole = hole is not None
-    arrays = (gathered, hole) if with_hole else (gathered,)
-    in_hbm = [pltpu.with_memory_space_constraint(a, pltpu.HBM) for a in arrays]
-    in_vmem = (*parts, drive) if with_hole else parts
-    out = jax.ShapeDtypeStruct(drive.shape, F32)
-    scratch = [pltpu.VMEM((n * size, cols), BF16)]
-    if not with_hole:
-        out = jax.ShapeDtypeStruct((size + EXPONENT_ROWS, cols), jnp.int16)
-        scratch.append(pltpu.VMEM(drive.shape, F32))
-    sems = [pltpu.SemaphoreType.DMA((n,))]
-    if with_hole:
-        scratch.append(pltpu.VMEM((n * size, cols), BF16))
-        scratch.append([pltpu.VMEM((size, n * size // groups), BF16) for _ in range(groups)])
-        sems += [pltpu.SemaphoreType.DMA((n,)), pltpu.SemaphoreType.DMA((groups,))]
-    depth = (2 if with_hole else 1) * n * size
+    size = hole.shape[0]
     return pl.pallas_call(
-        kernel,
-        out_shape=out,
-        in_specs=[hbm] * len(in_hbm) + [vmem] * len(in_vmem),
-        out_specs=vmem,
-        scratch_shapes=scratch + sems,
+        partner_kernel,
+        out_shape=(
+            jax.ShapeDtypeStruct((size + EXPONENT_ROWS, cols), jnp.int16),
+            jax.ShapeDtypeStruct((size, NEAR), BF16),
+        ),
+        in_specs=[hbm] * 2 + [vmem] * len(parts),
+        out_specs=(vmem, vmem),
+        scratch_shapes=[
+            pltpu.VMEM((n * size, cols), BF16),
+            pltpu.VMEM((size, cols), F32),
+            pltpu.SemaphoreType.DMA((n,)),
+            pltpu.SemaphoreType.DMA,
+        ],
         compiler_params=pltpu.CompilerParams(vmem_limit_bytes=24 << 20),
         cost_estimate=pl.CostEstimate(
-            flops=2 * size * cols * depth, bytes_accessed=4 * size * depth, transcendentals=0
+            flops=2 * size * cols * n * size, bytes_accessed=4 * size * n * size, transcendentals=0
         ),
-    )(*in_hbm, *in_vmem)
+    )(*in_hbm(gathered, hole), *parts)
+
+
+def own_product(gathered, hole, near_hole, parts, drive):
+    hbm = pl.BlockSpec(memory_space=pltpu.HBM)
+    vmem = pl.BlockSpec(memory_space=pltpu.VMEM)
+    n, _, cols = gathered.shape
+    size, width = drive.shape[0], 1024
+    groups = (hole.shape[1] - near_hole.shape[1]) // width
+    return pl.pallas_call(
+        own_kernel,
+        out_shape=jax.ShapeDtypeStruct(drive.shape, F32),
+        in_specs=[hbm] * 2 + [vmem] * (2 + len(parts)),
+        out_specs=vmem,
+        scratch_shapes=[
+            pltpu.VMEM((n * size, cols), BF16),
+            pltpu.VMEM((n * size, cols), BF16),
+            [pltpu.VMEM((size, width), BF16) for _ in range(groups)],
+            pltpu.SemaphoreType.DMA((n,)),
+            pltpu.SemaphoreType.DMA((n,)),
+            pltpu.SemaphoreType.DMA((groups,)),
+        ],
+        compiler_params=pltpu.CompilerParams(vmem_limit_bytes=24 << 20),
+        cost_estimate=pl.CostEstimate(
+            flops=4 * size * cols * n * size, bytes_accessed=8 * size * n * size, transcendentals=0
+        ),
+    )(*in_hbm(gathered, hole), near_hole, *parts, drive)
 
 
 def body(amplitudes, drive, pair_irrep, occ_irrep, ladder_ints, hole_ints, occ_energy, pair_energy):
@@ -205,10 +237,10 @@
     pair_occ = (occ_energy[:, None] + occ_energy[None, :]).reshape(-1)
     own_energy = lax.dynamic_slice_in_dim(pair_occ, row_rank() * size, size)
     denominator = pair_energy[None, :] - own_energy[:, None]
-    for_partner = products(partner_kernel, gathered, None, parts, drive)
+    for_partner, near_hole = partner_product(gathered, hole_kept, parts)
     from_partner = lax.ppermute(for_partner, "x", partner)
     scale = jnp.exp2(from_partner[size : size + 1].astype(F32) - FIXED_BITS)
-    residual = products(own_kernel, gathered, hole_kept, parts, drive)
+    residual = own_product(gathered, hole_kept, near_hole, parts, drive)
     residual = residual + from_partner[:size].astype(F32) * scale
     updated = (amplitudes.astype(F32) - residual / denominator).astype(BF16)
     return residual, updated

time: 89.6 us -> 89.5 us (level)
  no operation moved by 1% of the time
where the time goes in v7:
time: 89.5 us; the launch traced here: 88.9 us
  starting transfers between devices  44.1 us (49%)
  between operations  14.3 us (16%)
  waiting for transfers between devices  13.3 us (15%)
  Pallas kernels  9.16 us (10%)
  other arithmetic  5.19 us (6%)
  local copies, waits for them, and re-layouts  2.95 us (3%)
    ppermute x3, starting transfers between devices, body(): b = lax.ppermute(b, 'z', shift(NZ, -1))  17.7 us
    ppermute x3, starting transfers between devices, body(): f = lax.ppermute(f, 'z', shift(NZ, 1))  8 us
    ppermute x3, waiting for transfers between devices, body(): f = lax.ppermute(f, 'z', shift(NZ, 1))  6.14 us
    all_gather x1, waiting for transfers between devices, body(): gathered = lax.all_gather(rows, ('y', 'core'), axis=0, tiled=False)  5.49 us
    ppermute x1, starting transfers between devices, body(): other = lax.ppermute(amplitudes, 'x', [(i, NX - 1 - i) for i in range(NX)])  4.74 us
    ppermute x1, starting transfers between devices, body(): parts.append(lax.ppermute(b[:, size:], 'z', shift(NZ, -1)))  4.57 us
    pallas_call x1, Pallas kernels, own_product(): pl.pallas_call(own_kernel, out_shape=jax.ShapeDtypeStruct(drive.shape, F3...  4.45 us
    ppermute x1, starting transfers between devices, body(): lent = lax.ppermute(lent, 'x', partner)  3.95 us
  transfers between devices with their start and end apart: 12, of which 5 were waited for; matrix products, arithmetic and copies ran while one was open for 6% of the time, Pallas kernels for 7%

profile of v7, /device:TPU:1, one launch (start us, length us, event | category | flops | bytes accessed | tf_op | source)
XLA Modules:
  0.0 88.9 jit_solution(9909155108770836279)
XLA Ops:
  7.2 0.0 copy-start.2
  7.2 0.0 all-gather.2.cloned.1.call-start
  7.2 0.9 %constant_dynamic-slice_fusion = bf16[256,256]{1,0:T(8,128)(2,1)S(1)} fusion(bf16[512,256]{1,0:T(8,128)(2,1)} %ladder.1, s32[]{:T(128)S(6)} %select_n.23), kind=kLoop, calls=%fused_computation.13 | loop fusion | bytes 262148 | tf_op jit(solution)/shard_map/dynamic_slice | solution.py:212
  8.2 3.9 %collective-permute-start = (bf16[256,256]{1,0:T(8,128)(2,1)S(1)}, bf16[256,256]{1,0:T(8,128)(2,1)S(1)}, u32[]{:S(2)}, u32[]{:S(2)}) collective-permute-start(bf16[256,256]{1,0:T(8,128)(2,1)S(1)} %constant_dynamic-slice_fusion), channel_id=1, source_target_pairs={{0,1},{1,0},{2,3},{3,2},{4,5},{5,4},{6,7},{7,6},{8,9},{9,8},{10,11... | collective-permute-start | bytes 393224 | tf_op jit(solution)/shard_map/ppermute | solution.py:213
  12.1 1.9 %shard_map.95 = bf16[768,256]{1,0:T(8,128)(2,1)} custom-call(s32[64,128]{1,0:T(8,128)} %bitcast.8, bf16[512,256]{1,0:T(8,128)(2,1)} %ladder.1, bf16[256,256]{1,0:T(8,128)(2,1)} %amps.1), custom_call_target="tpu_custom_call" | custom-call | bytes 1048576 | tf_op jit(solution)/shard_map/pallas_call | solution.py:59
  14.0 0.8 fusion.5
  14.9 0.0 collective-permute-done
  14.9 0.8 fusion.1
  15.6 0.0 all-gather.2.cloned.1.call-update
  15.7 4.7 %collective-permute-start.1 = (bf16[256,256]{1,0:T(8,128)(2,1)}, bf16[256,256]{1,0:T(8,128)(2,1)S(1)}, u32[]{:S(2)}, u32[]{:S(2)}) collective-permute-start(bf16[256,256]{1,0:T(8,128)(2,1)} %amps.1), channel_id=1, source_target_pairs={{0,3},{1,2},{2,1},{3,0},{4,7},{5,6},{6,5},{7,4},{8,11},{9,10},{10,... | collective-permute-start | bytes 393224 | tf_op jit(solution)/shard_map/ppermute | solution.py:222
  20.4 0.9 %constant_dynamic-update-slice_fusion.1 = bf16[256,512]{1,0:T(8,128)(2,1)S(1)} fusion(bf16[256,256]{1,0:T(8,128)(2,1)} %amps.1), kind=kLoop, calls=%fused_computation.8 | loop fusion | bytes 262144
  21.3 1.6 %collective-permute-done.1 = bf16[256,256]{1,0:T(8,128)(2,1)S(1)} collective-permute-done((bf16[256,256]{1,0:T(8,128)(2,1)}, bf16[256,256]{1,0:T(8,128)(2,1)S(1)}, u32[]{:S(2)}, u32[]{:S(2)}) %collective-permute-start.1) | collective-permute-done | bytes 131104 | tf_op jit(solution)/shard_map/ppermute | solution.py:222
  23.0 4.2 %collective-permute-start.2 = (bf16[256,512]{1,0:T(8,128)(2,1)S(1)}, bf16[256,512]{1,0:T(8,128)(2,1)S(1)}, u32[]{:S(2)}, u32[]{:S(2)}) collective-permute-start(bf16[256,512]{1,0:T(8,128)(2,1)S(1)} %constant_dynamic-update-slice_fusion.refs_0_), channel_id=1, source_target_pairs={{0,4},{4,8},{8,12},{12,16},{16,20},{20,24},{24,28},{28,0},{1,5},{5... | collective-permute-start | bytes 786440 | tf_op jit(solution)/shard_map/ppermute | solution.py:227
  27.2 8.6 %collective-permute-start.3 = (bf16[256,512]{1,0:T(8,128)(2,1)S(1)}, bf16[256,512]{1,0:T(8,128)(2,1)S(1)}, u32[]{:S(2)}, u32[]{:S(2)}) collective-permute-start(bf16[256,512]{1,0:T(8,128)(2,1)S(1)} %constant_dynamic-update-slice_fusion.refs_0_), channel_id=1, source_target_pairs={{0,28},{4,0},{8,4},{12,8},{16,12},{20,16},{24,20},{28,24},{1,29},{... | collective-permute-start | bytes 786440 | tf_op jit(solution)/shard_map/ppermute | solution.py:228
  35.8 1.8 %collective-permute-done.2.refs_1_ = bf16[256,512]{1,0:T(8,128)(2,1)S(1)} collective-permute-done((bf16[256,512]{1,0:T(8,128)(2,1)S(1)}, bf16[256,512]{1,0:T(8,128)(2,1)S(1)}, u32[]{:S(2)}, u32[]{:S(2)}) %collective-permute-start.2) | collective-permute-done | bytes 262176 | tf_op jit(solution)/shard_map/ppermute | solution.py:227
  37.6 1.9 %collective-permute-start.4 = (bf16[256,512]{1,0:T(8,128)(2,1)S(1)}, bf16[256,512]{1,0:T(8,128)(2,1)S(1)}, u32[]{:S(2)}, u32[]{:S(2)}) collective-permute-start(bf16[256,512]{1,0:T(8,128)(2,1)S(1)} %collective-permute-done.2.refs_1_), channel_id=1, source_target_pairs={{0,4},{4,8},{8,12},{12,16},{16,20},{20,24},{24,28},{28,0},{1,5},{5... | collective-permute-start | bytes 786440 | tf_op jit(solution)/shard_map/ppermute | solution.py:227
  39.5 0.0 collective-permute-done.3.refs_2_
  39.5 4.6 %collective-permute-start.5 = (bf16[256,512]{1,0:T(8,128)(2,1)S(1)}, bf16[256,512]{1,0:T(8,128)(2,1)S(1)}, u32[]{:S(2)}, u32[]{:S(2)}) collective-permute-start(bf16[256,512]{1,0:T(8,128)(2,1)S(1)} %collective-permute-done.3.refs_2_), channel_id=1, source_target_pairs={{0,28},{4,0},{8,4},{12,8},{16,12},{20,16},{24,20},{28,24},{1,29},{... | collective-permute-start | bytes 786440 | tf_op jit(solution)/shard_map/ppermute | solution.py:228
  44.1 2.2 %collective-permute-done.4.refs_3_ = bf16[256,512]{1,0:T(8,128)(2,1)S(1)} collective-permute-done((bf16[256,512]{1,0:T(8,128)(2,1)S(1)}, bf16[256,512]{1,0:T(8,128)(2,1)S(1)}, u32[]{:S(2)}, u32[]{:S(2)}) %collective-permute-start.4) | collective-permute-done | bytes 262176 | tf_op jit(solution)/shard_map/ppermute | solution.py:227
  46.3 1.9 %collective-permute-start.6 = (bf16[256,512]{1,0:T(8,128)(2,1)S(1)}, bf16[256,512]{1,0:T(8,128)(2,1)S(1)}, u32[]{:S(2)}, u32[]{:S(2)}) collective-permute-start(bf16[256,512]{1,0:T(8,128)(2,1)S(1)} %collective-permute-done.4.refs_3_), channel_id=1, source_target_pairs={{0,4},{4,8},{8,12},{12,16},{16,20},{20,24},{24,28},{28,0},{1,5},{5... | collective-permute-start | bytes 786440 | tf_op jit(solution)/shard_map/ppermute | solution.py:227
  48.2 0.0 collective-permute-done.5.refs_4_
  48.2 4.6 %collective-permute-start.7 = (bf16[256,512]{1,0:T(8,128)(2,1)S(1)}, bf16[256,512]{1,0:T(8,128)(2,1)S(1)}, u32[]{:S(2)}, u32[]{:S(2)}) collective-permute-start(bf16[256,512]{1,0:T(8,128)(2,1)S(1)} %collective-permute-done.5.refs_4_), channel_id=1, source_target_pairs={{0,28},{4,0},{8,4},{12,8},{16,12},{20,16},{24,20},{28,24},{1,29},{... | collective-permute-start | bytes 786440 | tf_op jit(solution)/shard_map/ppermute | solution.py:228
  52.8 0.0 copy-done.2
  52.8 0.1 dynamic_slice.18
  52.9 2.1 %collective-permute-done.6.refs_5_ = bf16[256,512]{1,0:T(8,128)(2,1)S(1)} collective-permute-done((bf16[256,512]{1,0:T(8,128)(2,1)S(1)}, bf16[256,512]{1,0:T(8,128)(2,1)S(1)}, u32[]{:S(2)}, u32[]{:S(2)}) %collective-permute-start.6) | collective-permute-done | bytes 262176 | tf_op jit(solution)/shard_map/ppermute | solution.py:227
  55.0 1.9 %collective-permute-start.8 = (bf16[256,256]{1,0:T(8,128)(2,1)S(1)}, bf16[256,256]{1,0:T(8,128)(2,1)S(1)}, u32[]{:S(2)}, u32[]{:S(2)}) collective-permute-start(bf16[256,256]{1,0:T(8,128)(2,1)S(1)} %slice.16), channel_id=1, source_target_pairs={{0,4},{4,8},{8,12},{12,16},{16,20},{20,24},{24,28},{28,0},{1,5},{5... | collective-permute-start | bytes 393224 | tf_op jit(solution)/shard_map/ppermute | solution.py:230
  57.0 0.0 collective-permute-done.7.refs_6_
  57.0 4.6 %collective-permute-start.9 = (bf16[256,256]{1,0:T(8,128)(2,1)S(1)}, bf16[256,256]{1,0:T(8,128)(2,1)S(1)}, u32[]{:S(2)}, u32[]{:S(2)}) collective-permute-start(bf16[256,256]{1,0:T(8,128)(2,1)S(1)} %slice.17), channel_id=1, source_target_pairs={{0,28},{4,0},{8,4},{12,8},{16,12},{20,16},{24,20},{28,24},{1,29},{... | collective-permute-start | bytes 393224 | tf_op jit(solution)/shard_map/ppermute | solution.py:231
  61.6 3.5 %compare_select_fusion.hole = bf16[256,4096]{1,0:T(8,128)(2,1)} fusion(bf16[256,4096]{1,0:T(8,128)(2,1)} %param.13, s32[4096]{0:T(1024)S(1)} %copy-done.2, s32[256]{0:T(256)S(1)} %dynamic_slice.18), kind=kLoop, calls=%fused_computation | loop fusion | flops 2097152 | bytes 4211712 | tf_op jit(solution)/shard_map/jit(_where)/select_n | solution.py:234
  65.1 0.0 copy-start.3
  65.1 0.0 copy-start
  65.1 0.0 collective-permute-done.8.refs_7_
  65.1 0.0 collective-permute-done.9.refs_8_
  65.1 5.5 %all-gather.2.cloned.1.call-done.gathered = bf16[16,768,256]{2,1,0:T(8,128)(2,1)} async-done(((bf16[1,768,256]{2,1,0:T(8,128)(2,1)}), bf16[16,768,256]{2,1,0:T(8,128)(2,1)}) %all-gather.2.cloned.1.call-update) | async-done | bytes 6291472 | tf_op jit(solution)/shard_map/all_gather | solution.py:220
  70.6 2.8 %shard_map.96 = (s16[272,256]{1,0:T(8,128)(2,1)S(1)}, bf16[256,1024]{1,0:T(8,128)(2,1)S(1)}) custom-call(bf16[16,768,256]{2,1,0:T(8,128)(2,1)} %all-gather.2.cloned.1.call-done.gathered, bf16[256,4096]{1,0:T(8,128)(2,1)} %compare_select_fusion.hole, bf16[256,512]{1,0:T(8,128)(2,1)S(1)} %constant_dynamic-update-slice_fusion.refs_0_, ...), custom_call_target="tpu_custom_call" | custom-call | flops 536870912 | bytes 4194304 | tf_op jit(solution)/shard_map/pallas_call | solution.py:160
  73.4 3.1 %collective-permute-start.10 = (s16[272,256]{1,0:T(8,128)(2,1)S(1)}, s16[272,256]{1,0:T(8,128)(2,1)S(1)}, u32[]{:S(2)}, u32[]{:S(2)}) collective-permute-start(s16[272,256]{1,0:T(8,128)(2,1)S(1)} %get-tuple-element.5), channel_id=1, source_target_pairs={{0,1},{1,0},{2,3},{3,2},{4,5},{5,4},{6,7},{7,6},{8,9},{9,8},{10,11... | collective-permute-start | bytes 417800 | tf_op jit(solution)/shard_map/ppermute | solution.py:241
  76.5 0.0 copy-done.3
  76.6 0.1 broadcast_add_fusion
  76.6 0.1 add.60
  76.7 0.1 dynamic_slice.19
  76.8 0.0 copy-done
  76.8 0.0 copy-start.1
  76.8 0.0 copy-start.4
  76.8 4.5 %shard_map.97 = f32[256,256]{1,0:T(8,128)S(1)} custom-call(bf16[16,768,256]{2,1,0:T(8,128)(2,1)} %all-gather.2.cloned.1.call-done.gathered, bf16[256,4096]{1,0:T(8,128)(2,1)} %compare_select_fusion.hole, bf16[256,1024]{1,0:T(8,128)(2,1)S(1)} %get-tuple-element.4.near_hole, bf16[256,512]{1,0:T(8,128)(2,1)S(1)} %constant_dynamic-update-slice_fusion.refs_0_, ...), custom_call_target="tpu_custom_call" | custom-call | flops 1073741824 | bytes 8388608 | tf_op jit(solution)/shard_map/pallas_call | solution.py:187
  81.2 0.0 collective-permute-done.10
  81.3 0.0 copy-done.1
  81.3 0.0 copy-done.4
  81.3 0.8 subtract_convert_fusion
  (4 shorter events, 0.0 us)
Async XLA Ops:
  7.2 45.7 %copy-start.2 = (s32[4096]{0:T(1024)S(1)}, s32[4096]{0:T(1024)}, u32[]{:S(2)}) copy-start(s32[4096]{0:T(1024)} %param.11) | copy-start | bytes 49156
  7.2 63.5 %all-gather.2.cloned.1.call-start = ((), (), s32[]{:S(2)}) async-start(), calls=%async_computation | async-start | bytes 6684672 | tf_op jit(solution)/shard_map/all_gather | solution.py:220
  8.2 6.7 %collective-permute-start = (bf16[256,256]{1,0:T(8,128)(2,1)S(1)}, bf16[256,256]{1,0:T(8,128)(2,1)S(1)}, u32[]{:S(2)}, u32[]{:S(2)}) collective-permute-start(bf16[256,256]{1,0:T(8,128)(2,1)S(1)} %constant_dynamic-slice_fusion), channel_id=1, source_target_pairs={{0,1},{1,0},{2,3},{3,2},{4,5},{5,4},{6,7},{7,6},{8,9},{9,8},{10,11... | collective-permute-start | bytes 393224 | tf_op jit(solution)/shard_map/ppermute | solution.py:213
  15.7 7.3 %collective-permute-start.1 = (bf16[256,256]{1,0:T(8,128)(2,1)}, bf16[256,256]{1,0:T(8,128)(2,1)S(1)}, u32[]{:S(2)}, u32[]{:S(2)}) collective-permute-start(bf16[256,256]{1,0:T(8,128)(2,1)} %amps.1), channel_id=1, source_target_pairs={{0,3},{1,2},{2,1},{3,0},{4,7},{5,6},{6,5},{7,4},{8,11},{9,10},{10,... | collective-permute-start | bytes 393224 | tf_op jit(solution)/shard_map/ppermute | solution.py:222
  23.0 14.6 %collective-permute-start.2 = (bf16[256,512]{1,0:T(8,128)(2,1)S(1)}, bf16[256,512]{1,0:T(8,128)(2,1)S(1)}, u32[]{:S(2)}, u32[]{:S(2)}) collective-permute-start(bf16[256,512]{1,0:T(8,128)(2,1)S(1)} %constant_dynamic-update-slice_fusion.refs_0_), channel_id=1, source_target_pairs={{0,4},{4,8},{8,12},{12,16},{16,20},{20,24},{24,28},{28,0},{1,5},{5... | collective-permute-start | bytes 786440 | tf_op jit(solution)/shard_map/ppermute | solution.py:227
  27.2 12.3 %collective-permute-start.3 = (bf16[256,512]{1,0:T(8,128)(2,1)S(1)}, bf16[256,512]{1,0:T(8,128)(2,1)S(1)}, u32[]{:S(2)}, u32[]{:S(2)}) collective-permute-start(bf16[256,512]{1,0:T(8,128)(2,1)S(1)} %constant_dynamic-update-slice_fusion.refs_0_), channel_id=1, source_target_pairs={{0,28},{4,0},{8,4},{12,8},{16,12},{20,16},{24,20},{28,24},{1,29},{... | collective-permute-start | bytes 786440 | tf_op jit(solution)/shard_map/ppermute | solution.py:228
  37.6 8.7 %collective-permute-start.4 = (bf16[256,512]{1,0:T(8,128)(2,1)S(1)}, bf16[256,512]{1,0:T(8,128)(2,1)S(1)}, u32[]{:S(2)}, u32[]{:S(2)}) collective-permute-start(bf16[256,512]{1,0:T(8,128)(2,1)S(1)} %collective-permute-done.2.refs_1_), channel_id=1, source_target_pairs={{0,4},{4,8},{8,12},{12,16},{16,20},{20,24},{24,28},{28,0},{1,5},{5... | collective-permute-start | bytes 786440 | tf_op jit(solution)/shard_map/ppermute | solution.py:227
  39.5 8.7 %collective-permute-start.5 = (bf16[256,512]{1,0:T(8,128)(2,1)S(1)}, bf16[256,512]{1,0:T(8,128)(2,1)S(1)}, u32[]{:S(2)}, u32[]{:S(2)}) collective-permute-start(bf16[256,512]{1,0:T(8,128)(2,1)S(1)} %collective-permute-done.3.refs_2_), channel_id=1, source_target_pairs={{0,28},{4,0},{8,4},{12,8},{16,12},{20,16},{24,20},{28,24},{1,29},{... | collective-permute-start | bytes 786440 | tf_op jit(solution)/shard_map/ppermute | solution.py:228
  46.3 8.7 %collective-permute-start.6 = (bf16[256,512]{1,0:T(8,128)(2,1)S(1)}, bf16[256,512]{1,0:T(8,128)(2,1)S(1)}, u32[]{:S(2)}, u32[]{:S(2)}) collective-permute-start(bf16[256,512]{1,0:T(8,128)(2,1)S(1)} %collective-permute-done.4.refs_3_), channel_id=1, source_target_pairs={{0,4},{4,8},{8,12},{12,16},{16,20},{20,24},{24,28},{28,0},{1,5},{5... | collective-permute-start | bytes 786440 | tf_op jit(solution)/shard_map/ppermute | solution.py:227
  48.2 8.7 %collective-permute-start.7 = (bf16[256,512]{1,0:T(8,128)(2,1)S(1)}, bf16[256,512]{1,0:T(8,128)(2,1)S(1)}, u32[]{:S(2)}, u32[]{:S(2)}) collective-permute-start(bf16[256,512]{1,0:T(8,128)(2,1)S(1)} %collective-permute-done.5.refs_4_), channel_id=1, source_target_pairs={{0,28},{4,0},{8,4},{12,8},{16,12},{20,16},{24,20},{28,24},{1,29},{... | collective-permute-start | bytes 786440 | tf_op jit(solution)/shard_map/ppermute | solution.py:228
  55.0 10.1 %collective-permute-start.8 = (bf16[256,256]{1,0:T(8,128)(2,1)S(1)}, bf16[256,256]{1,0:T(8,128)(2,1)S(1)}, u32[]{:S(2)}, u32[]{:S(2)}) collective-permute-start(bf16[256,256]{1,0:T(8,128)(2,1)S(1)} %slice.16), channel_id=1, source_target_pairs={{0,4},{4,8},{8,12},{12,16},{16,20},{20,24},{24,28},{28,0},{1,5},{5... | collective-permute-start | bytes 393224 | tf_op jit(solution)/shard_map/ppermute | solution.py:230
  57.0 8.1 %collective-permute-start.9 = (bf16[256,256]{1,0:T(8,128)(2,1)S(1)}, bf16[256,256]{1,0:T(8,128)(2,1)S(1)}, u32[]{:S(2)}, u32[]{:S(2)}) collective-permute-start(bf16[256,256]{1,0:T(8,128)(2,1)S(1)} %slice.17), channel_id=1, source_target_pairs={{0,28},{4,0},{8,4},{12,8},{16,12},{20,16},{24,20},{28,24},{1,29},{... | collective-permute-start | bytes 393224 | tf_op jit(solution)/shard_map/ppermute | solution.py:231
  65.1 11.4 %copy-start.3 = (f32[64]{0:T(128)S(1)}, f32[64]{0:T(128)}, u32[]{:S(2)}) copy-start(f32[64]{0:T(128)} %param.14) | copy-start | bytes 772
  65.1 11.7 %copy-start = (f32[256,256]{1,0:T(8,128)S(1)}, f32[256,256]{1,0:T(8,128)}, u32[]{:S(2)}) copy-start(f32[256,256]{1,0:T(8,128)} %refs_9_.1) | copy-start | bytes 786436
  73.4 7.8 %collective-permute-start.10 = (s16[272,256]{1,0:T(8,128)(2,1)S(1)}, s16[272,256]{1,0:T(8,128)(2,1)S(1)}, u32[]{:S(2)}, u32[]{:S(2)}) collective-permute-start(s16[272,256]{1,0:T(8,128)(2,1)S(1)} %get-tuple-element.5), channel_id=1, source_target_pairs={{0,1},{1,0},{2,3},{3,2},{4,5},{5,4},{6,7},{7,6},{8,9},{9,8},{10,11... | collective-permute-start | bytes 417800 | tf_op jit(solution)/shard_map/ppermute | solution.py:241
  76.8 4.5 %copy-start.1 = (bf16[256,256]{1,0:T(8,128)(2,1)S(1)}, bf16[256,256]{1,0:T(8,128)(2,1)}, u32[]{:S(2)}) copy-start(bf16[256,256]{1,0:T(8,128)(2,1)} %amps.1) | copy-start | bytes 393220
  76.8 4.5 %copy-start.4 = (f32[256]{0:T(256)S(1)}, f32[256]{0:T(256)}, u32[]{:S(2)}) copy-start(f32[256]{0:T(256)} %param.15) | copy-start | bytes 3076
Sparse Core Ops, SparseCore 0:
  15.8 54.7 all-gather.1

commit v8 on v7

--- a/solution.py
+++ b/solution.py
@@ -96,23 +96,42 @@
 
 def partner_kernel(gathered, hole, *refs):
     parts, out_ref, near_hole, rows_v, acc, row_sems, hole_sem = refs[:9], *refs[9:]
-    size = acc.shape[0]
-    copies = ladder_copies(gathered, 2 * size, parts, rows_v, row_sems, size)
-    for mine in copies:
-        for copy in mine:
-            copy.start()
+    size, cols = acc.shape
+    z = lax.axis_index("z")
+    upper = (lax.axis_index("x") >= NX // 2).astype(jnp.int32)
+    halves = 1
+    copies = []
+    for h in range(halves):
+        for i, away in enumerate((0, -1, 1, -2, 2, -3, 3, NZ // 2)):
+            slot = lax.rem(z + NZ + away, NZ)
+            src = gathered.at[pl.ds(2 * slot, 2), pl.ds(2 * size, size), pl.ds(h * cols, cols)]
+            copies.append(pltpu.make_async_copy(src, rows_v.at[h, i], row_sems.at[h * NZ + i]))
+            copies[-1].start()
     hole_copy = pltpu.make_async_copy(hole.at[:, pl.ds(0, near_hole.shape[1])], near_hole, hole_sem)
     hole_copy.start()
-    acc[...] = jnp.zeros_like(acc)
-    add_ladder(copies, parts, rows_v, acc, size)
-    largest = jnp.max(jnp.abs(acc[...]), axis=0, keepdims=True)
-    exponent = jnp.ceil(jnp.log2(jnp.maximum(largest, 2.0**-100)))
-    fixed = jnp.round(acc[...] * jnp.exp2(FIXED_BITS - exponent))
-    fixed = jnp.clip(fixed, -FIXED_MOST, FIXED_MOST)
-    out_ref[:size, :] = fixed.astype(jnp.int32).astype(jnp.int16)
-    rows = out_ref.shape[0] - size
-    line = jnp.broadcast_to(exponent, (rows, exponent.shape[1]))
-    out_ref[size:, :] = line.astype(jnp.int32).astype(jnp.int16)
+    blocks = [(p, i, p, i) for p in range(NZ - 1) for i in range(2)]
+    blocks += [(NZ - 1, 0, NZ - 1, 0), (NZ, 0, NZ - 1, 1)]
+    extra = out_ref.shape[0] - size
+    for h in range(halves):
+        lanes = slice(h * cols, (h + 1) * cols)
+        acc[:, lanes] = jnp.zeros((size, cols), F32)
+        for p, i, chunk, j in blocks:
+            if j == 0:
+                copies[h * NZ + chunk].wait()
+            row = upper if j == 0 else 1 - upper
+            acc[:, lanes] += jnp.dot(
+                parts[p][:, i * size : (i + 1) * size],
+                rows_v[h, chunk, row],
+                preferred_element_type=F32,
+            )
+        sums = acc[:, lanes]
+        largest = jnp.max(jnp.abs(sums), axis=0, keepdims=True)
+        exponent = jnp.ceil(jnp.log2(jnp.maximum(largest, 2.0**-100)))
+        fixed = jnp.round(sums * jnp.exp2(FIXED_BITS - exponent))
+        fixed = jnp.clip(fixed, -FIXED_MOST, FIXED_MOST)
+        out_ref[:size, lanes] = fixed.astype(jnp.int32).astype(jnp.int16)
+        line = jnp.broadcast_to(exponent, (extra, cols))
+        out_ref[size:, lanes] = line.astype(jnp.int32).astype(jnp.int16)
     hole_copy.wait()
 
 
@@ -166,9 +185,9 @@
         in_specs=[hbm] * 2 + [vmem] * len(parts),
         out_specs=(vmem, vmem),
         scratch_shapes=[
-            pltpu.VMEM((n * size, cols), BF16),
+            pltpu.VMEM((1, NZ, 2, size, cols), BF16),
             pltpu.VMEM((size, cols), F32),
-            pltpu.SemaphoreType.DMA((n,)),
+            pltpu.SemaphoreType.DMA((NZ,)),
             pltpu.SemaphoreType.DMA,
         ],
         compiler_params=pltpu.CompilerParams(vmem_limit_bytes=24 << 20),

time: 89.5 us -> 89.4 us (level)
  no operation moved by 1% of the time
where the time goes in v8:
time: 89.4 us; the launch traced here: 88.8 us
  starting transfers between devices  44.1 us (49%)
  between operations  14.3 us (16%)
  waiting for transfers between devices  13.3 us (15%)
  Pallas kernels  9.03 us (10%)
  other arithmetic  5.19 us (6%)
  local copies, waits for them, and re-layouts  2.95 us (3%)
    ppermute x3, starting transfers between devices, body(): b = lax.ppermute(b, 'z', shift(NZ, -1))  17.7 us
    ppermute x3, starting transfers between devices, body(): f = lax.ppermute(f, 'z', shift(NZ, 1))  8 us
    ppermute x3, waiting for transfers between devices, body(): f = lax.ppermute(f, 'z', shift(NZ, 1))  6.14 us
    all_gather x1, waiting for transfers between devices, body(): gathered = lax.all_gather(rows, ('y', 'core'), axis=0, tiled=False)  5.49 us
    ppermute x1, starting transfers between devices, body(): other = lax.ppermute(amplitudes, 'x', [(i, NX - 1 - i) for i in range(NX)])  4.74 us
    ppermute x1, starting transfers between devices, body(): parts.append(lax.ppermute(b[:, size:], 'z', shift(NZ, -1)))  4.57 us
    pallas_call x1, Pallas kernels, own_product(): pl.pallas_call(own_kernel, out_shape=jax.ShapeDtypeStruct(drive.shape, F3...  4.45 us
    ppermute x1, starting transfers between devices, body(): lent = lax.ppermute(lent, 'x', partner)  3.95 us
  transfers between devices with their start and end apart: 12, of which 5 were waited for; matrix products, arithmetic and copies ran while one was open for 6% of the time, Pallas kernels for 7%

profile of v8, /device:TPU:1, one launch (start us, length us, event | category | flops | bytes accessed | tf_op | source)
XLA Modules:
  0.0 88.8 jit_solution(12158490223746866767)
XLA Ops:
  7.2 0.0 copy-start.2
  7.2 0.0 all-gather.2.cloned.1.call-start
  7.2 0.9 %constant_dynamic-slice_fusion = bf16[256,256]{1,0:T(8,128)(2,1)S(1)} fusion(bf16[512,256]{1,0:T(8,128)(2,1)} %ladder.1, s32[]{:T(128)S(6)} %select_n.23), kind=kLoop, calls=%fused_computation.13 | loop fusion | bytes 262148 | tf_op jit(solution)/shard_map/dynamic_slice | solution.py:231
  8.2 3.9 %collective-permute-start = (bf16[256,256]{1,0:T(8,128)(2,1)S(1)}, bf16[256,256]{1,0:T(8,128)(2,1)S(1)}, u32[]{:S(2)}, u32[]{:S(2)}) collective-permute-start(bf16[256,256]{1,0:T(8,128)(2,1)S(1)} %constant_dynamic-slice_fusion), channel_id=1, source_target_pairs={{0,1},{1,0},{2,3},{3,2},{4,5},{5,4},{6,7},{7,6},{8,9},{9,8},{10,11... | collective-permute-start | bytes 393224 | tf_op jit(solution)/shard_map/ppermute | solution.py:232
  12.1 1.9 %shard_map.95 = bf16[768,256]{1,0:T(8,128)(2,1)} custom-call(s32[64,128]{1,0:T(8,128)} %bitcast.8, bf16[512,256]{1,0:T(8,128)(2,1)} %ladder.1, bf16[256,256]{1,0:T(8,128)(2,1)} %amps.1), custom_call_target="tpu_custom_call" | custom-call | bytes 1048576 | tf_op jit(solution)/shard_map/pallas_call | solution.py:59
  14.0 0.8 fusion.5
  14.9 0.0 collective-permute-done
  14.9 0.8 fusion.1
  15.6 0.0 all-gather.2.cloned.1.call-update
  15.7 4.7 %collective-permute-start.1 = (bf16[256,256]{1,0:T(8,128)(2,1)}, bf16[256,256]{1,0:T(8,128)(2,1)S(1)}, u32[]{:S(2)}, u32[]{:S(2)}) collective-permute-start(bf16[256,256]{1,0:T(8,128)(2,1)} %amps.1), channel_id=1, source_target_pairs={{0,3},{1,2},{2,1},{3,0},{4,7},{5,6},{6,5},{7,4},{8,11},{9,10},{10,... | collective-permute-start | bytes 393224 | tf_op jit(solution)/shard_map/ppermute | solution.py:241
  20.4 0.9 %constant_dynamic-update-slice_fusion.1 = bf16[256,512]{1,0:T(8,128)(2,1)S(1)} fusion(bf16[256,256]{1,0:T(8,128)(2,1)} %amps.1), kind=kLoop, calls=%fused_computation.8 | loop fusion | bytes 262144
  21.3 1.6 %collective-permute-done.1 = bf16[256,256]{1,0:T(8,128)(2,1)S(1)} collective-permute-done((bf16[256,256]{1,0:T(8,128)(2,1)}, bf16[256,256]{1,0:T(8,128)(2,1)S(1)}, u32[]{:S(2)}, u32[]{:S(2)}) %collective-permute-start.1) | collective-permute-done | bytes 131104 | tf_op jit(solution)/shard_map/ppermute | solution.py:241
  23.0 4.2 %collective-permute-start.2 = (bf16[256,512]{1,0:T(8,128)(2,1)S(1)}, bf16[256,512]{1,0:T(8,128)(2,1)S(1)}, u32[]{:S(2)}, u32[]{:S(2)}) collective-permute-start(bf16[256,512]{1,0:T(8,128)(2,1)S(1)} %constant_dynamic-update-slice_fusion.refs_0_), channel_id=1, source_target_pairs={{0,4},{4,8},{8,12},{12,16},{16,20},{20,24},{24,28},{28,0},{1,5},{5... | collective-permute-start | bytes 786440 | tf_op jit(solution)/shard_map/ppermute | solution.py:246
  27.2 8.6 %collective-permute-start.3 = (bf16[256,512]{1,0:T(8,128)(2,1)S(1)}, bf16[256,512]{1,0:T(8,128)(2,1)S(1)}, u32[]{:S(2)}, u32[]{:S(2)}) collective-permute-start(bf16[256,512]{1,0:T(8,128)(2,1)S(1)} %constant_dynamic-update-slice_fusion.refs_0_), channel_id=1, source_target_pairs={{0,28},{4,0},{8,4},{12,8},{16,12},{20,16},{24,20},{28,24},{1,29},{... | collective-permute-start | bytes 786440 | tf_op jit(solution)/shard_map/ppermute | solution.py:247
  35.8 1.8 %collective-permute-done.2.refs_1_ = bf16[256,512]{1,0:T(8,128)(2,1)S(1)} collective-permute-done((bf16[256,512]{1,0:T(8,128)(2,1)S(1)}, bf16[256,512]{1,0:T(8,128)(2,1)S(1)}, u32[]{:S(2)}, u32[]{:S(2)}) %collective-permute-start.2) | collective-permute-done | bytes 262176 | tf_op jit(solution)/shard_map/ppermute | solution.py:246
  37.6 1.9 %collective-permute-start.4 = (bf16[256,512]{1,0:T(8,128)(2,1)S(1)}, bf16[256,512]{1,0:T(8,128)(2,1)S(1)}, u32[]{:S(2)}, u32[]{:S(2)}) collective-permute-start(bf16[256,512]{1,0:T(8,128)(2,1)S(1)} %collective-permute-done.2.refs_1_), channel_id=1, source_target_pairs={{0,4},{4,8},{8,12},{12,16},{16,20},{20,24},{24,28},{28,0},{1,5},{5... | collective-permute-start | bytes 786440 | tf_op jit(solution)/shard_map/ppermute | solution.py:246
  39.5 0.0 collective-permute-done.3.refs_2_
  39.5 4.6 %collective-permute-start.5 = (bf16[256,512]{1,0:T(8,128)(2,1)S(1)}, bf16[256,512]{1,0:T(8,128)(2,1)S(1)}, u32[]{:S(2)}, u32[]{:S(2)}) collective-permute-start(bf16[256,512]{1,0:T(8,128)(2,1)S(1)} %collective-permute-done.3.refs_2_), channel_id=1, source_target_pairs={{0,28},{4,0},{8,4},{12,8},{16,12},{20,16},{24,20},{28,24},{1,29},{... | collective-permute-start | bytes 786440 | tf_op jit(solution)/shard_map/ppermute | solution.py:247
  44.1 2.2 %collective-permute-done.4.refs_3_ = bf16[256,512]{1,0:T(8,128)(2,1)S(1)} collective-permute-done((bf16[256,512]{1,0:T(8,128)(2,1)S(1)}, bf16[256,512]{1,0:T(8,128)(2,1)S(1)}, u32[]{:S(2)}, u32[]{:S(2)}) %collective-permute-start.4) | collective-permute-done | bytes 262176 | tf_op jit(solution)/shard_map/ppermute | solution.py:246
  46.3 1.9 %collective-permute-start.6 = (bf16[256,512]{1,0:T(8,128)(2,1)S(1)}, bf16[256,512]{1,0:T(8,128)(2,1)S(1)}, u32[]{:S(2)}, u32[]{:S(2)}) collective-permute-start(bf16[256,512]{1,0:T(8,128)(2,1)S(1)} %collective-permute-done.4.refs_3_), channel_id=1, source_target_pairs={{0,4},{4,8},{8,12},{12,16},{16,20},{20,24},{24,28},{28,0},{1,5},{5... | collective-permute-start | bytes 786440 | tf_op jit(solution)/shard_map/ppermute | solution.py:246
  48.2 0.0 collective-permute-done.5.refs_4_
  48.2 4.6 %collective-permute-start.7 = (bf16[256,512]{1,0:T(8,128)(2,1)S(1)}, bf16[256,512]{1,0:T(8,128)(2,1)S(1)}, u32[]{:S(2)}, u32[]{:S(2)}) collective-permute-start(bf16[256,512]{1,0:T(8,128)(2,1)S(1)} %collective-permute-done.5.refs_4_), channel_id=1, source_target_pairs={{0,28},{4,0},{8,4},{12,8},{16,12},{20,16},{24,20},{28,24},{1,29},{... | collective-permute-start | bytes 786440 | tf_op jit(solution)/shard_map/ppermute | solution.py:247
  52.8 0.0 copy-done.2
  52.8 0.1 dynamic_slice.18
  52.9 2.1 %collective-permute-done.6.refs_5_ = bf16[256,512]{1,0:T(8,128)(2,1)S(1)} collective-permute-done((bf16[256,512]{1,0:T(8,128)(2,1)S(1)}, bf16[256,512]{1,0:T(8,128)(2,1)S(1)}, u32[]{:S(2)}, u32[]{:S(2)}) %collective-permute-start.6) | collective-permute-done | bytes 262176 | tf_op jit(solution)/shard_map/ppermute | solution.py:246
  55.0 1.9 %collective-permute-start.8 = (bf16[256,256]{1,0:T(8,128)(2,1)S(1)}, bf16[256,256]{1,0:T(8,128)(2,1)S(1)}, u32[]{:S(2)}, u32[]{:S(2)}) collective-permute-start(bf16[256,256]{1,0:T(8,128)(2,1)S(1)} %slice.16), channel_id=1, source_target_pairs={{0,4},{4,8},{8,12},{12,16},{16,20},{20,24},{24,28},{28,0},{1,5},{5... | collective-permute-start | bytes 393224 | tf_op jit(solution)/shard_map/ppermute | solution.py:249
  57.0 0.0 collective-permute-done.7.refs_6_
  57.0 4.6 %collective-permute-start.9 = (bf16[256,256]{1,0:T(8,128)(2,1)S(1)}, bf16[256,256]{1,0:T(8,128)(2,1)S(1)}, u32[]{:S(2)}, u32[]{:S(2)}) collective-permute-start(bf16[256,256]{1,0:T(8,128)(2,1)S(1)} %slice.17), channel_id=1, source_target_pairs={{0,28},{4,0},{8,4},{12,8},{16,12},{20,16},{24,20},{28,24},{1,29},{... | collective-permute-start | bytes 393224 | tf_op jit(solution)/shard_map/ppermute | solution.py:250
  61.6 3.5 %compare_select_fusion.hole = bf16[256,4096]{1,0:T(8,128)(2,1)} fusion(bf16[256,4096]{1,0:T(8,128)(2,1)} %param.13, s32[4096]{0:T(1024)S(1)} %copy-done.2, s32[256]{0:T(256)S(1)} %dynamic_slice.18), kind=kLoop, calls=%fused_computation | loop fusion | flops 2097152 | bytes 4211712 | tf_op jit(solution)/shard_map/jit(_where)/select_n | solution.py:253
  65.1 0.0 copy-start.3
  65.1 0.0 copy-start
  65.1 0.0 collective-permute-done.8.refs_7_
  65.1 0.0 collective-permute-done.9.refs_8_
  65.1 5.5 %all-gather.2.cloned.1.call-done.gathered = bf16[16,768,256]{2,1,0:T(8,128)(2,1)} async-done(((bf16[1,768,256]{2,1,0:T(8,128)(2,1)}), bf16[16,768,256]{2,1,0:T(8,128)(2,1)}) %all-gather.2.cloned.1.call-update) | async-done | bytes 6291472 | tf_op jit(solution)/shard_map/all_gather | solution.py:239
  70.6 2.7 %shard_map.96 = (s16[272,256]{1,0:T(8,128)(2,1)S(1)}, bf16[256,1024]{1,0:T(8,128)(2,1)S(1)}) custom-call(bf16[16,768,256]{2,1,0:T(8,128)(2,1)} %all-gather.2.cloned.1.call-done.gathered, bf16[256,4096]{1,0:T(8,128)(2,1)} %compare_select_fusion.hole, bf16[256,512]{1,0:T(8,128)(2,1)S(1)} %constant_dynamic-update-slice_fusion.refs_0_, ...), custom_call_target="tpu_custom_call" | custom-call | flops 536870912 | bytes 4194304 | tf_op jit(solution)/shard_map/pallas_call | solution.py:179
  73.3 3.1 %collective-permute-start.10 = (s16[272,256]{1,0:T(8,128)(2,1)S(1)}, s16[272,256]{1,0:T(8,128)(2,1)S(1)}, u32[]{:S(2)}, u32[]{:S(2)}) collective-permute-start(s16[272,256]{1,0:T(8,128)(2,1)S(1)} %get-tuple-element.5), channel_id=1, source_target_pairs={{0,1},{1,0},{2,3},{3,2},{4,5},{5,4},{6,7},{7,6},{8,9},{9,8},{10,11... | collective-permute-start | bytes 417800 | tf_op jit(solution)/shard_map/ppermute | solution.py:260
  76.4 0.0 copy-done.3
  76.4 0.1 broadcast_add_fusion
  76.5 0.1 add.60
  76.6 0.1 dynamic_slice.19
  76.6 0.0 copy-done
  76.6 0.0 copy-start.1
  76.6 0.0 copy-start.4
  76.6 4.5 %shard_map.97 = f32[256,256]{1,0:T(8,128)S(1)} custom-call(bf16[16,768,256]{2,1,0:T(8,128)(2,1)} %all-gather.2.cloned.1.call-done.gathered, bf16[256,4096]{1,0:T(8,128)(2,1)} %compare_select_fusion.hole, bf16[256,1024]{1,0:T(8,128)(2,1)S(1)} %get-tuple-element.4.near_hole, bf16[256,512]{1,0:T(8,128)(2,1)S(1)} %constant_dynamic-update-slice_fusion.refs_0_, ...), custom_call_target="tpu_custom_call" | custom-call | flops 1073741824 | bytes 8388608 | tf_op jit(solution)/shard_map/pallas_call | solution.py:206
  81.1 0.0 collective-permute-done.10
  81.1 0.0 copy-done.1
  81.1 0.0 copy-done.4
  81.2 0.8 subtract_convert_fusion
  (4 shorter events, 0.0 us)
Async XLA Ops:
  7.2 45.7 %copy-start.2 = (s32[4096]{0:T(1024)S(1)}, s32[4096]{0:T(1024)}, u32[]{:S(2)}) copy-start(s32[4096]{0:T(1024)} %param.11) | copy-start | bytes 49156
  7.2 63.5 %all-gather.2.cloned.1.call-start = ((), (), s32[]{:S(2)}) async-start(), calls=%async_computation | async-start | bytes 6684672 | tf_op jit(solution)/shard_map/all_gather | solution.py:239
  8.2 6.7 %collective-permute-start = (bf16[256,256]{1,0:T(8,128)(2,1)S(1)}, bf16[256,256]{1,0:T(8,128)(2,1)S(1)}, u32[]{:S(2)}, u32[]{:S(2)}) collective-permute-start(bf16[256,256]{1,0:T(8,128)(2,1)S(1)} %constant_dynamic-slice_fusion), channel_id=1, source_target_pairs={{0,1},{1,0},{2,3},{3,2},{4,5},{5,4},{6,7},{7,6},{8,9},{9,8},{10,11... | collective-permute-start | bytes 393224 | tf_op jit(solution)/shard_map/ppermute | solution.py:232
  15.7 7.3 %collective-permute-start.1 = (bf16[256,256]{1,0:T(8,128)(2,1)}, bf16[256,256]{1,0:T(8,128)(2,1)S(1)}, u32[]{:S(2)}, u32[]{:S(2)}) collective-permute-start(bf16[256,256]{1,0:T(8,128)(2,1)} %amps.1), channel_id=1, source_target_pairs={{0,3},{1,2},{2,1},{3,0},{4,7},{5,6},{6,5},{7,4},{8,11},{9,10},{10,... | collective-permute-start | bytes 393224 | tf_op jit(solution)/shard_map/ppermute | solution.py:241
  23.0 14.6 %collective-permute-start.2 = (bf16[256,512]{1,0:T(8,128)(2,1)S(1)}, bf16[256,512]{1,0:T(8,128)(2,1)S(1)}, u32[]{:S(2)}, u32[]{:S(2)}) collective-permute-start(bf16[256,512]{1,0:T(8,128)(2,1)S(1)} %constant_dynamic-update-slice_fusion.refs_0_), channel_id=1, source_target_pairs={{0,4},{4,8},{8,12},{12,16},{16,20},{20,24},{24,28},{28,0},{1,5},{5... | collective-permute-start | bytes 786440 | tf_op jit(solution)/shard_map/ppermute | solution.py:246
  27.2 12.3 %collective-permute-start.3 = (bf16[256,512]{1,0:T(8,128)(2,1)S(1)}, bf16[256,512]{1,0:T(8,128)(2,1)S(1)}, u32[]{:S(2)}, u32[]{:S(2)}) collective-permute-start(bf16[256,512]{1,0:T(8,128)(2,1)S(1)} %constant_dynamic-update-slice_fusion.refs_0_), channel_id=1, source_target_pairs={{0,28},{4,0},{8,4},{12,8},{16,12},{20,16},{24,20},{28,24},{1,29},{... | collective-permute-start | bytes 786440 | tf_op jit(solution)/shard_map/ppermute | solution.py:247
  37.6 8.7 %collective-permute-start.4 = (bf16[256,512]{1,0:T(8,128)(2,1)S(1)}, bf16[256,512]{1,0:T(8,128)(2,1)S(1)}, u32[]{:S(2)}, u32[]{:S(2)}) collective-permute-start(bf16[256,512]{1,0:T(8,128)(2,1)S(1)} %collective-permute-done.2.refs_1_), channel_id=1, source_target_pairs={{0,4},{4,8},{8,12},{12,16},{16,20},{20,24},{24,28},{28,0},{1,5},{5... | collective-permute-start | bytes 786440 | tf_op jit(solution)/shard_map/ppermute | solution.py:246
  39.5 8.7 %collective-permute-start.5 = (bf16[256,512]{1,0:T(8,128)(2,1)S(1)}, bf16[256,512]{1,0:T(8,128)(2,1)S(1)}, u32[]{:S(2)}, u32[]{:S(2)}) collective-permute-start(bf16[256,512]{1,0:T(8,128)(2,1)S(1)} %collective-permute-done.3.refs_2_), channel_id=1, source_target_pairs={{0,28},{4,0},{8,4},{12,8},{16,12},{20,16},{24,20},{28,24},{1,29},{... | collective-permute-start | bytes 786440 | tf_op jit(solution)/shard_map/ppermute | solution.py:247
  46.3 8.7 %collective-permute-start.6 = (bf16[256,512]{1,0:T(8,128)(2,1)S(1)}, bf16[256,512]{1,0:T(8,128)(2,1)S(1)}, u32[]{:S(2)}, u32[]{:S(2)}) collective-permute-start(bf16[256,512]{1,0:T(8,128)(2,1)S(1)} %collective-permute-done.4.refs_3_), channel_id=1, source_target_pairs={{0,4},{4,8},{8,12},{12,16},{16,20},{20,24},{24,28},{28,0},{1,5},{5... | collective-permute-start | bytes 786440 | tf_op jit(solution)/shard_map/ppermute | solution.py:246
  48.2 8.7 %collective-permute-start.7 = (bf16[256,512]{1,0:T(8,128)(2,1)S(1)}, bf16[256,512]{1,0:T(8,128)(2,1)S(1)}, u32[]{:S(2)}, u32[]{:S(2)}) collective-permute-start(bf16[256,512]{1,0:T(8,128)(2,1)S(1)} %collective-permute-done.5.refs_4_), channel_id=1, source_target_pairs={{0,28},{4,0},{8,4},{12,8},{16,12},{20,16},{24,20},{28,24},{1,29},{... | collective-permute-start | bytes 786440 | tf_op jit(solution)/shard_map/ppermute | solution.py:247
  55.0 10.1 %collective-permute-start.8 = (bf16[256,256]{1,0:T(8,128)(2,1)S(1)}, bf16[256,256]{1,0:T(8,128)(2,1)S(1)}, u32[]{:S(2)}, u32[]{:S(2)}) collective-permute-start(bf16[256,256]{1,0:T(8,128)(2,1)S(1)} %slice.16), channel_id=1, source_target_pairs={{0,4},{4,8},{8,12},{12,16},{16,20},{20,24},{24,28},{28,0},{1,5},{5... | collective-permute-start | bytes 393224 | tf_op jit(solution)/shard_map/ppermute | solution.py:249
  57.0 8.1 %collective-permute-start.9 = (bf16[256,256]{1,0:T(8,128)(2,1)S(1)}, bf16[256,256]{1,0:T(8,128)(2,1)S(1)}, u32[]{:S(2)}, u32[]{:S(2)}) collective-permute-start(bf16[256,256]{1,0:T(8,128)(2,1)S(1)} %slice.17), channel_id=1, source_target_pairs={{0,28},{4,0},{8,4},{12,8},{16,12},{20,16},{24,20},{28,24},{1,29},{... | collective-permute-start | bytes 393224 | tf_op jit(solution)/shard_map/ppermute | solution.py:250
  65.1 11.3 %copy-start.3 = (f32[64]{0:T(128)S(1)}, f32[64]{0:T(128)}, u32[]{:S(2)}) copy-start(f32[64]{0:T(128)} %param.14) | copy-start | bytes 772
  65.1 11.5 %copy-start = (f32[256,256]{1,0:T(8,128)S(1)}, f32[256,256]{1,0:T(8,128)}, u32[]{:S(2)}) copy-start(f32[256,256]{1,0:T(8,128)} %refs_9_.1) | copy-start | bytes 786436
  73.3 7.8 %collective-permute-start.10 = (s16[272,256]{1,0:T(8,128)(2,1)S(1)}, s16[272,256]{1,0:T(8,128)(2,1)S(1)}, u32[]{:S(2)}, u32[]{:S(2)}) collective-permute-start(s16[272,256]{1,0:T(8,128)(2,1)S(1)} %get-tuple-element.5), channel_id=1, source_target_pairs={{0,1},{1,0},{2,3},{3,2},{4,5},{5,4},{6,7},{7,6},{8,9},{9,8},{10,11... | collective-permute-start | bytes 417800 | tf_op jit(solution)/shard_map/ppermute | solution.py:260
  76.6 4.5 %copy-start.1 = (bf16[256,256]{1,0:T(8,128)(2,1)S(1)}, bf16[256,256]{1,0:T(8,128)(2,1)}, u32[]{:S(2)}) copy-start(bf16[256,256]{1,0:T(8,128)(2,1)} %amps.1) | copy-start | bytes 393220
  76.6 4.5 %copy-start.4 = (f32[256]{0:T(256)S(1)}, f32[256]{0:T(256)}, u32[]{:S(2)}) copy-start(f32[256]{0:T(256)} %param.15) | copy-start | bytes 3076
Sparse Core Ops, SparseCore 0:
  15.8 54.7 all-gather.1

commit v9 on v6

--- a/solution.py
+++ b/solution.py
@@ -202,8 +202,9 @@
     hole_kept = jnp.where(
         own_occ[:, None] == occ_irrep[None, :], hole_ints, jnp.zeros_like(hole_ints)
     )
-    pair_occ = (occ_energy[:, None] + occ_energy[None, :]).reshape(-1)
-    own_energy = lax.dynamic_slice_in_dim(pair_occ, row_rank() * size, size)
+    span = size // occ_energy.shape[0]
+    outer = lax.dynamic_slice_in_dim(occ_energy, row_rank() * span, span)
+    own_energy = (outer[:, None] + occ_energy[None, :]).reshape(-1)
     denominator = pair_energy[None, :] - own_energy[:, None]
     for_partner = products(partner_kernel, gathered, None, parts, drive)
     from_partner = lax.ppermute(for_partner, "x", partner)

time: 89.6 us -> 89.6 us (level)
  no operation moved by 1% of the time
where the time goes in v9:
time: 89.6 us; the launch traced here: 89 us
  starting transfers between devices  44.1 us (49%)
  between operations  14.3 us (16%)
  waiting for transfers between devices  13.2 us (15%)
  Pallas kernels  9.32 us (10%)
  other arithmetic  5.18 us (6%)
  local copies, waits for them, and re-layouts  2.96 us (3%)
    ppermute x3, starting transfers between devices, body(): b = lax.ppermute(b, 'z', shift(NZ, -1))  17.7 us
    ppermute x3, starting transfers between devices, body(): f = lax.ppermute(f, 'z', shift(NZ, 1))  8 us
    pallas_call x2, Pallas kernels, products(): pl.pallas_call(kernel, out_shape=out, in_specs=[hbm] * len(in_hbm) + [vme...  7.4 us
    ppermute x3, waiting for transfers between devices, body(): f = lax.ppermute(f, 'z', shift(NZ, 1))  6.14 us
    all_gather x1, waiting for transfers between devices, body(): gathered = lax.all_gather(rows, ('y', 'core'), axis=0, tiled=False)  5.42 us
    ppermute x1, starting transfers between devices, body(): other = lax.ppermute(amplitudes, 'x', [(i, NX - 1 - i) for i in range(NX)])  4.74 us
    ppermute x1, starting transfers between devices, body(): parts.append(lax.ppermute(b[:, size:], 'z', shift(NZ, -1)))  4.57 us
    ppermute x1, starting transfers between devices, body(): lent = lax.ppermute(lent, 'x', partner)  3.95 us
  transfers between devices with their start and end apart: 12, of which 5 were waited for; matrix products, arithmetic and copies ran while one was open for 6% of the time, Pallas kernels for 7%

profile of v9, /device:TPU:1, one launch (start us, length us, event | category | flops | bytes accessed | tf_op | source)
XLA Modules:
  0.0 89.0 jit_solution(3485893664764764683)
XLA Ops:
  7.2 0.0 copy-start.2
  7.2 0.0 all-gather.2.cloned.1.call-start
  7.2 0.9 %constant_dynamic-slice_fusion = bf16[256,256]{1,0:T(8,128)(2,1)S(1)} fusion(bf16[512,256]{1,0:T(8,128)(2,1)} %ladder.1, s32[]{:T(128)S(6)} %select_n.25), kind=kLoop, calls=%fused_computation.13 | loop fusion | bytes 262148 | tf_op jit(solution)/shard_map/dynamic_slice | solution.py:180
  8.2 3.9 %collective-permute-start = (bf16[256,256]{1,0:T(8,128)(2,1)S(1)}, bf16[256,256]{1,0:T(8,128)(2,1)S(1)}, u32[]{:S(2)}, u32[]{:S(2)}) collective-permute-start(bf16[256,256]{1,0:T(8,128)(2,1)S(1)} %constant_dynamic-slice_fusion), channel_id=1, source_target_pairs={{0,1},{1,0},{2,3},{3,2},{4,5},{5,4},{6,7},{7,6},{8,9},{9,8},{10,11... | collective-permute-start | bytes 393224 | tf_op jit(solution)/shard_map/ppermute | solution.py:181
  12.1 1.9 %shard_map.95 = bf16[768,256]{1,0:T(8,128)(2,1)} custom-call(s32[64,128]{1,0:T(8,128)} %bitcast.8, bf16[512,256]{1,0:T(8,128)(2,1)} %ladder.1, bf16[256,256]{1,0:T(8,128)(2,1)} %amps.1), custom_call_target="tpu_custom_call" | custom-call | bytes 1048576 | tf_op jit(solution)/shard_map/pallas_call | solution.py:58
  14.1 0.8 fusion.5
  14.9 0.0 collective-permute-done
  14.9 0.8 fusion.1
  15.7 0.0 all-gather.2.cloned.1.call-update
  15.7 4.7 %collective-permute-start.1 = (bf16[256,256]{1,0:T(8,128)(2,1)}, bf16[256,256]{1,0:T(8,128)(2,1)S(1)}, u32[]{:S(2)}, u32[]{:S(2)}) collective-permute-start(bf16[256,256]{1,0:T(8,128)(2,1)} %amps.1), channel_id=1, source_target_pairs={{0,3},{1,2},{2,1},{3,0},{4,7},{5,6},{6,5},{7,4},{8,11},{9,10},{10,... | collective-permute-start | bytes 393224 | tf_op jit(solution)/shard_map/ppermute | solution.py:190
  20.4 0.9 %constant_dynamic-update-slice_fusion.1 = bf16[256,512]{1,0:T(8,128)(2,1)S(1)} fusion(bf16[256,256]{1,0:T(8,128)(2,1)} %amps.1), kind=kLoop, calls=%fused_computation.7 | loop fusion | bytes 262144
  21.4 1.6 %collective-permute-done.1 = bf16[256,256]{1,0:T(8,128)(2,1)S(1)} collective-permute-done((bf16[256,256]{1,0:T(8,128)(2,1)}, bf16[256,256]{1,0:T(8,128)(2,1)S(1)}, u32[]{:S(2)}, u32[]{:S(2)}) %collective-permute-start.1) | collective-permute-done | bytes 131104 | tf_op jit(solution)/shard_map/ppermute | solution.py:190
  23.0 4.2 %collective-permute-start.2 = (bf16[256,512]{1,0:T(8,128)(2,1)S(1)}, bf16[256,512]{1,0:T(8,128)(2,1)S(1)}, u32[]{:S(2)}, u32[]{:S(2)}) collective-permute-start(bf16[256,512]{1,0:T(8,128)(2,1)S(1)} %constant_dynamic-update-slice_fusion.refs_0_), channel_id=1, source_target_pairs={{0,4},{4,8},{8,12},{12,16},{16,20},{20,24},{24,28},{28,0},{1,5},{5... | collective-permute-start | bytes 786440 | tf_op jit(solution)/shard_map/ppermute | solution.py:195
  27.2 8.6 %collective-permute-start.3 = (bf16[256,512]{1,0:T(8,128)(2,1)S(1)}, bf16[256,512]{1,0:T(8,128)(2,1)S(1)}, u32[]{:S(2)}, u32[]{:S(2)}) collective-permute-start(bf16[256,512]{1,0:T(8,128)(2,1)S(1)} %constant_dynamic-update-slice_fusion.refs_0_), channel_id=1, source_target_pairs={{0,28},{4,0},{8,4},{12,8},{16,12},{20,16},{24,20},{28,24},{1,29},{... | collective-permute-start | bytes 786440 | tf_op jit(solution)/shard_map/ppermute | solution.py:196
  35.8 1.8 %collective-permute-done.2.refs_1_ = bf16[256,512]{1,0:T(8,128)(2,1)S(1)} collective-permute-done((bf16[256,512]{1,0:T(8,128)(2,1)S(1)}, bf16[256,512]{1,0:T(8,128)(2,1)S(1)}, u32[]{:S(2)}, u32[]{:S(2)}) %collective-permute-start.2) | collective-permute-done | bytes 262176 | tf_op jit(solution)/shard_map/ppermute | solution.py:195
  37.6 1.9 %collective-permute-start.4 = (bf16[256,512]{1,0:T(8,128)(2,1)S(1)}, bf16[256,512]{1,0:T(8,128)(2,1)S(1)}, u32[]{:S(2)}, u32[]{:S(2)}) collective-permute-start(bf16[256,512]{1,0:T(8,128)(2,1)S(1)} %collective-permute-done.2.refs_1_), channel_id=1, source_target_pairs={{0,4},{4,8},{8,12},{12,16},{16,20},{20,24},{24,28},{28,0},{1,5},{5... | collective-permute-start | bytes 786440 | tf_op jit(solution)/shard_map/ppermute | solution.py:195
  39.5 0.0 collective-permute-done.3.refs_2_
  39.5 4.6 %collective-permute-start.5 = (bf16[256,512]{1,0:T(8,128)(2,1)S(1)}, bf16[256,512]{1,0:T(8,128)(2,1)S(1)}, u32[]{:S(2)}, u32[]{:S(2)}) collective-permute-start(bf16[256,512]{1,0:T(8,128)(2,1)S(1)} %collective-permute-done.3.refs_2_), channel_id=1, source_target_pairs={{0,28},{4,0},{8,4},{12,8},{16,12},{20,16},{24,20},{28,24},{1,29},{... | collective-permute-start | bytes 786440 | tf_op jit(solution)/shard_map/ppermute | solution.py:196
  44.1 2.2 %collective-permute-done.4.refs_3_ = bf16[256,512]{1,0:T(8,128)(2,1)S(1)} collective-permute-done((bf16[256,512]{1,0:T(8,128)(2,1)S(1)}, bf16[256,512]{1,0:T(8,128)(2,1)S(1)}, u32[]{:S(2)}, u32[]{:S(2)}) %collective-permute-start.4) | collective-permute-done | bytes 262176 | tf_op jit(solution)/shard_map/ppermute | solution.py:195
  46.3 1.9 %collective-permute-start.6 = (bf16[256,512]{1,0:T(8,128)(2,1)S(1)}, bf16[256,512]{1,0:T(8,128)(2,1)S(1)}, u32[]{:S(2)}, u32[]{:S(2)}) collective-permute-start(bf16[256,512]{1,0:T(8,128)(2,1)S(1)} %collective-permute-done.4.refs_3_), channel_id=1, source_target_pairs={{0,4},{4,8},{8,12},{12,16},{16,20},{20,24},{24,28},{28,0},{1,5},{5... | collective-permute-start | bytes 786440 | tf_op jit(solution)/shard_map/ppermute | solution.py:195
  48.2 0.0 collective-permute-done.5.refs_4_
  48.2 4.6 %collective-permute-start.7 = (bf16[256,512]{1,0:T(8,128)(2,1)S(1)}, bf16[256,512]{1,0:T(8,128)(2,1)S(1)}, u32[]{:S(2)}, u32[]{:S(2)}) collective-permute-start(bf16[256,512]{1,0:T(8,128)(2,1)S(1)} %collective-permute-done.5.refs_4_), channel_id=1, source_target_pairs={{0,28},{4,0},{8,4},{12,8},{16,12},{20,16},{24,20},{28,24},{1,29},{... | collective-permute-start | bytes 786440 | tf_op jit(solution)/shard_map/ppermute | solution.py:196
  52.8 0.0 copy-done.2
  52.8 0.1 dynamic_slice.18
  52.9 2.1 %collective-permute-done.6.refs_5_ = bf16[256,512]{1,0:T(8,128)(2,1)S(1)} collective-permute-done((bf16[256,512]{1,0:T(8,128)(2,1)S(1)}, bf16[256,512]{1,0:T(8,128)(2,1)S(1)}, u32[]{:S(2)}, u32[]{:S(2)}) %collective-permute-start.6) | collective-permute-done | bytes 262176 | tf_op jit(solution)/shard_map/ppermute | solution.py:195
  55.0 1.9 %collective-permute-start.8 = (bf16[256,256]{1,0:T(8,128)(2,1)S(1)}, bf16[256,256]{1,0:T(8,128)(2,1)S(1)}, u32[]{:S(2)}, u32[]{:S(2)}) collective-permute-start(bf16[256,256]{1,0:T(8,128)(2,1)S(1)} %slice.16), channel_id=1, source_target_pairs={{0,4},{4,8},{8,12},{12,16},{16,20},{20,24},{24,28},{28,0},{1,5},{5... | collective-permute-start | bytes 393224 | tf_op jit(solution)/shard_map/ppermute | solution.py:198
  57.0 0.0 collective-permute-done.7.refs_6_
  57.0 0.0 copy-start.4
  57.0 4.6 %collective-permute-start.9 = (bf16[256,256]{1,0:T(8,128)(2,1)S(1)}, bf16[256,256]{1,0:T(8,128)(2,1)S(1)}, u32[]{:S(2)}, u32[]{:S(2)}) collective-permute-start(bf16[256,256]{1,0:T(8,128)(2,1)S(1)} %slice.17), channel_id=1, source_target_pairs={{0,28},{4,0},{8,4},{12,8},{16,12},{20,16},{24,20},{28,24},{1,29},{... | collective-permute-start | bytes 393224 | tf_op jit(solution)/shard_map/ppermute | solution.py:199
  61.6 3.5 %compare_select_fusion.hole = bf16[256,4096]{1,0:T(8,128)(2,1)} fusion(bf16[256,4096]{1,0:T(8,128)(2,1)} %param.13, s32[4096]{0:T(1024)S(1)} %copy-done.2, s32[256]{0:T(256)S(1)} %dynamic_slice.18), kind=kLoop, calls=%fused_computation | loop fusion | flops 2097152 | bytes 4211712 | tf_op jit(solution)/shard_map/jit(_where)/select_n | solution.py:202
  65.1 0.0 copy-done.4
  65.1 0.1 dynamic_slice.19
  65.2 0.0 copy-start
  65.2 0.0 collective-permute-done.8.refs_7_
  65.2 0.0 collective-permute-done.9.refs_8_
  65.2 5.4 %all-gather.2.cloned.1.call-done.gathered = bf16[16,768,256]{2,1,0:T(8,128)(2,1)} async-done(((bf16[1,768,256]{2,1,0:T(8,128)(2,1)}), bf16[16,768,256]{2,1,0:T(8,128)(2,1)}) %all-gather.2.cloned.1.call-update) | async-done | bytes 6291472 | tf_op jit(solution)/shard_map/all_gather | solution.py:188
  70.6 2.8 %shard_map.97 = s16[272,256]{1,0:T(8,128)(2,1)S(1)} custom-call(bf16[16,768,256]{2,1,0:T(8,128)(2,1)} %all-gather.2.cloned.1.call-done.gathered, bf16[256,512]{1,0:T(8,128)(2,1)S(1)} %constant_dynamic-update-slice_fusion.refs_0_, bf16[256,512]{1,0:T(8,128)(2,1)S(1)} %collective-permute-done.2.refs_1_, bf16[256,512]{1,0:T(8,128)(2,1)S(1)} %collective-permute-done.3.refs_2_, ...), custom_call_target="tpu_custom_call" | custom-call | flops 536870912 | bytes 4194304 | tf_op jit(solution)/shard_map/pallas_call | solution.py:162
  73.4 3.1 %collective-permute-start.10 = (s16[272,256]{1,0:T(8,128)(2,1)S(1)}, s16[272,256]{1,0:T(8,128)(2,1)S(1)}, u32[]{:S(2)}, u32[]{:S(2)}) collective-permute-start(s16[272,256]{1,0:T(8,128)(2,1)S(1)} %shard_map.97), channel_id=1, source_target_pairs={{0,1},{1,0},{2,3},{3,2},{4,5},{5,4},{6,7},{7,6},{8,9},{9,8},{10,11... | collective-permute-start | bytes 417800 | tf_op jit(solution)/shard_map/ppermute | solution.py:210
  76.5 0.1 broadcast_add_fusion
  76.6 0.1 add.66
  76.7 0.0 copy-done
  76.7 0.0 copy-start.1
  76.7 0.0 copy-start.3
  76.7 4.6 %shard_map.96 = f32[256,256]{1,0:T(8,128)S(1)} custom-call(bf16[16,768,256]{2,1,0:T(8,128)(2,1)} %all-gather.2.cloned.1.call-done.gathered, bf16[256,4096]{1,0:T(8,128)(2,1)} %compare_select_fusion.hole, bf16[256,512]{1,0:T(8,128)(2,1)S(1)} %constant_dynamic-update-slice_fusion.refs_0_, bf16[256,512]{1,0:T(8,128)(2,1)S(1)} %collective-permute-done.2.refs_1_, ...), custom_call_target="tpu_custom_call" | custom-call | flops 1073741824 | bytes 8388608 | tf_op jit(solution)/shard_map/pallas_call | solution.py:162
  81.3 0.0 collective-permute-done.10
  81.3 0.0 copy-done.1
  81.4 0.0 copy-done.3
  81.4 0.8 subtract_convert_fusion
  (4 shorter events, 0.0 us)
Async XLA Ops:
  7.2 45.7 %copy-start.2 = (s32[4096]{0:T(1024)S(1)}, s32[4096]{0:T(1024)}, u32[]{:S(2)}) copy-start(s32[4096]{0:T(1024)} %param.11) | copy-start | bytes 49156
  7.2 63.5 %all-gather.2.cloned.1.call-start = ((), (), s32[]{:S(2)}) async-start(), calls=%async_computation | async-start | bytes 6684672 | tf_op jit(solution)/shard_map/all_gather | solution.py:188
  8.2 6.7 %collective-permute-start = (bf16[256,256]{1,0:T(8,128)(2,1)S(1)}, bf16[256,256]{1,0:T(8,128)(2,1)S(1)}, u32[]{:S(2)}, u32[]{:S(2)}) collective-permute-start(bf16[256,256]{1,0:T(8,128)(2,1)S(1)} %constant_dynamic-slice_fusion), channel_id=1, source_target_pairs={{0,1},{1,0},{2,3},{3,2},{4,5},{5,4},{6,7},{7,6},{8,9},{9,8},{10,11... | collective-permute-start | bytes 393224 | tf_op jit(solution)/shard_map/ppermute | solution.py:181
  15.7 7.3 %collective-permute-start.1 = (bf16[256,256]{1,0:T(8,128)(2,1)}, bf16[256,256]{1,0:T(8,128)(2,1)S(1)}, u32[]{:S(2)}, u32[]{:S(2)}) collective-permute-start(bf16[256,256]{1,0:T(8,128)(2,1)} %amps.1), channel_id=1, source_target_pairs={{0,3},{1,2},{2,1},{3,0},{4,7},{5,6},{6,5},{7,4},{8,11},{9,10},{10,... | collective-permute-start | bytes 393224 | tf_op jit(solution)/shard_map/ppermute | solution.py:190
  23.0 14.6 %collective-permute-start.2 = (bf16[256,512]{1,0:T(8,128)(2,1)S(1)}, bf16[256,512]{1,0:T(8,128)(2,1)S(1)}, u32[]{:S(2)}, u32[]{:S(2)}) collective-permute-start(bf16[256,512]{1,0:T(8,128)(2,1)S(1)} %constant_dynamic-update-slice_fusion.refs_0_), channel_id=1, source_target_pairs={{0,4},{4,8},{8,12},{12,16},{16,20},{20,24},{24,28},{28,0},{1,5},{5... | collective-permute-start | bytes 786440 | tf_op jit(solution)/shard_map/ppermute | solution.py:195
  27.2 12.3 %collective-permute-start.3 = (bf16[256,512]{1,0:T(8,128)(2,1)S(1)}, bf16[256,512]{1,0:T(8,128)(2,1)S(1)}, u32[]{:S(2)}, u32[]{:S(2)}) collective-permute-start(bf16[256,512]{1,0:T(8,128)(2,1)S(1)} %constant_dynamic-update-slice_fusion.refs_0_), channel_id=1, source_target_pairs={{0,28},{4,0},{8,4},{12,8},{16,12},{20,16},{24,20},{28,24},{1,29},{... | collective-permute-start | bytes 786440 | tf_op jit(solution)/shard_map/ppermute | solution.py:196
  37.6 8.7 %collective-permute-start.4 = (bf16[256,512]{1,0:T(8,128)(2,1)S(1)}, bf16[256,512]{1,0:T(8,128)(2,1)S(1)}, u32[]{:S(2)}, u32[]{:S(2)}) collective-permute-start(bf16[256,512]{1,0:T(8,128)(2,1)S(1)} %collective-permute-done.2.refs_1_), channel_id=1, source_target_pairs={{0,4},{4,8},{8,12},{12,16},{16,20},{20,24},{24,28},{28,0},{1,5},{5... | collective-permute-start | bytes 786440 | tf_op jit(solution)/shard_map/ppermute | solution.py:195
  39.5 8.7 %collective-permute-start.5 = (bf16[256,512]{1,0:T(8,128)(2,1)S(1)}, bf16[256,512]{1,0:T(8,128)(2,1)S(1)}, u32[]{:S(2)}, u32[]{:S(2)}) collective-permute-start(bf16[256,512]{1,0:T(8,128)(2,1)S(1)} %collective-permute-done.3.refs_2_), channel_id=1, source_target_pairs={{0,28},{4,0},{8,4},{12,8},{16,12},{20,16},{24,20},{28,24},{1,29},{... | collective-permute-start | bytes 786440 | tf_op jit(solution)/shard_map/ppermute | solution.py:196
  46.3 8.7 %collective-permute-start.6 = (bf16[256,512]{1,0:T(8,128)(2,1)S(1)}, bf16[256,512]{1,0:T(8,128)(2,1)S(1)}, u32[]{:S(2)}, u32[]{:S(2)}) collective-permute-start(bf16[256,512]{1,0:T(8,128)(2,1)S(1)} %collective-permute-done.4.refs_3_), channel_id=1, source_target_pairs={{0,4},{4,8},{8,12},{12,16},{16,20},{20,24},{24,28},{28,0},{1,5},{5... | collective-permute-start | bytes 786440 | tf_op jit(solution)/shard_map/ppermute | solution.py:195
  48.2 8.7 %collective-permute-start.7 = (bf16[256,512]{1,0:T(8,128)(2,1)S(1)}, bf16[256,512]{1,0:T(8,128)(2,1)S(1)}, u32[]{:S(2)}, u32[]{:S(2)}) collective-permute-start(bf16[256,512]{1,0:T(8,128)(2,1)S(1)} %collective-permute-done.5.refs_4_), channel_id=1, source_target_pairs={{0,28},{4,0},{8,4},{12,8},{16,12},{20,16},{24,20},{28,24},{1,29},{... | collective-permute-start | bytes 786440 | tf_op jit(solution)/shard_map/ppermute | solution.py:196
  55.0 10.2 %collective-permute-start.8 = (bf16[256,256]{1,0:T(8,128)(2,1)S(1)}, bf16[256,256]{1,0:T(8,128)(2,1)S(1)}, u32[]{:S(2)}, u32[]{:S(2)}) collective-permute-start(bf16[256,256]{1,0:T(8,128)(2,1)S(1)} %slice.16), channel_id=1, source_target_pairs={{0,4},{4,8},{8,12},{12,16},{16,20},{20,24},{24,28},{28,0},{1,5},{5... | collective-permute-start | bytes 393224 | tf_op jit(solution)/shard_map/ppermute | solution.py:198
  57.0 8.1 %copy-start.4 = (f32[64]{0:T(128)S(1)}, f32[64]{0:T(128)}, u32[]{:S(2)}) copy-start(f32[64]{0:T(128)} %param.14) | copy-start | bytes 772
  57.0 8.2 %collective-permute-start.9 = (bf16[256,256]{1,0:T(8,128)(2,1)S(1)}, bf16[256,256]{1,0:T(8,128)(2,1)S(1)}, u32[]{:S(2)}, u32[]{:S(2)}) collective-permute-start(bf16[256,256]{1,0:T(8,128)(2,1)S(1)} %slice.17), channel_id=1, source_target_pairs={{0,28},{4,0},{8,4},{12,8},{16,12},{20,16},{24,20},{28,24},{1,29},{... | collective-permute-start | bytes 393224 | tf_op jit(solution)/shard_map/ppermute | solution.py:199
  65.2 11.5 %copy-start = (f32[256,256]{1,0:T(8,128)S(1)}, f32[256,256]{1,0:T(8,128)}, u32[]{:S(2)}) copy-start(f32[256,256]{1,0:T(8,128)} %refs_9_.1) | copy-start | bytes 786436
  73.4 7.9 %collective-permute-start.10 = (s16[272,256]{1,0:T(8,128)(2,1)S(1)}, s16[272,256]{1,0:T(8,128)(2,1)S(1)}, u32[]{:S(2)}, u32[]{:S(2)}) collective-permute-start(s16[272,256]{1,0:T(8,128)(2,1)S(1)} %shard_map.97), channel_id=1, source_target_pairs={{0,1},{1,0},{2,3},{3,2},{4,5},{5,4},{6,7},{7,6},{8,9},{9,8},{10,11... | collective-permute-start | bytes 417800 | tf_op jit(solution)/shard_map/ppermute | solution.py:210
  76.7 4.7 %copy-start.1 = (bf16[256,256]{1,0:T(8,128)(2,1)S(1)}, bf16[256,256]{1,0:T(8,128)(2,1)}, u32[]{:S(2)}) copy-start(bf16[256,256]{1,0:T(8,128)(2,1)} %amps.1) | copy-start | bytes 393220
  76.7 4.7 %copy-start.3 = (f32[256]{0:T(256)S(1)}, f32[256]{0:T(256)}, u32[]{:S(2)}) copy-start(f32[256]{0:T(256)} %param.15) | copy-start | bytes 3076
Sparse Core Ops, SparseCore 0:
  15.8 54.7 all-gather.1

commit v10 on v6

--- a/solution.py
+++ b/solution.py
@@ -96,12 +96,23 @@
 def partner_kernel(gathered, *refs):
     parts, out_ref, rows_v, acc, row_sems = refs[:9], *refs[9:]
     size = acc.shape[0]
-    copies = ladder_copies(gathered, 2 * size, parts, rows_v, row_sems, size)
-    for mine in copies:
-        for copy in mine:
-            copy.start()
+    z = lax.axis_index("z")
+    upper = (lax.axis_index("x") >= NX // 2).astype(jnp.int32)
+    copies = []
+    for i, away in enumerate((0, -1, 1, -2, 2, -3, 3, NZ // 2)):
+        src = gathered.at[pl.ds(2 * lax.rem(z + NZ + away, NZ), 2), pl.ds(2 * size, size)]
+        dst = rows_v.at[pl.ds(2 * i, 2)]
+        copies.append(pltpu.make_async_copy(src, dst, row_sems.at[i]))
+        copies[-1].start()
     acc[...] = jnp.zeros_like(acc)
-    add_ladder(copies, parts, rows_v, acc, size)
+    blocks = [(p, i, p, i) for p in range(NZ - 1) for i in range(2)]
+    blocks += [(NZ - 1, 0, NZ - 1, 0), (NZ, 0, NZ - 1, 1)]
+    for p, i, chunk, j in blocks:
+        if j == 0:
+            copies[chunk].wait()
+        part = parts[p][:, i * size : (i + 1) * size]
+        row = upper if j == 0 else 1 - upper
+        acc[...] += jnp.dot(part, rows_v[2 * chunk + row], preferred_element_type=F32)
     largest = jnp.max(jnp.abs(acc[...]), axis=0, keepdims=True)
     exponent = jnp.ceil(jnp.log2(jnp.maximum(largest, 2.0**-100)))
     fixed = jnp.round(acc[...] * jnp.exp2(FIXED_BITS - exponent))
@@ -149,7 +160,8 @@
     in_hbm = [pltpu.with_memory_space_constraint(a, pltpu.HBM) for a in arrays]
     in_vmem = (*parts, drive) if with_hole else parts
     out = jax.ShapeDtypeStruct(drive.shape, F32)
-    scratch = [pltpu.VMEM((n * size, cols), BF16)]
+    shape = (n * size, cols) if with_hole else (n, size, cols)
+    scratch = [pltpu.VMEM(shape, BF16)]
     if not with_hole:
         out = jax.ShapeDtypeStruct((size + EXPONENT_ROWS, cols), jnp.int16)
         scratch.append(pltpu.VMEM(drive.shape, F32))

time: 89.6 us -> 89.6 us (level)
  no operation moved by 1% of the time
where the time goes in v10:
time: 89.6 us; the launch traced here: 89 us
  starting transfers between devices  44.1 us (49%)
  between operations  14.3 us (16%)
  waiting for transfers between devices  13.3 us (15%)
  Pallas kernels  9.26 us (10%)
  other arithmetic  5.19 us (6%)
  local copies, waits for them, and re-layouts  2.95 us (3%)
    ppermute x3, starting transfers between devices, body(): b = lax.ppermute(b, 'z', shift(NZ, -1))  17.7 us
    ppermute x3, starting transfers between devices, body(): f = lax.ppermute(f, 'z', shift(NZ, 1))  8 us
    pallas_call x2, Pallas kernels, products(): pl.pallas_call(kernel, out_shape=out, in_specs=[hbm] * len(in_hbm) + [vme...  7.35 us
    ppermute x3, waiting for transfers between devices, body(): f = lax.ppermute(f, 'z', shift(NZ, 1))  6.14 us
    all_gather x1, waiting for transfers between devices, body(): gathered = lax.all_gather(rows, ('y', 'core'), axis=0, tiled=False)  5.5 us
    ppermute x1, starting transfers between devices, body(): other = lax.ppermute(amplitudes, 'x', [(i, NX - 1 - i) for i in range(NX)])  4.74 us
    ppermute x1, starting transfers between devices, body(): parts.append(lax.ppermute(b[:, size:], 'z', shift(NZ, -1)))  4.57 us
    ppermute x1, starting transfers between devices, body(): lent = lax.ppermute(lent, 'x', partner)  3.95 us
  transfers between devices with their start and end apart: 12, of which 5 were waited for; matrix products, arithmetic and copies ran while one was open for 6% of the time, Pallas kernels for 7%

profile of v10, /device:TPU:1, one launch (start us, length us, event | category | flops | bytes accessed | tf_op | source)
XLA Modules:
  0.0 89.0 jit_solution(16336932770826358249)
XLA Ops:
  7.2 0.0 copy-start.2
  7.2 0.0 all-gather.2.cloned.1.call-start
  7.2 0.9 %constant_dynamic-slice_fusion = bf16[256,256]{1,0:T(8,128)(2,1)S(1)} fusion(bf16[512,256]{1,0:T(8,128)(2,1)} %ladder.1, s32[]{:T(128)S(6)} %select_n.23), kind=kLoop, calls=%fused_computation.13 | loop fusion | bytes 262148 | tf_op jit(solution)/shard_map/dynamic_slice | solution.py:192
  8.2 3.9 %collective-permute-start = (bf16[256,256]{1,0:T(8,128)(2,1)S(1)}, bf16[256,256]{1,0:T(8,128)(2,1)S(1)}, u32[]{:S(2)}, u32[]{:S(2)}) collective-permute-start(bf16[256,256]{1,0:T(8,128)(2,1)S(1)} %constant_dynamic-slice_fusion), channel_id=1, source_target_pairs={{0,1},{1,0},{2,3},{3,2},{4,5},{5,4},{6,7},{7,6},{8,9},{9,8},{10,11... | collective-permute-start | bytes 393224 | tf_op jit(solution)/shard_map/ppermute | solution.py:193
  12.1 1.9 %shard_map.95 = bf16[768,256]{1,0:T(8,128)(2,1)} custom-call(s32[64,128]{1,0:T(8,128)} %bitcast.8, bf16[512,256]{1,0:T(8,128)(2,1)} %ladder.1, bf16[256,256]{1,0:T(8,128)(2,1)} %amps.1), custom_call_target="tpu_custom_call" | custom-call | bytes 1048576 | tf_op jit(solution)/shard_map/pallas_call | solution.py:58
  14.1 0.8 fusion.5
  14.9 0.0 collective-permute-done
  14.9 0.8 fusion.1
  15.7 0.0 all-gather.2.cloned.1.call-update
  15.7 4.7 %collective-permute-start.1 = (bf16[256,256]{1,0:T(8,128)(2,1)}, bf16[256,256]{1,0:T(8,128)(2,1)S(1)}, u32[]{:S(2)}, u32[]{:S(2)}) collective-permute-start(bf16[256,256]{1,0:T(8,128)(2,1)} %amps.1), channel_id=1, source_target_pairs={{0,3},{1,2},{2,1},{3,0},{4,7},{5,6},{6,5},{7,4},{8,11},{9,10},{10,... | collective-permute-start | bytes 393224 | tf_op jit(solution)/shard_map/ppermute | solution.py:202
  20.4 0.9 %constant_dynamic-update-slice_fusion.1 = bf16[256,512]{1,0:T(8,128)(2,1)S(1)} fusion(bf16[256,256]{1,0:T(8,128)(2,1)} %amps.1), kind=kLoop, calls=%fused_computation.8 | loop fusion | bytes 262144
  21.4 1.6 %collective-permute-done.1 = bf16[256,256]{1,0:T(8,128)(2,1)S(1)} collective-permute-done((bf16[256,256]{1,0:T(8,128)(2,1)}, bf16[256,256]{1,0:T(8,128)(2,1)S(1)}, u32[]{:S(2)}, u32[]{:S(2)}) %collective-permute-start.1) | collective-permute-done | bytes 131104 | tf_op jit(solution)/shard_map/ppermute | solution.py:202
  23.0 4.2 %collective-permute-start.2 = (bf16[256,512]{1,0:T(8,128)(2,1)S(1)}, bf16[256,512]{1,0:T(8,128)(2,1)S(1)}, u32[]{:S(2)}, u32[]{:S(2)}) collective-permute-start(bf16[256,512]{1,0:T(8,128)(2,1)S(1)} %constant_dynamic-update-slice_fusion.refs_0_), channel_id=1, source_target_pairs={{0,4},{4,8},{8,12},{12,16},{16,20},{20,24},{24,28},{28,0},{1,5},{5... | collective-permute-start | bytes 786440 | tf_op jit(solution)/shard_map/ppermute | solution.py:207
  27.2 8.6 %collective-permute-start.3 = (bf16[256,512]{1,0:T(8,128)(2,1)S(1)}, bf16[256,512]{1,0:T(8,128)(2,1)S(1)}, u32[]{:S(2)}, u32[]{:S(2)}) collective-permute-start(bf16[256,512]{1,0:T(8,128)(2,1)S(1)} %constant_dynamic-update-slice_fusion.refs_0_), channel_id=1, source_target_pairs={{0,28},{4,0},{8,4},{12,8},{16,12},{20,16},{24,20},{28,24},{1,29},{... | collective-permute-start | bytes 786440 | tf_op jit(solution)/shard_map/ppermute | solution.py:208
  35.8 1.8 %collective-permute-done.2.refs_1_ = bf16[256,512]{1,0:T(8,128)(2,1)S(1)} collective-permute-done((bf16[256,512]{1,0:T(8,128)(2,1)S(1)}, bf16[256,512]{1,0:T(8,128)(2,1)S(1)}, u32[]{:S(2)}, u32[]{:S(2)}) %collective-permute-start.2) | collective-permute-done | bytes 262176 | tf_op jit(solution)/shard_map/ppermute | solution.py:207
  37.6 1.9 %collective-permute-start.4 = (bf16[256,512]{1,0:T(8,128)(2,1)S(1)}, bf16[256,512]{1,0:T(8,128)(2,1)S(1)}, u32[]{:S(2)}, u32[]{:S(2)}) collective-permute-start(bf16[256,512]{1,0:T(8,128)(2,1)S(1)} %collective-permute-done.2.refs_1_), channel_id=1, source_target_pairs={{0,4},{4,8},{8,12},{12,16},{16,20},{20,24},{24,28},{28,0},{1,5},{5... | collective-permute-start | bytes 786440 | tf_op jit(solution)/shard_map/ppermute | solution.py:207
  39.5 0.0 collective-permute-done.3.refs_2_
  39.5 4.6 %collective-permute-start.5 = (bf16[256,512]{1,0:T(8,128)(2,1)S(1)}, bf16[256,512]{1,0:T(8,128)(2,1)S(1)}, u32[]{:S(2)}, u32[]{:S(2)}) collective-permute-start(bf16[256,512]{1,0:T(8,128)(2,1)S(1)} %collective-permute-done.3.refs_2_), channel_id=1, source_target_pairs={{0,28},{4,0},{8,4},{12,8},{16,12},{20,16},{24,20},{28,24},{1,29},{... | collective-permute-start | bytes 786440 | tf_op jit(solution)/shard_map/ppermute | solution.py:208
  44.1 2.2 %collective-permute-done.4.refs_3_ = bf16[256,512]{1,0:T(8,128)(2,1)S(1)} collective-permute-done((bf16[256,512]{1,0:T(8,128)(2,1)S(1)}, bf16[256,512]{1,0:T(8,128)(2,1)S(1)}, u32[]{:S(2)}, u32[]{:S(2)}) %collective-permute-start.4) | collective-permute-done | bytes 262176 | tf_op jit(solution)/shard_map/ppermute | solution.py:207
  46.3 1.9 %collective-permute-start.6 = (bf16[256,512]{1,0:T(8,128)(2,1)S(1)}, bf16[256,512]{1,0:T(8,128)(2,1)S(1)}, u32[]{:S(2)}, u32[]{:S(2)}) collective-permute-start(bf16[256,512]{1,0:T(8,128)(2,1)S(1)} %collective-permute-done.4.refs_3_), channel_id=1, source_target_pairs={{0,4},{4,8},{8,12},{12,16},{16,20},{20,24},{24,28},{28,0},{1,5},{5... | collective-permute-start | bytes 786440 | tf_op jit(solution)/shard_map/ppermute | solution.py:207
  48.2 0.0 collective-permute-done.5.refs_4_
  48.2 4.6 %collective-permute-start.7 = (bf16[256,512]{1,0:T(8,128)(2,1)S(1)}, bf16[256,512]{1,0:T(8,128)(2,1)S(1)}, u32[]{:S(2)}, u32[]{:S(2)}) collective-permute-start(bf16[256,512]{1,0:T(8,128)(2,1)S(1)} %collective-permute-done.5.refs_4_), channel_id=1, source_target_pairs={{0,28},{4,0},{8,4},{12,8},{16,12},{20,16},{24,20},{28,24},{1,29},{... | collective-permute-start | bytes 786440 | tf_op jit(solution)/shard_map/ppermute | solution.py:208
  52.8 0.0 copy-done.2
  52.8 0.1 dynamic_slice.18
  52.9 2.1 %collective-permute-done.6.refs_5_ = bf16[256,512]{1,0:T(8,128)(2,1)S(1)} collective-permute-done((bf16[256,512]{1,0:T(8,128)(2,1)S(1)}, bf16[256,512]{1,0:T(8,128)(2,1)S(1)}, u32[]{:S(2)}, u32[]{:S(2)}) %collective-permute-start.6) | collective-permute-done | bytes 262176 | tf_op jit(solution)/shard_map/ppermute | solution.py:207
  55.0 1.9 %collective-permute-start.8 = (bf16[256,256]{1,0:T(8,128)(2,1)S(1)}, bf16[256,256]{1,0:T(8,128)(2,1)S(1)}, u32[]{:S(2)}, u32[]{:S(2)}) collective-permute-start(bf16[256,256]{1,0:T(8,128)(2,1)S(1)} %slice.16), channel_id=1, source_target_pairs={{0,4},{4,8},{8,12},{12,16},{16,20},{20,24},{24,28},{28,0},{1,5},{5... | collective-permute-start | bytes 393224 | tf_op jit(solution)/shard_map/ppermute | solution.py:210
  57.0 0.0 collective-permute-done.7.refs_6_
  57.0 4.6 %collective-permute-start.9 = (bf16[256,256]{1,0:T(8,128)(2,1)S(1)}, bf16[256,256]{1,0:T(8,128)(2,1)S(1)}, u32[]{:S(2)}, u32[]{:S(2)}) collective-permute-start(bf16[256,256]{1,0:T(8,128)(2,1)S(1)} %slice.17), channel_id=1, source_target_pairs={{0,28},{4,0},{8,4},{12,8},{16,12},{20,16},{24,20},{28,24},{1,29},{... | collective-permute-start | bytes 393224 | tf_op jit(solution)/shard_map/ppermute | solution.py:211
  61.6 3.5 %compare_select_fusion.hole = bf16[256,4096]{1,0:T(8,128)(2,1)} fusion(bf16[256,4096]{1,0:T(8,128)(2,1)} %param.13, s32[4096]{0:T(1024)S(1)} %copy-done.2, s32[256]{0:T(256)S(1)} %dynamic_slice.18), kind=kLoop, calls=%fused_computation | loop fusion | flops 2097152 | bytes 4211712 | tf_op jit(solution)/shard_map/jit(_where)/select_n | solution.py:214
  65.1 0.0 copy-start.3
  65.1 0.0 copy-start
  65.1 0.0 collective-permute-done.8.refs_7_
  65.1 0.0 collective-permute-done.9.refs_8_
  65.1 5.5 %all-gather.2.cloned.1.call-done.gathered = bf16[16,768,256]{2,1,0:T(8,128)(2,1)} async-done(((bf16[1,768,256]{2,1,0:T(8,128)(2,1)}), bf16[16,768,256]{2,1,0:T(8,128)(2,1)}) %all-gather.2.cloned.1.call-update) | async-done | bytes 6291472 | tf_op jit(solution)/shard_map/all_gather | solution.py:200
  70.6 2.7 %shard_map.97 = s16[272,256]{1,0:T(8,128)(2,1)S(1)} custom-call(bf16[16,768,256]{2,1,0:T(8,128)(2,1)} %all-gather.2.cloned.1.call-done.gathered, bf16[256,512]{1,0:T(8,128)(2,1)S(1)} %constant_dynamic-update-slice_fusion.refs_0_, bf16[256,512]{1,0:T(8,128)(2,1)S(1)} %collective-permute-done.2.refs_1_, bf16[256,512]{1,0:T(8,128)(2,1)S(1)} %collective-permute-done.3.refs_2_, ...), custom_call_target="tpu_custom_call" | custom-call | flops 536870912 | bytes 4194304 | tf_op jit(solution)/shard_map/pallas_call | solution.py:174
  73.4 3.1 %collective-permute-start.10 = (s16[272,256]{1,0:T(8,128)(2,1)S(1)}, s16[272,256]{1,0:T(8,128)(2,1)S(1)}, u32[]{:S(2)}, u32[]{:S(2)}) collective-permute-start(s16[272,256]{1,0:T(8,128)(2,1)S(1)} %shard_map.97), channel_id=1, source_target_pairs={{0,1},{1,0},{2,3},{3,2},{4,5},{5,4},{6,7},{7,6},{8,9},{9,8},{10,11... | collective-permute-start | bytes 417800 | tf_op jit(solution)/shard_map/ppermute | solution.py:221
  76.5 0.0 copy-done.3
  76.5 0.1 broadcast_add_fusion
  76.6 0.1 add.60
  76.6 0.1 dynamic_slice.19
  76.7 0.0 copy-done
  76.7 0.0 copy-start.1
  76.7 0.0 copy-start.4
  76.7 4.6 %shard_map.96 = f32[256,256]{1,0:T(8,128)S(1)} custom-call(bf16[16,768,256]{2,1,0:T(8,128)(2,1)} %all-gather.2.cloned.1.call-done.gathered, bf16[256,4096]{1,0:T(8,128)(2,1)} %compare_select_fusion.hole, bf16[256,512]{1,0:T(8,128)(2,1)S(1)} %constant_dynamic-update-slice_fusion.refs_0_, bf16[256,512]{1,0:T(8,128)(2,1)S(1)} %collective-permute-done.2.refs_1_, ...), custom_call_target="tpu_custom_call" | custom-call | flops 1073741824 | bytes 8388608 | tf_op jit(solution)/shard_map/pallas_call | solution.py:174
  81.3 0.0 collective-permute-done.10
  81.4 0.0 copy-done.1
  81.4 0.0 copy-done.4
  81.4 0.8 subtract_convert_fusion
  (4 shorter events, 0.0 us)
Async XLA Ops:
  7.2 45.7 %copy-start.2 = (s32[4096]{0:T(1024)S(1)}, s32[4096]{0:T(1024)}, u32[]{:S(2)}) copy-start(s32[4096]{0:T(1024)} %param.11) | copy-start | bytes 49156
  7.2 63.5 %all-gather.2.cloned.1.call-start = ((), (), s32[]{:S(2)}) async-start(), calls=%async_computation | async-start | bytes 6684672 | tf_op jit(solution)/shard_map/all_gather | solution.py:200
  8.2 6.7 %collective-permute-start = (bf16[256,256]{1,0:T(8,128)(2,1)S(1)}, bf16[256,256]{1,0:T(8,128)(2,1)S(1)}, u32[]{:S(2)}, u32[]{:S(2)}) collective-permute-start(bf16[256,256]{1,0:T(8,128)(2,1)S(1)} %constant_dynamic-slice_fusion), channel_id=1, source_target_pairs={{0,1},{1,0},{2,3},{3,2},{4,5},{5,4},{6,7},{7,6},{8,9},{9,8},{10,11... | collective-permute-start | bytes 393224 | tf_op jit(solution)/shard_map/ppermute | solution.py:193
  15.7 7.3 %collective-permute-start.1 = (bf16[256,256]{1,0:T(8,128)(2,1)}, bf16[256,256]{1,0:T(8,128)(2,1)S(1)}, u32[]{:S(2)}, u32[]{:S(2)}) collective-permute-start(bf16[256,256]{1,0:T(8,128)(2,1)} %amps.1), channel_id=1, source_target_pairs={{0,3},{1,2},{2,1},{3,0},{4,7},{5,6},{6,5},{7,4},{8,11},{9,10},{10,... | collective-permute-start | bytes 393224 | tf_op jit(solution)/shard_map/ppermute | solution.py:202
  23.0 14.6 %collective-permute-start.2 = (bf16[256,512]{1,0:T(8,128)(2,1)S(1)}, bf16[256,512]{1,0:T(8,128)(2,1)S(1)}, u32[]{:S(2)}, u32[]{:S(2)}) collective-permute-start(bf16[256,512]{1,0:T(8,128)(2,1)S(1)} %constant_dynamic-update-slice_fusion.refs_0_), channel_id=1, source_target_pairs={{0,4},{4,8},{8,12},{12,16},{16,20},{20,24},{24,28},{28,0},{1,5},{5... | collective-permute-start | bytes 786440 | tf_op jit(solution)/shard_map/ppermute | solution.py:207
  27.2 12.3 %collective-permute-start.3 = (bf16[256,512]{1,0:T(8,128)(2,1)S(1)}, bf16[256,512]{1,0:T(8,128)(2,1)S(1)}, u32[]{:S(2)}, u32[]{:S(2)}) collective-permute-start(bf16[256,512]{1,0:T(8,128)(2,1)S(1)} %constant_dynamic-update-slice_fusion.refs_0_), channel_id=1, source_target_pairs={{0,28},{4,0},{8,4},{12,8},{16,12},{20,16},{24,20},{28,24},{1,29},{... | collective-permute-start | bytes 786440 | tf_op jit(solution)/shard_map/ppermute | solution.py:208
  37.6 8.7 %collective-permute-start.4 = (bf16[256,512]{1,0:T(8,128)(2,1)S(1)}, bf16[256,512]{1,0:T(8,128)(2,1)S(1)}, u32[]{:S(2)}, u32[]{:S(2)}) collective-permute-start(bf16[256,512]{1,0:T(8,128)(2,1)S(1)} %collective-permute-done.2.refs_1_), channel_id=1, source_target_pairs={{0,4},{4,8},{8,12},{12,16},{16,20},{20,24},{24,28},{28,0},{1,5},{5... | collective-permute-start | bytes 786440 | tf_op jit(solution)/shard_map/ppermute | solution.py:207
  39.5 8.7 %collective-permute-start.5 = (bf16[256,512]{1,0:T(8,128)(2,1)S(1)}, bf16[256,512]{1,0:T(8,128)(2,1)S(1)}, u32[]{:S(2)}, u32[]{:S(2)}) collective-permute-start(bf16[256,512]{1,0:T(8,128)(2,1)S(1)} %collective-permute-done.3.refs_2_), channel_id=1, source_target_pairs={{0,28},{4,0},{8,4},{12,8},{16,12},{20,16},{24,20},{28,24},{1,29},{... | collective-permute-start | bytes 786440 | tf_op jit(solution)/shard_map/ppermute | solution.py:208
  46.3 8.7 %collective-permute-start.6 = (bf16[256,512]{1,0:T(8,128)(2,1)S(1)}, bf16[256,512]{1,0:T(8,128)(2,1)S(1)}, u32[]{:S(2)}, u32[]{:S(2)}) collective-permute-start(bf16[256,512]{1,0:T(8,128)(2,1)S(1)} %collective-permute-done.4.refs_3_), channel_id=1, source_target_pairs={{0,4},{4,8},{8,12},{12,16},{16,20},{20,24},{24,28},{28,0},{1,5},{5... | collective-permute-start | bytes 786440 | tf_op jit(solution)/shard_map/ppermute | solution.py:207
  48.2 8.7 %collective-permute-start.7 = (bf16[256,512]{1,0:T(8,128)(2,1)S(1)}, bf16[256,512]{1,0:T(8,128)(2,1)S(1)}, u32[]{:S(2)}, u32[]{:S(2)}) collective-permute-start(bf16[256,512]{1,0:T(8,128)(2,1)S(1)} %collective-permute-done.5.refs_4_), channel_id=1, source_target_pairs={{0,28},{4,0},{8,4},{12,8},{16,12},{20,16},{24,20},{28,24},{1,29},{... | collective-permute-start | bytes 786440 | tf_op jit(solution)/shard_map/ppermute | solution.py:208
  55.0 10.1 %collective-permute-start.8 = (bf16[256,256]{1,0:T(8,128)(2,1)S(1)}, bf16[256,256]{1,0:T(8,128)(2,1)S(1)}, u32[]{:S(2)}, u32[]{:S(2)}) collective-permute-start(bf16[256,256]{1,0:T(8,128)(2,1)S(1)} %slice.16), channel_id=1, source_target_pairs={{0,4},{4,8},{8,12},{12,16},{16,20},{20,24},{24,28},{28,0},{1,5},{5... | collective-permute-start | bytes 393224 | tf_op jit(solution)/shard_map/ppermute | solution.py:210
  57.0 8.1 %collective-permute-start.9 = (bf16[256,256]{1,0:T(8,128)(2,1)S(1)}, bf16[256,256]{1,0:T(8,128)(2,1)S(1)}, u32[]{:S(2)}, u32[]{:S(2)}) collective-permute-start(bf16[256,256]{1,0:T(8,128)(2,1)S(1)} %slice.17), channel_id=1, source_target_pairs={{0,28},{4,0},{8,4},{12,8},{16,12},{20,16},{24,20},{28,24},{1,29},{... | collective-permute-start | bytes 393224 | tf_op jit(solution)/shard_map/ppermute | solution.py:211
  65.1 11.4 %copy-start.3 = (f32[64]{0:T(128)S(1)}, f32[64]{0:T(128)}, u32[]{:S(2)}) copy-start(f32[64]{0:T(128)} %param.14) | copy-start | bytes 772
  65.1 11.6 %copy-start = (f32[256,256]{1,0:T(8,128)S(1)}, f32[256,256]{1,0:T(8,128)}, u32[]{:S(2)}) copy-start(f32[256,256]{1,0:T(8,128)} %refs_9_.1) | copy-start | bytes 786436
  73.4 8.0 %collective-permute-start.10 = (s16[272,256]{1,0:T(8,128)(2,1)S(1)}, s16[272,256]{1,0:T(8,128)(2,1)S(1)}, u32[]{:S(2)}, u32[]{:S(2)}) collective-permute-start(s16[272,256]{1,0:T(8,128)(2,1)S(1)} %shard_map.97), channel_id=1, source_target_pairs={{0,1},{1,0},{2,3},{3,2},{4,5},{5,4},{6,7},{7,6},{8,9},{9,8},{10,11... | collective-permute-start | bytes 417800 | tf_op jit(solution)/shard_map/ppermute | solution.py:221
  76.7 4.7 %copy-start.1 = (bf16[256,256]{1,0:T(8,128)(2,1)S(1)}, bf16[256,256]{1,0:T(8,128)(2,1)}, u32[]{:S(2)}) copy-start(bf16[256,256]{1,0:T(8,128)(2,1)} %amps.1) | copy-start | bytes 393220
  76.7 4.7 %copy-start.4 = (f32[256]{0:T(256)S(1)}, f32[256]{0:T(256)}, u32[]{:S(2)}) copy-start(f32[256]{0:T(256)} %param.15) | copy-start | bytes 3076
Sparse Core Ops, SparseCore 0:
  15.8 54.7 all-gather.1
